TPU v7x, 256 devices: a whole 4x4x8 slice. The times are simulated.
256 devices in a mesh: dp: 64 (over y, z, core), mp: 4 (over x).
Axes of the slice: x: 4, y: 4, z: 8, core: 2. Of those that a mesh axis runs over, the one named last changes fastest.
Arguments:
- passage_states: bfloat16 [768, 180, 768], P('dp'), may hold values from -6 to 6
- query_states: bfloat16 [192, 32, 768], P('dp'), may hold values from -6 to 6
- lengths: int32 [768], replicated, may hold values from 22 to 180, as said below
- owner_map: int32 [768], replicated, may hold values from 0 to 767, as said below
- candidates: int32 [192, 64], P('dp', 'mp'), may hold values from 0 to 767, as said below
- teacher_scores: float32 [192, 64], P('dp', 'mp'), may hold values from -8 to 8
- up_weight: bfloat16 [768, 3072], P(None, 'mp'), may hold values from -0.21875 to 0.21875
- down_weight: bfloat16 [3072, 768], P('mp'), may hold values from -0.109375 to 0.109375
- proj_weight: bfloat16 [768, 128], replicated, may hold values from -0.21875 to 0.21875
Outputs:
- query_loss: float32 [192], P('dp')
- grad_up: float32 [768, 3072], P('dp', 'mp')
- grad_down: float32 [3072, 768], P('mp', 'dp')
- grad_proj: float32 [768, 128], P('dp')
Inputs may be any that keep to these rules, and one draw needn't show every extreme that they name: A permutation: passage id k sits at pool position owner_map[k], held by dp index owner_map[k] // 12. `candidates`: on one device (the 3 queries of one dp index and the 16 candidate columns of one mp index) at most 2 candidate slots name passages of one owner; in every draw some owner gets exactly 2 from every device. A passage may appear more than once. `lengths`: the 12 pool positions of each dp index include one passage of 180 tokens.
All inputs are finite; a program needn't handle non-finite values.
Results may differ from a plain program's by a relative error of at most 0.03.
Values may be sent and summed in bfloat16 or wider, within the bound.
A program may use at most 192 MiB of HBM per device.

v0:
```python
import jax
import jax.numpy as jnp
from jax import lax
from jax.sharding import PartitionSpec as P

TAU = 0.05
EPS = 1e-06


def up_section(token_rows, up_weight, down_weight):
    pre_act = jnp.dot(token_rows, up_weight, preferred_element_type=jnp.float32)
    hidden = jax.nn.gelu(pre_act).astype(jnp.bfloat16)
    return (pre_act, hidden, jnp.dot(hidden, down_weight, preferred_element_type=jnp.float32))


def proj_section(token_rows, ffn_total, proj_weight):
    mixed = (token_rows.astype(jnp.float32) + ffn_total).astype(jnp.bfloat16)
    projected = jnp.dot(mixed, proj_weight, preferred_element_type=jnp.float32)
    inverse_norm = lax.rsqrt(jnp.sum(projected * projected, axis=-1, keepdims=True) + EPS)
    unit_rows = projected * inverse_norm
    return (mixed, unit_rows, inverse_norm, unit_rows.astype(jnp.bfloat16))


def back_section(
    token_rows, pre_act, hidden, mixed, unit_rows, inverse_norm, emb_cot, down_weight, proj_weight
):
    along = jnp.sum(emb_cot * unit_rows, axis=-1, keepdims=True)
    unit_cot = (inverse_norm * (emb_cot - unit_rows * along)).astype(jnp.bfloat16)
    grad_proj = jnp.dot(mixed.T, unit_cot, preferred_element_type=jnp.float32)
    mixed_cot = jnp.dot(unit_cot, proj_weight.T, preferred_element_type=jnp.float32).astype(
        jnp.bfloat16
    )
    grad_down = jnp.dot(hidden.T, mixed_cot, preferred_element_type=jnp.float32)
    hidden_cot = jnp.dot(mixed_cot, down_weight.T, preferred_element_type=jnp.float32)
    pre_cot = jax.vjp(jax.nn.gelu, pre_act)[1](hidden_cot)[0].astype(jnp.bfloat16)
    grad_up = jnp.dot(token_rows.T, pre_cot, preferred_element_type=jnp.float32)
    return (grad_up, grad_down, grad_proj)


def smooth_scores(query_slots, blocks, slot_len):
    similar = jnp.einsum("sie,ste->sit", query_slots, blocks, preferred_element_type=jnp.float32)
    live_mask = jnp.arange(blocks.shape[1])[None, :] < slot_len[:, None]
    exp_terms = jnp.where(live_mask[:, None, :], jnp.exp(similar / TAU), 0.0)
    denoms = jnp.sum(exp_terms, axis=-1)
    scores = TAU * jnp.sum(jnp.log(denoms), axis=-1)
    return (scores, exp_terms / denoms[..., None])


def slot_grads(score_cot, attend, query_slots, blocks):
    weights = (score_cot[:, None, None] * attend).astype(jnp.bfloat16)
    query_cot = jnp.einsum("sit,ste->sie", weights, blocks, preferred_element_type=jnp.float32)
    block_cot = jnp.einsum("sit,sie->ste", weights, query_slots, preferred_element_type=jnp.float32)
    return (query_cot, block_cot)


def owned_sum(asked_local, block_cot, p_dev):
    onehot_table = (asked_local.reshape(-1)[None, :] == jnp.arange(p_dev)[:, None]).astype(
        jnp.float32
    )
    flat_cot = block_cot.reshape(onehot_table.shape[1], -1)
    return jnp.dot(onehot_table, flat_cot, precision=lax.Precision.HIGHEST)


def local(
    passage_states,
    query_states,
    lengths,
    owner_map,
    candidates,
    teacher_scores,
    up_weight,
    down_weight,
    proj_weight,
):
    p_dev, pass_len, model_width = passage_states.shape
    q_dev, query_len, unused_width = query_states.shape
    cand_sub = candidates.shape[1]
    emb_width = proj_weight.shape[1]
    owners = lax.axis_size("dp")
    slot_count = q_dev * cand_sub
    capacity = max(2, (slot_count + owners - 1) // owners)
    pass_rows = passage_states.reshape(p_dev * pass_len, model_width)
    query_rows = query_states.reshape(q_dev * query_len, model_width)
    pass_pre, pass_hidden, pass_part = up_section(pass_rows, up_weight, down_weight)
    query_pre, query_hidden, query_part = up_section(query_rows, up_weight, down_weight)
    pass_total, query_total = (
        lax.psum(pass_part.astype(jnp.bfloat16), "mp").astype(jnp.float32),
        lax.psum(query_part.astype(jnp.bfloat16), "mp").astype(jnp.float32),
    )
    pass_mixed, pass_unit, pass_inverse, pass_flat = proj_section(
        pass_rows, pass_total, proj_weight
    )
    query_mixed, query_unit, query_inverse, query_flat = proj_section(
        query_rows, query_total, proj_weight
    )
    pass_emb = pass_flat.reshape(p_dev, pass_len, emb_width)
    query_emb = query_flat.reshape(q_dev, query_len, emb_width)
    positions = jnp.take(owner_map, candidates.reshape(slot_count))
    slot_owner = positions // p_dev
    local_index = positions % p_dev
    owner_onehot = (slot_owner[:, None] == jnp.arange(owners)[None, :]).astype(jnp.int32)
    slot_rank = jnp.sum((jnp.cumsum(owner_onehot, axis=0) - owner_onehot) * owner_onehot, axis=1)
    teacher = teacher_scores.reshape(slot_count)
    requests = (
        jnp.full((owners, capacity), -1, jnp.int32).at[slot_owner, slot_rank].set(local_index)
    )
    asked_local = lax.all_to_all(requests, "dp", split_axis=0, concat_axis=0, tiled=True)
    filled = asked_local >= 0
    picked = jnp.take(pass_emb, jnp.maximum(asked_local, 0), axis=0)
    picked = jnp.where(filled[:, :, None, None], picked, jnp.zeros_like(picked))
    arrived = lax.all_to_all(picked, "dp", split_axis=0, concat_axis=0, tiled=True)
    blocks = arrived[slot_owner, slot_rank]
    query_slots = jnp.repeat(query_emb, cand_sub, axis=0)
    slot_len = jnp.take(lengths, positions)
    scores, attend = smooth_scores(query_slots, blocks, slot_len)
    student_exp = jnp.exp(scores).reshape(q_dev, cand_sub)
    teacher_exp = jnp.exp(teacher).reshape(q_dev, cand_sub)
    cross_terms = teacher_exp * (teacher - scores).reshape(q_dev, cand_sub)
    student_sum, teacher_sum, cross_sum = lax.psum(
        (jnp.sum(student_exp, axis=1), jnp.sum(teacher_exp, axis=1), jnp.sum(cross_terms, axis=1)),
        "mp",
    )
    query_loss = cross_sum / teacher_sum - jnp.log(teacher_sum) + jnp.log(student_sum)
    score_cot = (student_exp / student_sum[:, None] - teacher_exp / teacher_sum[:, None]).reshape(
        slot_count
    )
    query_slot_cot, block_cot = slot_grads(score_cot, attend, query_slots, blocks)
    query_cot = jnp.sum(query_slot_cot.reshape(q_dev, cand_sub, query_len, emb_width), axis=1)
    block_back = (
        jnp.zeros((owners, capacity, pass_len, emb_width), jnp.float32)
        .at[slot_owner, slot_rank]
        .set(block_cot)
    )
    returned = lax.all_to_all(
        block_back.astype(jnp.bfloat16), "dp", split_axis=0, concat_axis=0, tiled=True
    ).astype(block_back.dtype)
    pass_cot = owned_sum(asked_local, returned, p_dev)
    pass_cot, query_cot = (
        lax.psum(pass_cot.reshape(p_dev * pass_len, emb_width).astype(jnp.bfloat16), "mp").astype(
            jnp.float32
        ),
        lax.psum(query_cot.reshape(q_dev * query_len, emb_width).astype(jnp.bfloat16), "mp").astype(
            jnp.float32
        ),
    )
    pass_terms = back_section(
        pass_rows,
        pass_pre,
        pass_hidden,
        pass_mixed,
        pass_unit,
        pass_inverse,
        pass_cot,
        down_weight,
        proj_weight,
    )
    query_terms = back_section(
        query_rows,
        query_pre,
        query_hidden,
        query_mixed,
        query_unit,
        query_inverse,
        query_cot,
        down_weight,
        proj_weight,
    )
    grad_up, grad_down, grad_proj = (
        lax.psum_scatter(pass_terms[0] + query_terms[0], "dp", scatter_dimension=0, tiled=True),
        lax.psum_scatter(pass_terms[1] + query_terms[1], "dp", scatter_dimension=1, tiled=True),
        lax.psum_scatter(pass_terms[2] + query_terms[2], "dp", scatter_dimension=0, tiled=True),
    )
    return (query_loss, grad_up, grad_down, grad_proj)


def solution(mesh):
    return jax.shard_map(
        local,
        mesh=mesh,
        in_specs=(
            P("dp", None, None),
            P("dp", None, None),
            P(),
            P(),
            P("dp", "mp"),
            P("dp", "mp"),
            P(None, "mp"),
            P("mp", None),
            P(),
        ),
        out_specs=(P("dp"), P("dp", "mp"), P("mp", "dp"), P("dp", None)),
        check_vma=False,
    )
```

profile of v0, /device:TPU:1, one launch (start us, length us, event | category | flops | bytes accessed | tf_op | source)
XLA Modules:
  0.0 855.8 jit_solution(9354439785966228718)
XLA Ops:
  7.2 5.7 reshape.135
  13.3 4.9 fusion.65
  21.0 5.4 convolution_convert_fusion.1
  31.9 22.2 %all_to_all.19 = s32[64,1,2]{2,1,0:T(1,128)S(1)} all-to-all(s32[64,1,2]{2,1,0:T(1,128)S(1)} %copy.42), channel_id=1, replica_groups=mesh['dp'=64,'mp'=4] {'dp'}, dimensions={0} | all-to-all | bytes 1024 | tf_op jit(solution)/shard_map/all_to_all | solution.py:107
  54.7 61.9 %all-reduce.16.cloned.1.call-done = (bf16[96,768]{1,0:T(8,128)(2,1)}, bf16[2160,768]{1,0:T(8,128)(2,1)}) async-done(((bf16[96,768]{1,0:T(8,128)(2,1)}, bf16[2160,768]{1,0:T(8,128)(2,1)}), (bf16[96,768]{1,0:T(8,128)(2,1)}, bf16[2160,768]{1,0:T(8,128)(2,1)})) %all-reduce.16.cloned.1.call-update) | async-done | bytes 3465232 | tf_op jit(solution)/shard_map/psum | solution.py:88
  116.7 4.1 multiply_reduce_fusion
  123.1 3.9 gather_fusion
  127.1 3.9 select_select_fusion
  131.0 13.7 %copy.48 = bf16[64,2,180,128]{3,1,2,0:T(2,128)(2,1)} copy(bf16[64,2,180,128]{3,2,1,0:T(8,128)(2,1)S(1)} %select_select_fusion) | data formatting | bytes 11796480 | tf_op jit(solution)/shard_map/jit(_where)/select_n | solution.py:110
  144.7 11.2 %all-to-all-start.1 = ((bf16[64,2,180,128]{3,1,2,0:T(2,128)(2,1)}), bf16[64,2,180,128]{3,1,2,0:T(2,128)(2,1)}, u32[]{:S(2)}, u32[]{:S(2)}) async-start(bf16[64,2,180,128]{3,1,2,0:T(2,128)(2,1)} %copy.48), calls=%async_computation.1 | async-start | bytes 11796480 | tf_op jit(solution)/shard_map/all_to_all | solution.py:111
  156.4 131.9 %all-to-all-done.1 = bf16[64,2,180,128]{3,1,2,0:T(2,128)(2,1)} async-done(((bf16[64,2,180,128]{3,1,2,0:T(2,128)(2,1)}), bf16[64,2,180,128]{3,1,2,0:T(2,128)(2,1)}, u32[]{:S(2)}, u32[]{:S(2)}) %all-to-all-start.1) | async-done | bytes 5898272 | tf_op jit(solution)/shard_map/all_to_all | solution.py:111
  288.3 6.1 copy.49
  294.4 5.1 gather_fusion.1
  299.6 4.4 fusion.59
  304.3 7.2 all-reduce.5
  312.1 5.6 fusion.55
  317.8 5.2 broadcast_in_dim.79
  323.0 11.1 %scatter_fusion.1 = f32[64,2,180,128]{3,2,1,0:T(8,128)} fusion(f32[64,2,180,128]{3,2,1,0:T(8,128)} %broadcast_in_dim.79, s32[48]{0:T(128)S(1)} %get-tuple-element.42, f32[48,180,128]{2,1,0:T(8,128)} %fusion.55), kind=kCustom, calls=%fused_computation.5 | custom fusion | bytes 13271424 | tf_op jit(solution)/shard_map/scatter | solution.py:132
  334.1 8.2 copy.62
  342.3 24.9 %copy.51 = bf16[64,2,180,128]{3,1,2,0:T(2,128)(2,1)} copy(bf16[64,2,180,128]{3,0,2,1:T(8,128)(2,1)S(1)} %copy.62) | data formatting | bytes 11796480 | tf_op jit(solution)/shard_map/convert_element_type | solution.py:135
  367.2 7.9 all-to-all-start.2
  379.7 24.1 %psum.55 = bf16[96,128]{1,0:T(8,128)(2,1)S(1)} all-reduce(bf16[96,128]{1,0:T(8,128)(2,1)S(1)} %bitcast.90), channel_id=1, replica_groups=mesh['dp'=64,'mp'=4] {'mp'}, use_global_device_ids=true, to_apply=%region_19.21 | all-reduce | flops 12288 | bytes 49152 | tf_op jit(solution)/shard_map/psum | solution.py:142
  403.9 103.6 %all-to-all-done.2 = bf16[64,2,180,128]{3,1,2,0:T(2,128)(2,1)} async-done(((bf16[64,2,180,128]{3,1,2,0:T(2,128)(2,1)}), bf16[64,2,180,128]{3,1,2,0:T(2,128)(2,1)}, u32[]{:S(2)}, u32[]{:S(2)}) %all-to-all-start.2) | async-done | bytes 5898272 | tf_op jit(solution)/shard_map/all_to_all | solution.py:134
  514.8 39.5 %all-reduce.12.cloned.1.call-done = bf16[2160,128]{1,0:T(8,128)(2,1)} async-done(((bf16[2160,128]{1,0:T(8,128)(2,1)}), bf16[2160,128]{1,0:T(8,128)(2,1)}) %all-reduce.12.cloned.1.call-update) | async-done | bytes 552976 | tf_op jit(solution)/shard_map/psum | solution.py:139
  564.4 18.1 %fusion.11 = f32[768,768]{1,0:T(8,128)} fusion(bf16[2160,768]{1,0:T(8,128)(2,1)} %reshape.135, f32[2160,768]{1,0:T(8,128)} %copy-done.18, bf16[2160,768]{1,0:T(8,128)(2,1)} %convolution_convert_fusion.2, bf16[768,768]{1,0:T(8,128)(2,1)S(1)} %copy-done), kind=kOutput, calls=%fused_computation.24 | convolution fusion | flops 5129256960 | bytes 16809984 | tf_op jit(solution)/shard_map/dot_general | solution.py:36
  582.5 7.5 fusion.56
  591.5 4.4 add_bitcast_fusion
  596.0 148.3 %fusion.57 = (f32[768,16]{0,1:T(8,128)}, f32[16,128]{1,0:T(8,128)S(1)}) fusion(f32[768,768]{0,1:T(8,128)S(1)} %convolution_add_fusion, f32[768,128]{1,0:T(8,128)} %convolution_add_fusion.1), kind=kCustom, calls=%all-reduce-scatter.2 | all-reduce-scatter fusion | flops 917505 | bytes 2810880
  750.3 4.9 collective-permute-start.31
  758.5 14.6 %collective-permute-start.25 = (f32[16,128]{1,0:T(8,128)S(1)}, f32[16,128]{1,0:T(8,128)S(1)}, u32[]{:S(2)}, u32[]{:S(2)}) collective-permute-start(f32[16,128]{1,0:T(8,128)S(1)} %get-tuple-element.36), channel_id=1, source_target_pairs={{0,40},{4,44},{8,48},{12,52},{16,56},{20,60},{24,64},{28,68},{32,7... | collective-permute-start | bytes 24584
  775.4 5.5 collective-permute-start.23
  811.3 3.8 collective-permute-start.9
  (171 shorter events, 110.5 us)
Async XLA Ops:
  7.2 109.5 %all-reduce.16.cloned.1.call-start = ((), (), s32[]{:S(2)}) async-start(), calls=%async_computation.5 | async-start | bytes 6930432 | tf_op jit(solution)/shard_map/psum | solution.py:88
  144.7 143.7 %all-to-all-start.1 = ((bf16[64,2,180,128]{3,1,2,0:T(2,128)(2,1)}), bf16[64,2,180,128]{3,1,2,0:T(2,128)(2,1)}, u32[]{:S(2)}, u32[]{:S(2)}) async-start(bf16[64,2,180,128]{3,1,2,0:T(2,128)(2,1)} %copy.48), calls=%async_computation.1 | async-start | bytes 11796480 | tf_op jit(solution)/shard_map/all_to_all | solution.py:111
  367.2 140.3 %all-to-all-start.2 = ((bf16[64,2,180,128]{3,1,2,0:T(2,128)(2,1)}), bf16[64,2,180,128]{3,1,2,0:T(2,128)(2,1)}, u32[]{:S(2)}, u32[]{:S(2)}) async-start(bf16[64,2,180,128]{3,1,2,0:T(2,128)(2,1)} %copy.51), calls=%async_computation.2 | async-start | bytes 11796480 | tf_op jit(solution)/shard_map/all_to_all | solution.py:134
  375.1 179.3 %all-reduce.12.cloned.1.call-start = ((), (), s32[]{:S(2)}) async-start(), calls=%async_computation.3 | async-start | bytes 1105920 | tf_op jit(solution)/shard_map/psum | solution.py:139
  513.6 333.2 %all-reduce.14.cloned.1.call-start = ((), (), s32[]{:S(2)}) async-start(), calls=%async_computation.4 | async-start | bytes 4718592
  745.1 62.2 %collective-permute-start.15 = (f32[768,12]{0,1:T(8,128)S(1)}, f32[768,12]{0,1:T(8,128)S(1)}, u32[]{:S(2)}, u32[]{:S(2)}) collective-permute-start(f32[768,12]{0,1:T(8,128)S(1)} %slice.12), channel_id=1, source_target_pairs={{0,64},{4,68},{8,72},{12,76},{16,80},{20,84},{24,88},{28,92},{32,9... | collective-permute-start | bytes 110600
  746.4 10.8 %collective-permute-start.30 = (f32[16,128]{1,0:T(8,128)S(1)}, f32[16,128]{1,0:T(8,128)S(1)}, u32[]{:S(2)}, u32[]{:S(2)}) collective-permute-start(f32[16,128]{1,0:T(8,128)S(1)} %get-tuple-element.36), channel_id=1, source_target_pairs={{0,60},{4,64},{8,68},{12,72},{16,76},{20,80},{24,84},{28,88},{32,9... | collective-permute-start | bytes 24584
  747.7 10.9 %collective-permute-start.29 = (f32[16,128]{1,0:T(8,128)S(1)}, f32[16,128]{1,0:T(8,128)S(1)}, u32[]{:S(2)}, u32[]{:S(2)}) collective-permute-start(f32[16,128]{1,0:T(8,128)S(1)} %get-tuple-element.36), channel_id=1, source_target_pairs={{0,56},{4,60},{8,64},{12,68},{16,72},{20,76},{24,80},{28,84},{32,8... | collective-permute-start | bytes 24584
  749.0 24.2 %collective-permute-start.28 = (f32[16,128]{1,0:T(8,128)S(1)}, f32[16,128]{1,0:T(8,128)S(1)}, u32[]{:S(2)}, u32[]{:S(2)}) collective-permute-start(f32[16,128]{1,0:T(8,128)S(1)} %get-tuple-element.36), channel_id=1, source_target_pairs={{0,52},{4,56},{8,60},{12,64},{16,68},{20,72},{24,76},{28,80},{32,8... | collective-permute-start | bytes 24584
  755.9 19.4 %collective-permute-start.27 = (f32[16,128]{1,0:T(8,128)S(1)}, f32[16,128]{1,0:T(8,128)S(1)}, u32[]{:S(2)}, u32[]{:S(2)}) collective-permute-start(f32[16,128]{1,0:T(8,128)S(1)} %get-tuple-element.36), channel_id=1, source_target_pairs={{0,48},{4,52},{8,56},{12,60},{16,64},{20,68},{24,72},{28,76},{32,8... | collective-permute-start | bytes 24584
  757.2 23.7 %collective-permute-start.26 = (f32[16,128]{1,0:T(8,128)S(1)}, f32[16,128]{1,0:T(8,128)S(1)}, u32[]{:S(2)}, u32[]{:S(2)}) collective-permute-start(f32[16,128]{1,0:T(8,128)S(1)} %get-tuple-element.36), channel_id=1, source_target_pairs={{0,44},{4,48},{8,52},{12,56},{16,60},{20,64},{24,68},{28,72},{32,7... | collective-permute-start | bytes 24584
  758.5 25.8 %collective-permute-start.25 = (f32[16,128]{1,0:T(8,128)S(1)}, f32[16,128]{1,0:T(8,128)S(1)}, u32[]{:S(2)}, u32[]{:S(2)}) collective-permute-start(f32[16,128]{1,0:T(8,128)S(1)} %get-tuple-element.36), channel_id=1, source_target_pairs={{0,40},{4,44},{8,48},{12,52},{16,56},{20,60},{24,64},{28,68},{32,7... | collective-permute-start | bytes 24584
  773.1 13.9 %collective-permute-start.24 = (f32[16,128]{1,0:T(8,128)S(1)}, f32[16,128]{1,0:T(8,128)S(1)}, u32[]{:S(2)}, u32[]{:S(2)}) collective-permute-start(f32[16,128]{1,0:T(8,128)S(1)} %get-tuple-element.36), channel_id=1, source_target_pairs={{0,36},{4,40},{8,44},{12,48},{16,52},{20,56},{24,60},{28,64},{32,6... | collective-permute-start | bytes 24584
  775.4 14.9 %collective-permute-start.23 = (f32[16,128]{1,0:T(8,128)S(1)}, f32[16,128]{1,0:T(8,128)S(1)}, u32[]{:S(2)}, u32[]{:S(2)}) collective-permute-start(f32[16,128]{1,0:T(8,128)S(1)} %get-tuple-element.36), channel_id=1, source_target_pairs={{0,32},{4,36},{8,40},{12,44},{16,48},{20,52},{24,56},{28,60},{32,6... | collective-permute-start | bytes 24584
  780.9 12.5 %collective-permute-start.22 = (f32[16,128]{1,0:T(8,128)S(1)}, f32[16,128]{1,0:T(8,128)S(1)}, u32[]{:S(2)}, u32[]{:S(2)}) collective-permute-start(f32[16,128]{1,0:T(8,128)S(1)} %get-tuple-element.36), channel_id=1, source_target_pairs={{0,28},{4,32},{8,36},{12,40},{16,44},{20,48},{24,52},{28,56},{32,6... | collective-permute-start | bytes 24584
  784.3 11.0 %collective-permute-start.21 = (f32[16,128]{1,0:T(8,128)S(1)}, f32[16,128]{1,0:T(8,128)S(1)}, u32[]{:S(2)}, u32[]{:S(2)}) collective-permute-start(f32[16,128]{1,0:T(8,128)S(1)} %get-tuple-element.36), channel_id=1, source_target_pairs={{0,24},{4,28},{8,32},{12,36},{16,40},{20,44},{24,48},{28,52},{32,5... | collective-permute-start | bytes 24584
  787.1 11.8 %collective-permute-start.20 = (f32[16,128]{1,0:T(8,128)S(1)}, f32[16,128]{1,0:T(8,128)S(1)}, u32[]{:S(2)}, u32[]{:S(2)}) collective-permute-start(f32[16,128]{1,0:T(8,128)S(1)} %get-tuple-element.36), channel_id=1, source_target_pairs={{0,20},{4,24},{8,28},{12,32},{16,36},{20,40},{24,44},{28,48},{32,5... | collective-permute-start | bytes 24584
  790.3 11.1 %collective-permute-start.19 = (f32[16,128]{1,0:T(8,128)S(1)}, f32[16,128]{1,0:T(8,128)S(1)}, u32[]{:S(2)}, u32[]{:S(2)}) collective-permute-start(f32[16,128]{1,0:T(8,128)S(1)} %get-tuple-element.36), channel_id=1, source_target_pairs={{0,16},{4,20},{8,24},{12,28},{16,32},{20,36},{24,40},{28,44},{32,4... | collective-permute-start | bytes 24584
  793.4 9.3 %collective-permute-start.18 = (f32[16,128]{1,0:T(8,128)S(1)}, f32[16,128]{1,0:T(8,128)S(1)}, u32[]{:S(2)}, u32[]{:S(2)}) collective-permute-start(f32[16,128]{1,0:T(8,128)S(1)} %get-tuple-element.36), channel_id=1, source_target_pairs={{0,12},{4,16},{8,20},{12,24},{16,28},{20,32},{24,36},{28,40},{32,4... | collective-permute-start | bytes 24584
  795.3 8.7 %collective-permute-start.17 = (f32[16,128]{1,0:T(8,128)S(1)}, f32[16,128]{1,0:T(8,128)S(1)}, u32[]{:S(2)}, u32[]{:S(2)}) collective-permute-start(f32[16,128]{1,0:T(8,128)S(1)} %get-tuple-element.36), channel_id=1, source_target_pairs={{0,8},{4,12},{8,16},{12,20},{16,24},{20,28},{24,32},{28,36},{32,40... | collective-permute-start | bytes 24584
  801.4 9.9 %collective-permute-start.14 = (f32[768,16]{0,1:T(8,128)}, f32[768,16]{0,1:T(8,128)S(1)}, u32[]{:S(2)}, u32[]{:S(2)}) collective-permute-start(f32[768,16]{0,1:T(8,128)} %get-tuple-element.35), channel_id=1, source_target_pairs={{0,60},{4,64},{8,68},{12,72},{16,76},{20,80},{24,84},{28,88},{32,9... | collective-permute-start | bytes 147464
  802.7 12.4 %collective-permute-start.13 = (f32[768,16]{0,1:T(8,128)}, f32[768,16]{0,1:T(8,128)S(1)}, u32[]{:S(2)}, u32[]{:S(2)}) collective-permute-start(f32[768,16]{0,1:T(8,128)} %get-tuple-element.35), channel_id=1, source_target_pairs={{0,56},{4,60},{8,64},{12,68},{16,72},{20,76},{24,80},{28,84},{32,8... | collective-permute-start | bytes 147464
  804.0 14.3 %collective-permute-start.12 = (f32[768,16]{0,1:T(8,128)}, f32[768,16]{0,1:T(8,128)S(1)}, u32[]{:S(2)}, u32[]{:S(2)}) collective-permute-start(f32[768,16]{0,1:T(8,128)} %get-tuple-element.35), channel_id=1, source_target_pairs={{0,52},{4,56},{8,60},{12,64},{16,68},{20,72},{24,76},{28,80},{32,8... | collective-permute-start | bytes 147464
  805.3 15.8 %collective-permute-start.11 = (f32[768,16]{0,1:T(8,128)}, f32[768,16]{0,1:T(8,128)S(1)}, u32[]{:S(2)}, u32[]{:S(2)}) collective-permute-start(f32[768,16]{0,1:T(8,128)} %get-tuple-element.35), channel_id=1, source_target_pairs={{0,48},{4,52},{8,56},{12,60},{16,64},{20,68},{24,72},{28,76},{32,8... | collective-permute-start | bytes 147464
  807.3 17.0 %collective-permute-start.10 = (f32[768,16]{0,1:T(8,128)}, f32[768,16]{0,1:T(8,128)S(1)}, u32[]{:S(2)}, u32[]{:S(2)}) collective-permute-start(f32[768,16]{0,1:T(8,128)} %get-tuple-element.35), channel_id=1, source_target_pairs={{0,44},{4,48},{8,52},{12,56},{16,60},{20,64},{24,68},{28,72},{32,7... | collective-permute-start | bytes 147464
  811.3 18.8 %collective-permute-start.9 = (f32[768,16]{0,1:T(8,128)}, f32[768,16]{0,1:T(8,128)S(1)}, u32[]{:S(2)}, u32[]{:S(2)}) collective-permute-start(f32[768,16]{0,1:T(8,128)} %get-tuple-element.35), channel_id=1, source_target_pairs={{0,40},{4,44},{8,48},{12,52},{16,56},{20,60},{24,64},{28,68},{32,7... | collective-permute-start | bytes 147464
  815.1 17.4 %collective-permute-start.8 = (f32[768,16]{0,1:T(8,128)}, f32[768,16]{0,1:T(8,128)S(1)}, u32[]{:S(2)}, u32[]{:S(2)}) collective-permute-start(f32[768,16]{0,1:T(8,128)} %get-tuple-element.35), channel_id=1, source_target_pairs={{0,36},{4,40},{8,44},{12,48},{16,52},{20,56},{24,60},{28,64},{32,6... | collective-permute-start | bytes 147464
  818.3 16.4 %collective-permute-start.7 = (f32[768,16]{0,1:T(8,128)}, f32[768,16]{0,1:T(8,128)S(1)}, u32[]{:S(2)}, u32[]{:S(2)}) collective-permute-start(f32[768,16]{0,1:T(8,128)} %get-tuple-element.35), channel_id=1, source_target_pairs={{0,32},{4,36},{8,40},{12,44},{16,48},{20,52},{24,56},{28,60},{32,6... | collective-permute-start | bytes 147464
  821.2 16.3 %collective-permute-start.6 = (f32[768,16]{0,1:T(8,128)}, f32[768,16]{0,1:T(8,128)S(1)}, u32[]{:S(2)}, u32[]{:S(2)}) collective-permute-start(f32[768,16]{0,1:T(8,128)} %get-tuple-element.35), channel_id=1, source_target_pairs={{0,28},{4,32},{8,36},{12,40},{16,44},{20,48},{24,52},{28,56},{32,6... | collective-permute-start | bytes 147464
  824.3 15.6 %collective-permute-start.5 = (f32[768,16]{0,1:T(8,128)}, f32[768,16]{0,1:T(8,128)S(1)}, u32[]{:S(2)}, u32[]{:S(2)}) collective-permute-start(f32[768,16]{0,1:T(8,128)} %get-tuple-element.35), channel_id=1, source_target_pairs={{0,24},{4,28},{8,32},{12,36},{16,40},{20,44},{24,48},{28,52},{32,5... | collective-permute-start | bytes 147464
  830.1 12.5 %collective-permute-start.4 = (f32[768,16]{0,1:T(8,128)}, f32[768,16]{0,1:T(8,128)S(1)}, u32[]{:S(2)}, u32[]{:S(2)}) collective-permute-start(f32[768,16]{0,1:T(8,128)} %get-tuple-element.35), channel_id=1, source_target_pairs={{0,20},{4,24},{8,28},{12,32},{16,36},{20,40},{24,44},{28,48},{32,5... | collective-permute-start | bytes 147464
  832.5 10.0 %collective-permute-start.3 = (f32[768,16]{0,1:T(8,128)}, f32[768,16]{0,1:T(8,128)S(1)}, u32[]{:S(2)}, u32[]{:S(2)}) collective-permute-start(f32[768,16]{0,1:T(8,128)} %get-tuple-element.35), channel_id=1, source_target_pairs={{0,16},{4,20},{8,24},{12,28},{16,32},{20,36},{24,40},{28,44},{32,4... | collective-permute-start | bytes 147464
  (24 other events, 438.6 us)
Sparse Core Ops, SparseCore 0:
  26.6 90.0 all-reduce.15
  513.7 40.5 all-reduce.11
  596.1 192.6 all-reduce.13
where the time goes:
time: 866 us; the launch traced here: 856 us
  waiting for transfers between devices  339 us (39%)
  blocking collectives  202 us (23%)
  local copies, waits for them, and re-layouts  109 us (13%)
  starting transfers between devices  109 us (13%)
  matrix products  68.8 us (8%)
  between operations  16.3 us (2%)
  other arithmetic  12.4 us (1%)
    unnamed x1, blocking collectives  148 us
    all_to_all x1, waiting for transfers between devices, local(): lax.all_to_all(picked, 'dp', split_axis=0, concat_axis=0, tiled=True)  132 us
    all_to_all x1, waiting for transfers between devices, local(): lax.all_to_all(block_back.astype(jnp.bfloat16), 'dp', split_axis=0, conca...  104 us
    unnamed x33, starting transfers between devices  89.9 us
    psum x1, waiting for transfers between devices, local(): lax.psum(query_part.astype(jnp.bfloat16), 'mp').astype(jnp.float32)  61.9 us
    psum x1, waiting for transfers between devices, local(): lax.psum(pass_cot.reshape(p_dev * pass_len, emb_width).astype(jnp.bfloat1...  39.5 us
    convert_element_type x1, local copies, waits for them, and re-layouts, local(): block_back.astype(jnp.bfloat16)  24.9 us
    psum x1, blocking collectives, local(): lax.psum(query_cot.reshape(q_dev * query_len, emb_width).astype(jnp.bfloa...  24.1 us
  transfers between devices with their start and end apart: 37, of which 6 were waited for; matrix products, arithmetic and copies ran while one was open for 20% of the time, Pallas kernels for 0%

commit v1 on v0

v1 whole, which is shorter than its diff:
```python
import jax
import jax.numpy as jnp
from jax import lax
from jax.sharding import PartitionSpec as P

TAU = 0.05
EPS = 1e-06
F32 = jnp.float32
BF16 = jnp.bfloat16


def dot(a, b, dims):
    return lax.dot_general(a, b, (dims, ((), ())), preferred_element_type=F32)


def project(rows, ffn, proj_weight):
    mixed = (rows.astype(F32) + ffn.astype(F32)).astype(BF16)
    projected = dot(mixed, proj_weight, (((mixed.ndim - 1,), (0,))))
    inverse = lax.rsqrt(jnp.sum(projected * projected, axis=-1, keepdims=True) + EPS)
    return mixed, projected * inverse, inverse


def unit_cotangent(g, unit, inverse):
    along = jnp.sum(g * unit, axis=-1, keepdims=True)
    return (inverse * (g - unit * along)).astype(BF16)


def local(
    passage_states,
    query_states,
    lengths,
    owner_map,
    candidates,
    teacher_scores,
    up_weight,
    down_weight,
    proj_weight,
):
    p_dev, pass_len, width = passage_states.shape
    q_dev, q_len, _ = query_states.shape
    emb = proj_weight.shape[1]
    n_dp, n_mp = lax.axis_size("dp"), lax.axis_size("mp")
    me_dp, me_mp = lax.axis_index("dp"), lax.axis_index("mp")
    p_own = p_dev // n_mp
    q_rows = q_dev * q_len
    q_own = q_rows // n_mp
    queries = n_dp * q_dev

    positions = jnp.take(owner_map, candidates)
    table = jnp.stack([positions.astype(F32), teacher_scores], axis=1)
    table = lax.all_gather(table.reshape(q_dev, -1), ("dp", "mp"), axis=0, tiled=True)
    table = table.reshape(n_dp, n_mp, q_dev, 2, -1)
    table = jnp.transpose(table, (3, 0, 2, 1, 4)).reshape(2, queries, -1)
    pos_all, teacher = table[0], table[1]
    teacher_exp = jnp.exp(teacher)
    teacher_sum = jnp.sum(teacher_exp, axis=1)
    teacher_dot = jnp.sum(teacher_exp * teacher, axis=1)
    base = me_dp * p_dev + me_mp * p_own
    mine = base + jnp.arange(p_own)
    hit = pos_all[None] == mine[:, None, None].astype(F32)
    count = jnp.sum(hit.astype(F32), axis=2)
    teacher_mass = jnp.sum(jnp.where(hit, teacher_exp[None], 0.0), axis=2)

    rows_q = query_states.reshape(q_rows, width)
    pre_q = dot(rows_q, up_weight, ((1,), (0,)))
    hid_q = jax.nn.gelu(pre_q).astype(BF16)
    part_q = dot(hid_q, down_weight, ((1,), (0,))).astype(BF16)
    ffn_q = lax.psum_scatter(part_q, "mp", scatter_dimension=0, tiled=True)
    own_q = lax.dynamic_slice_in_dim(rows_q, me_mp * q_own, q_own, 0)
    mixed_q, unit_q, inv_q = project(own_q, ffn_q, proj_weight)
    q_all = lax.all_gather(unit_q.astype(BF16), ("dp", "mp"), axis=0, tiled=True)

    pre_p = dot(passage_states, up_weight, ((2,), (0,)))
    hid_p = jax.nn.gelu(pre_p).astype(BF16)
    part_p = dot(hid_p, down_weight, ((2,), (0,))).astype(BF16)
    ffn_p = lax.psum_scatter(part_p, "mp", scatter_dimension=0, tiled=True)
    own_p = lax.dynamic_slice_in_dim(passage_states, me_mp * p_own, p_own, 0)
    mixed_p, unit_p, inv_p = project(own_p, ffn_p, proj_weight)
    emb_p = unit_p.astype(BF16)

    own_len = lax.dynamic_slice_in_dim(lengths, base, p_own, 0)
    similar = dot(emb_p, q_all, ((2,), (1,)))
    live = jnp.arange(pass_len)[None, :] < own_len[:, None]
    terms = jnp.where(live[:, :, None], jnp.exp(similar / TAU), 0.0)
    denom = jnp.sum(terms, axis=1)
    scores = TAU * jnp.sum(jnp.log(denom).reshape(p_own, queries, q_len), axis=2)
    student = count * jnp.exp(scores)
    sums = lax.psum(
        jnp.stack([jnp.sum(student, axis=0), jnp.sum(teacher_mass * scores, axis=0)]),
        ("dp", "mp"),
    )
    student_sum = sums[0]
    loss = (teacher_dot - sums[1]) / teacher_sum - jnp.log(teacher_sum) + jnp.log(student_sum)
    query_loss = lax.dynamic_slice_in_dim(loss, me_dp * q_dev, q_dev, 0)
    score_cot = student / student_sum - teacher_mass / teacher_sum
    scale = (score_cot[:, :, None] / denom.reshape(p_own, queries, q_len)).reshape(p_own, 1, -1)
    weights = (terms * scale).astype(BF16)
    cot_p = dot(weights, q_all, ((2,), (0,)))
    cot_q = dot(weights, emb_p, ((0, 1), (0, 1))).astype(BF16)
    cot_q = lax.psum_scatter(cot_q, ("dp", "mp"), scatter_dimension=0, tiled=True).astype(F32)

    uc_p = unit_cotangent(cot_p, unit_p, inv_p)
    uc_q = unit_cotangent(cot_q, unit_q, inv_q)
    grad_proj = dot(mixed_p, uc_p, ((0, 1), (0, 1))) + dot(mixed_q, uc_q, ((0,), (0,)))
    uc_p = lax.all_gather(uc_p, "mp", axis=0, tiled=True)
    uc_q = lax.all_gather(uc_q, "mp", axis=0, tiled=True)

    def back(rows, pre, hid, uc):
        axes = tuple(range(rows.ndim - 1))
        last = (rows.ndim - 1,)
        mixed_cot = dot(uc, proj_weight, (last, (1,))).astype(BF16)
        down = dot(mixed_cot, hid, (axes, axes))
        hid_cot = dot(mixed_cot, down_weight, (last, (1,)))
        pre_cot = jax.vjp(jax.nn.gelu, pre)[1](hid_cot)[0].astype(BF16)
        return dot(rows, pre_cot, (axes, axes)), down

    up_p, down_p = back(passage_states, pre_p, hid_p, uc_p)
    up_q, down_q = back(rows_q, pre_q, hid_q, uc_q)
    grads = jnp.concatenate([up_p + up_q, down_p + down_q, grad_proj], axis=1).astype(BF16)
    grads = lax.psum_scatter(grads, "dp", scatter_dimension=0, tiled=True).astype(F32)
    hidden = up_weight.shape[1]
    grad_proj = lax.psum(grads[:, 2 * hidden :], "mp")
    return (query_loss, grads[:, :hidden], grads[:, hidden : 2 * hidden].T, grad_proj)


def solution(mesh):
    return jax.shard_map(
        local,
        mesh=mesh,
        in_specs=(
            P("dp", None, None),
            P("dp", None, None),
            P(),
            P(),
            P("dp", "mp"),
            P("dp", "mp"),
            P(None, "mp"),
            P("mp", None),
            P(),
        ),
        out_specs=(P("dp"), P("dp", "mp"), P("mp", "dp"), P("dp", None)),
        check_vma=False,
    )
```

time: 866 us -> 855 us (0.987)
  waiting for transfers between devices: 339 us -> 498 us
  starting transfers between devices: 109 us -> 0.2 us
  local copies, waits for them, and re-layouts: 109 us -> 10.7 us
  blocking collectives: 202 us -> 232 us
  matrix products: 68.8 us -> 78.7 us
    unnamed x36 -> x7, waiting for transfers between devices: 1.74 us -> 463 us
    all_to_all x2 -> x0, waiting for transfers between devices: 236 us -> none  [the longest x1 132 us: local(): lax.all_to_all(picked, 'dp', split_axis=0, concat_axis=0, tiled=True)]
    unnamed x1 -> x0, blocking collectives: 148 us -> none
    all_gather x0 -> x3, blocking collectives: none -> 141 us  [the longest x1 121 us: local(): lax.all_gather(table.reshape(q_dev, -1), ('dp', 'mp'), axis=0, tiled=True)]
    psum x2 -> x0, waiting for transfers between devices: 101 us -> none  [the longest x1 61.9 us: local(): lax.psum(query_part.astype(jnp.bfloat16), 'mp').astype(jnp.float32)]
    unnamed x33 -> x2, starting transfers between devices: 89.9 us -> 0.08 us
    psum x2, blocking collectives: 31.3 us -> 91.1 us  [the longest x1 77.4 us: local(): lax.psum(jnp.stack([jnp.sum(student, axis=0), jnp.sum(teacher_mass * scor...]
    convert_element_type x2 -> x0, local copies, waits for them, and re-layouts: 26.6 us -> none  [the longest x1 24.9 us: local(): block_back.astype(jnp.bfloat16)]
  transfers between devices with their start and end apart: 37 -> 5, of which waited for: 6 -> 4; matrix products, arithmetic and copies ran while one was open for 20% -> 6% of each run, Pallas kernels for 0% -> 0%
where the time goes in v1:
time: 855 us; the launch traced here: 846 us
  waiting for transfers between devices  498 us (58%)
  blocking collectives  232 us (27%)
  matrix products  78.7 us (9%)
  between operations  15 us (2%)
  other arithmetic  10.9 us (1%)
  local copies, waits for them, and re-layouts  10.7 us (1%)
    unnamed x7, waiting for transfers between devices  463 us
    all_gather x1, blocking collectives, local(): lax.all_gather(table.reshape(q_dev, -1), ('dp', 'mp'), axis=0, tiled=True)  121 us
    dot_general x17, matrix products, dot(): return lax.dot_general(a, b, (dims, ((), ())), preferred_element_type=F32)  78.7 us
    psum x1, blocking collectives, local(): lax.psum(jnp.stack([jnp.sum(student, axis=0), jnp.sum(teacher_mass * scor...  77.4 us
    all_gather x1, waiting for transfers between devices, local(): lax.all_gather(unit_q.astype(BF16), ('dp', 'mp'), axis=0, tiled=True)  24.4 us
  transfers between devices with their start and end apart: 5, of which 4 were waited for; matrix products, arithmetic and copies ran while one was open for 6% of the time, Pallas kernels for 0%

profile of v1, /device:TPU:1, one launch (start us, length us, event | category | flops | bytes accessed | tf_op | source)
XLA Modules:
  0.0 845.7 jit_solution(8222616005173502417)
XLA Ops:
  7.2 1.8 fusion.84
  9.0 1.0 convolution_convert_fusion.3
  10.1 5.2 fusion.26
  15.3 2.7 copy-done.11
  18.0 5.6 convolution_convert_fusion.1
  23.7 11.4 %reduce-scatter.9.cloned.1.call-done = bf16[24,768]{1,0:T(8,128)(2,1)} async-done(((bf16[96,768]{1,0:T(8,128)(2,1)}), bf16[24,768]{1,0:T(8,128)(2,1)}) %reduce-scatter.9.cloned.1.call-update) | async-done | bytes 36880 | tf_op jit(solution)/shard_map/reduce_scatter | solution.py:68
  35.1 1.0 multiply_reduce_fusion.3
  37.9 121.3 %all-gather = f32[256,3,32]{2,1,0:T(4,128)S(1)} all-gather(f32[1,3,32]{2,1,0:T(4,128)S(1)} %reshape.147), channel_id=1, replica_groups=mesh['dp'=64,'mp'=4] {'dp','mp'}, dimensions={0}, use_global_device_ids=true | all-gather | bytes 98688 | tf_op jit(solution)/shard_map/all_gather | solution.py:51
  159.7 2.4 multiply_reduce_fusion
  164.1 2.0 multiply_reduce_fusion.1
  166.1 24.4 %all-gather.3.cloned.1.call-done = bf16[6144,128]{1,0:T(8,128)(2,1)} async-done(((bf16[24,128]{1,0:T(8,128)(2,1)}), bf16[6144,128]{1,0:T(8,128)(2,1)}) %all-gather.3.cloned.1.call-update) | async-done | bytes 1572880 | tf_op jit(solution)/shard_map/all_gather | solution.py:71
  190.5 8.1 fusion.1
  199.0 77.4 %psum.14 = f32[2,192]{1,0:T(2,128)S(1)} all-reduce(f32[2,192]{1,0:T(2,128)S(1)} %pad_maximum_fusion.2), channel_id=1, replica_groups=mesh['dp'=64,'mp'=4] {'dp','mp'}, use_global_device_ids=true, to_apply=%region_11.12 | all-reduce | flops 384 | bytes 3072 | tf_op jit(solution)/shard_map/psum | solution.py:88
  277.3 9.5 %fusion.2 = bf16[6144,128]{1,0:T(8,128)(2,1)} fusion(f32[3,180,6144]{2,1,0:T(8,128)} %get-tuple-element.37, f32[3,6144]{1,0:T(4,128)S(1)} %div.56, pred[3,180]{1,0:T(4,128)(4,1)S(1)} %iota_compare_fusion, f32[3,180,128]{2,1,0:T(8,128)S(1)} %get-tuple-element.35, f32[3,180]{1,0:T(4,128)S(1)} %add_rsqrt_fusion), kind=kOutput, calls=%fused_computation.8 | convolution fusion | flops 863542272 | bytes 15196812 | tf_op jit(solution)/shard_map/dot_general | solution.py:13
  286.8 6.9 fusion.18
  293.7 2.7 fusion.32
  296.5 10.2 %all_gather.14 = bf16[12,180,128]{2,1,0:T(8,128)(2,1)S(1)} all-gather(bf16[3,180,128]{2,1,0:T(8,128)(2,1)S(1)} %fusion.32), channel_id=1, replica_groups=mesh['dp'=64,'mp'=4] {'mp'}, dimensions={0}, use_global_device_ids=true | all-gather | bytes 691200 | tf_op jit(solution)/shard_map/all_gather | solution.py:105
  306.6 1.1 convolution_convert_fusion
  307.7 9.4 %fusion.80 = f32[768,768,1]{0,1,2:T(8,128)} fusion(bf16[12,180,768]{2,1,0:T(8,128)(2,1)S(1)} %convolution_convert_fusion, f32[12,180,768]{2,1,0:T(8,128)} %copy-done.11), kind=kOutput, calls=%fused_computation.125 | convolution fusion | flops 2562969600 | bytes 12312576 | tf_op jit(solution)/shard_map/dot_general | solution.py:13
  317.1 1.6 convolution_bitcast_fusion.1
  318.8 19.5 %fusion.10 = f32[768,768,1]{1,0,2:T(8,128)} fusion(bf16[12,180,768]{2,1,0:T(8,128)(2,1)} %param.9, f32[12,180,768]{2,1,0:T(8,128)} %copy-done.11, bf16[12,180,768]{2,1,0:T(8,128)(2,1)} %copy-done.3, bf16[768,768]{1,0:T(8,128)(2,1)S(1)} %copy-done), kind=kOutput, calls=%fused_computation.17 | convolution fusion | flops 5129256960 | bytes 16809984 | tf_op jit(solution)/shard_map/dot_general | solution.py:13
  338.2 269.3 %reduce-scatter.11.cloned.1.call-done = bf16[24,128]{1,0:T(8,128)(2,1)} async-done(((bf16[6144,128]{1,0:T(8,128)(2,1)}), bf16[24,128]{1,0:T(8,128)(2,1)}) %reduce-scatter.11.cloned.1.call-update) | async-done | bytes 6160
  607.5 0.9 fusion.55
  608.4 0.8 fusion.57
  609.2 9.3 %all_gather.15 = bf16[96,128]{1,0:T(8,128)(2,1)S(1)} all-gather(bf16[24,128]{1,0:T(8,128)(2,1)S(1)} %fusion.57), channel_id=1, replica_groups=mesh['dp'=64,'mp'=4] {'mp'}, dimensions={0}, use_global_device_ids=true | all-gather | bytes 30720 | tf_op jit(solution)/shard_map/all_gather | solution.py:106
  618.7 2.7 fusion.22
  621.4 2.2 fusion.16
  623.7 1.0 fusion.28
  624.7 1.7 pad_maximum_fusion
  628.5 193.1 %all-reduce.4.cloned.1.call-done = bf16[768,1664]{0,1:T(8,128)(2,1)} async-done(((bf16[768,1664]{0,1:T(8,128)(2,1)}), bf16[768,1664]{0,1:T(8,128)(2,1)}) %all-reduce.4.cloned.1.call-update) | async-done | bytes 2555920
  821.7 1.3 dynamic-slice_convert_fusion
  823.8 13.7 %psum.15 = f32[12,128]{0,1:T(8,128)S(1)} all-reduce(f32[12,128]{0,1:T(8,128)S(1)} %slice.38), channel_id=1, replica_groups=mesh['dp'=64,'mp'=4] {'mp'}, use_global_device_ids=true, to_apply=%region_17.18 | all-reduce | flops 1536 | bytes 12288 | tf_op jit(solution)/shard_map/psum | solution.py:122
  (81 shorter events, 9.7 us)
Async XLA Ops:
  7.2 1.8 copy-start
  7.2 27.9 %reduce-scatter.9.cloned.1.call-start = ((), (), s32[]{:S(2)}) async-start(), calls=%async_computation.4 | async-start | bytes 184320 | tf_op jit(solution)/shard_map/reduce_scatter | solution.py:68
  10.0 154.0 %reduce-scatter.7.cloned.1.call-start = ((), (), s32[]{:S(2)}) async-start(), calls=%async_computation.3 | async-start | bytes 4239360 | tf_op jit(solution)/shard_map/reduce_scatter | solution.py:76
  15.3 2.7 copy-start.11
  18.0 17.1 %copy-start.4 = (bf16[768,128]{1,0:T(8,128)(2,1)S(1)}, bf16[768,128]{1,0:T(8,128)(2,1)}, u32[]{:S(2)}) copy-start(bf16[768,128]{1,0:T(8,128)(2,1)} %param.17) | copy-start | bytes 589828
  18.0 17.1 %copy-start.5 = (bf16[3,32,768]{2,1,0:T(8,128)(2,1)S(1)}, bf16[3,32,768]{2,1,0:T(8,128)(2,1)}, u32[]{:S(2)}) copy-start(bf16[3,32,768]{2,1,0:T(8,128)(2,1)} %param.10) | copy-start | bytes 442372
  18.0 18.9 %copy-start.7 = (s32[3,16]{1,0:T(4,128)S(1)}, s32[3,16]{1,0:T(4,128)}, u32[]{:S(2)}) copy-start(s32[3,16]{1,0:T(4,128)} %param.13) | copy-start | bytes 580
  23.6 13.4 %copy-start.1 = (s32[768]{0:T(1024)S(1)}, s32[768]{0:T(1024)}, u32[]{:S(2)}) copy-start(s32[768]{0:T(1024)} %param.12) | copy-start | bytes 9220
  23.6 14.3 %copy-start.9 = (f32[3,16]{1,0:T(4,128)S(1)}, f32[3,16]{1,0:T(4,128)}, u32[]{:S(2)}) copy-start(f32[3,16]{1,0:T(4,128)} %param.14) | copy-start | bytes 580
  23.6 166.9 %all-gather.3.cloned.1.call-start = ((), (), s32[]{:S(2)}) async-start(), calls=%async_computation.5 | async-start | bytes 1579008 | tf_op jit(solution)/shard_map/all_gather | solution.py:71
  36.8 570.7 %reduce-scatter.11.cloned.1.call-start = ((), (), s32[]{:S(2)}) async-start(), calls=%async_computation.7 | async-start | bytes 1579008
  296.4 525.2 %all-reduce.4.cloned.1.call-start = ((), (), s32[]{:S(2)}) async-start(), calls=%async_computation.6 | async-start | bytes 5111808
  307.7 9.4 %copy-start.3 = (bf16[12,180,768]{2,1,0:T(8,128)(2,1)}, bf16[12,180,768]{2,1,0:T(8,128)(2,1)S(1)}, u32[]{:S(2)}) copy-start(bf16[12,180,768]{2,1,0:T(8,128)(2,1)S(1)} %convolution_convert_fusion) | copy-start | bytes 9953284
  307.7 9.4 %copy-start.2 = (bf16[3,180,768]{2,1,0:T(8,128)(2,1)S(1)}, bf16[3,180,768]{2,1,0:T(8,128)(2,1)}, u32[]{:S(2)}) copy-start(bf16[3,180,768]{2,1,0:T(8,128)(2,1)} %reduce-scatter.7.cloned.1.call-done) | copy-start | bytes 2488324
  623.6 2.8 copy-start.6
  623.6 3.0 copy-start.10
  623.7 4.2 copy-start.8
Sparse Core Ops, SparseCore 0:
  10.5 24.5 reduce-scatter.8
  37.8 45.0 reduce-scatter.6
  87.6 102.8 all-gather.2
  296.6 310.9 reduce-scatter.10
  626.5 195.1 all-reduce.3

commit v2 on v1

v2 whole, which is shorter than its diff:
```python
import functools

import jax
import jax.numpy as jnp
from jax import lax
from jax.experimental import pallas as pl
from jax.experimental.pallas import tpu as pltpu
from jax.sharding import PartitionSpec as P

TAU = 0.05
EPS = 1e-06
F32 = jnp.float32
BF16 = jnp.bfloat16
NY, NZ, NC, NX = 4, 8, 2, 4
MESH = pl.DeviceIdType.MESH
VMEM = pl.BlockSpec(memory_space=pltpu.VMEM)


def dot(a, b, dims):
    return lax.dot_general(a, b, (dims, ((), ())), preferred_element_type=F32)


def place():
    dp, x = lax.axis_index("dp"), lax.axis_index("mp")
    return dp // (NZ * NC), (dp // NC) % NZ, dp % NC, x


def at(y, z, c, x):
    return ((y * NZ + z) * NC + c, x)


def peers(axis):
    y, z, c, x = place()
    out = []
    size = {"x": NX, "y": NY, "z": NZ, "c": NC}[axis]
    mine = {"x": x, "y": y, "z": z, "c": c}[axis]
    for k in range(1, size):
        to = (mine + k) % size
        frm = (mine + size - k) % size
        who = {"x": (y, z, c, to), "y": (to, z, c, x), "z": (y, to, c, x), "c": (y, z, to, x)}[axis]
        out.append((k, at(*who), to, frm))
    return out


def greet(axes):
    barrier = pltpu.get_barrier_semaphore()
    total = 0
    for axis in axes:
        for _, who, _, _ in peers(axis):
            pl.semaphore_signal(barrier, inc=1, device_id=who, device_id_type=MESH)
            total += 1
    pl.semaphore_wait(barrier, total)


class Stage:
    def __init__(self, axis, send_sem, recv_sem):
        self.axis, self.send_sem, self.recv_sem = axis, send_sem, recv_sem
        self.sent = []

    def start(self, src, dst):
        for k, who, to, _ in peers(self.axis):
            copy = pltpu.make_async_remote_copy(
                src_ref=src(to),
                dst_ref=dst(k),
                send_sem=self.send_sem.at[k - 1],
                recv_sem=self.recv_sem.at[k - 1],
                device_id=who,
                device_id_type=MESH,
            )
            copy.start()
            self.sent.append(copy)

    def arrive(self, dst):
        for k, who, _, frm in peers(self.axis):
            ref = dst(k, frm)
            pltpu.make_async_remote_copy(
                src_ref=ref,
                dst_ref=ref,
                send_sem=self.send_sem.at[k - 1],
                recv_sem=self.recv_sem.at[k - 1],
                device_id=who,
                device_id_type=MESH,
            ).wait_recv()

    def finish(self):
        for copy in self.sent:
            copy.wait_send()


def sems(n):
    return [pltpu.SemaphoreType.DMA((max(n, 1),)), pltpu.SemaphoreType.DMA((max(n, 1),))]


def call(kernel, outs, scratch, number, *args):
    return pl.pallas_call(
        kernel,
        out_shape=outs,
        in_specs=[VMEM] * len(args),
        out_specs=[VMEM] * len(outs),
        scratch_shapes=scratch,
        compiler_params=pltpu.CompilerParams(
            collective_id=number, has_side_effects=True, vmem_limit_bytes=48 * 2**20
        ),
        cost_estimate=pl.CostEstimate(flops=10**9, bytes_accessed=60 * 10**6, transcendentals=0),
    )(*args)


def gather_kernel(
    part, rows, proj, table, q_all, t_all, mixed, unit, inverse, pbuf, tbuf, *sem
):
    y, z, c, x = place()
    greet("xzyc")
    sx, tx = Stage("x", sem[0], sem[1]), Stage("x", sem[2], sem[3])
    sz, tz = Stage("z", sem[4], sem[5]), Stage("z", sem[6], sem[7])
    sy, ty = Stage("y", sem[8], sem[9]), Stage("y", sem[10], sem[11])
    sc, tc = Stage("c", sem[12], sem[13]), Stage("c", sem[14], sem[15])
    tx.start(lambda to: table, lambda k: tbuf.at[x])
    sx.start(lambda to: part, lambda k: pbuf.at[x])
    tbuf[x] = table[...]
    pbuf[x] = part[...]
    tx.arrive(lambda k, frm: tbuf.at[frm])
    merged = tbuf[0]
    for i in range(1, NX):
        merged = merged + tbuf[i]
    t_all[c, y, z] = merged
    tz.start(lambda to: t_all.at[c, y, z], lambda k: t_all.at[c, y, z])
    sx.arrive(lambda k, frm: pbuf.at[frm])
    ffn = pbuf[0].astype(F32)
    for i in range(1, NX):
        ffn = ffn + pbuf[i].astype(F32)
    blend = (rows[...].astype(F32) + ffn).astype(BF16)
    mixed[...] = blend
    projected = jnp.dot(blend, proj[...], preferred_element_type=F32)
    inv = lax.rsqrt(jnp.sum(projected * projected, axis=-1, keepdims=True) + EPS)
    inverse[...] = inv
    unit[...] = projected * inv
    q_all[c, y, z] = (projected * inv).astype(BF16)
    sz.start(lambda to: q_all.at[c, y, z], lambda k: q_all.at[c, y, z])
    tz.arrive(lambda k, frm: t_all.at[c, y, frm])
    ty.start(lambda to: t_all.at[c, y], lambda k: t_all.at[c, y])
    sz.arrive(lambda k, frm: q_all.at[c, y, frm])
    sy.start(lambda to: q_all.at[c, y], lambda k: q_all.at[c, y])
    ty.arrive(lambda k, frm: t_all.at[c, frm])
    tc.start(lambda to: t_all.at[c], lambda k: t_all.at[c])
    sy.arrive(lambda k, frm: q_all.at[c, frm])
    sc.start(lambda to: q_all.at[c], lambda k: q_all.at[c])
    tc.arrive(lambda k, frm: t_all.at[frm])
    sc.arrive(lambda k, frm: q_all.at[frm])
    for stage in (sx, tx, sz, tz, sy, ty, sc, tc):
        stage.finish()


def gather_queries(part, rows, proj, table):
    n, width = part.shape
    emb = proj.shape[1]
    shape = jax.ShapeDtypeStruct
    outs = [
        shape((NC, NY, NZ, n, emb), BF16),
        shape((NC, NY, NZ) + table.shape, F32),
        shape((n, width), BF16),
        shape((n, emb), F32),
        shape((n, 1), F32),
    ]
    scratch = [pltpu.VMEM((NX, n, width), BF16), pltpu.VMEM((NX,) + table.shape, F32)]
    for size in (NX, NX, NZ, NZ, NY, NY, NC, NC):
        scratch += sems(size - 1)
    return call(gather_kernel, outs, scratch, 1, part, rows, proj, table)


def total_kernel(vec, out, abuf, bbuf, *sem):
    y, z, c, x = place()
    barrier = pltpu.get_barrier_semaphore()
    groups = [
        (NY * NX, y * NX + x, lambda i: at(i // NX, z, c, i % NX)),
        (NZ * NC, z * NC + c, lambda i: at(y, i // NC, i % NC, x)),
    ]
    for size, mine, who in groups:
        for k in range(1, size):
            pl.semaphore_signal(
                barrier, inc=1, device_id=who((mine + k) % size), device_id_type=MESH
            )
    pl.semaphore_wait(barrier, NY * NX + NZ * NC - 2)
    held = vec
    for (size, mine, who), buf, send, recv in zip(
        groups, (abuf, bbuf), (sem[0], sem[2]), (sem[1], sem[3])
    ):
        copies = []
        buf[mine] = held[...]
        for k in range(1, size):
            copy = pltpu.make_async_remote_copy(
                src_ref=held,
                dst_ref=buf.at[mine],
                send_sem=send.at[k - 1],
                recv_sem=recv.at[k - 1],
                device_id=who((mine + k) % size),
                device_id_type=MESH,
            )
            copy.start()
            copies.append(copy)
        for k in range(1, size):
            ref = buf.at[(mine + size - k) % size]
            pltpu.make_async_remote_copy(
                src_ref=ref,
                dst_ref=ref,
                send_sem=send.at[k - 1],
                recv_sem=recv.at[k - 1],
                device_id=who((mine + k) % size),
                device_id_type=MESH,
            ).wait_recv()
        total = buf[0]
        for i in range(1, size):
            total = total + buf[i]
        for copy in copies:
            copy.wait_send()
        out[...] = total
        held = out


def total(vec):
    outs = [jax.ShapeDtypeStruct(vec.shape, F32)]
    scratch = [
        pltpu.VMEM((NY * NX,) + vec.shape, F32),
        pltpu.VMEM((NZ * NC,) + vec.shape, F32),
    ] + sems(NY * NX - 1) + sems(NZ * NC - 1)
    return call(total_kernel, outs, scratch, 2, vec)[0]


def add_into(dst, index, first, others):
    def body(i, carry):
        value = first(i).astype(F32)
        for other in others:
            value = value + other[i].astype(F32)
        dst[i] = value.astype(dst.dtype)
        return carry

    lax.fori_loop(0, index, body, 0)


def cot_kernel(cot, uc, out, uc_all, cbuf, abuf, ybuf, bbuf, zbuf, xbuf, *sem):
    y, z, c, x = place()
    greet("xzyc")
    sc, su = Stage("c", sem[0], sem[1]), Stage("x", sem[2], sem[3])
    sy, sz, sx = Stage("y", sem[4], sem[5]), Stage("z", sem[6], sem[7]), Stage("x", sem[8], sem[9])
    sc.start(lambda to: cot.at[to], lambda k: cbuf)
    su.start(lambda to: uc, lambda k: uc_all.at[x])
    uc_all[x] = uc[...]
    sc.arrive(lambda k, frm: cbuf)
    for i in range(NY):
        add_into(abuf.at[i], NZ, lambda j: cot[c, i, j], [cbuf.at[i]])
    sy.start(lambda to: abuf.at[to], lambda k: ybuf.at[k - 1])
    sy.arrive(lambda k, frm: ybuf.at[k - 1])
    add_into(bbuf, NZ, lambda j: abuf[y, j], [ybuf.at[i] for i in range(NY - 1)])
    sz.start(lambda to: bbuf.at[to], lambda k: zbuf.at[k - 1])
    sz.arrive(lambda k, frm: zbuf.at[k - 1])
    value = bbuf[z].astype(F32)
    for i in range(NZ - 1):
        value = value + zbuf[i].astype(F32)
    xbuf[x] = value.astype(BF16)
    sx.start(lambda to: xbuf.at[x], lambda k: xbuf.at[x])
    sx.arrive(lambda k, frm: xbuf.at[frm])
    value = xbuf[0].astype(F32)
    for i in range(1, NX):
        value = value + xbuf[i].astype(F32)
    out[...] = value
    su.arrive(lambda k, frm: uc_all.at[frm])
    for stage in (sc, su, sy, sz, sx):
        stage.finish()


def exchange_cot(cot, uc):
    n, emb = cot.shape[-2:]
    outs = [
        jax.ShapeDtypeStruct((n, emb), F32),
        jax.ShapeDtypeStruct((NX,) + uc.shape, BF16),
    ]
    scratch = [
        pltpu.VMEM((NY, NZ, n, emb), BF16),
        pltpu.VMEM((NY, NZ, n, emb), BF16),
        pltpu.VMEM((NY - 1, NZ, n, emb), BF16),
        pltpu.VMEM((NZ, n, emb), BF16),
        pltpu.VMEM((NZ - 1, n, emb), BF16),
        pltpu.VMEM((NX, n, emb), BF16),
    ]
    for size in (NC, NX, NY, NZ, NX):
        scratch += sems(size - 1)
    return call(cot_kernel, outs, scratch, 3, cot, uc)


def grad_kernel(emb, grads, out, proj_out, cbuf, abuf, ybuf, bbuf, zbuf, xbuf, *sem):
    y, z, c, x = place()
    greet("xzyc")
    sc = Stage("c", sem[0], sem[1])
    sy, sz, sx = Stage("y", sem[2], sem[3]), Stage("z", sem[4], sem[5]), Stage("x", sem[6], sem[7])
    sc.start(lambda to: grads.at[to], lambda k: cbuf)
    sc.arrive(lambda k, frm: cbuf)
    for i in range(NY):
        add_into(abuf.at[i], NZ, lambda j: grads[c, i, j], [cbuf.at[i]])
    sy.start(lambda to: abuf.at[to], lambda k: ybuf.at[k - 1])
    sy.arrive(lambda k, frm: ybuf.at[k - 1])
    add_into(bbuf, NZ, lambda j: abuf[y, j], [ybuf.at[i] for i in range(NY - 1)])
    sz.start(lambda to: bbuf.at[to], lambda k: zbuf.at[k - 1])
    sz.arrive(lambda k, frm: zbuf.at[k - 1])
    value = bbuf[z].astype(F32)
    for i in range(NZ - 1):
        value = value + zbuf[i].astype(F32)
    width = value.shape[1] - emb
    out[...] = value[:, :width]
    xbuf[x] = value[:, width:]
    sx.start(lambda to: xbuf.at[x], lambda k: xbuf.at[x])
    sx.arrive(lambda k, frm: xbuf.at[frm])
    value = xbuf[0]
    for i in range(1, NX):
        value = value + xbuf[i]
    proj_out[...] = value
    for stage in (sc, sy, sz, sx):
        stage.finish()


def exchange_grads(grads, emb):
    n, width = grads.shape[-2:]
    outs = [
        jax.ShapeDtypeStruct((n, width - emb), F32),
        jax.ShapeDtypeStruct((n, emb), F32),
    ]
    scratch = [
        pltpu.VMEM((NY, NZ, n, width), BF16),
        pltpu.VMEM((NY, NZ, n, width), BF16),
        pltpu.VMEM((NY - 1, NZ, n, width), BF16),
        pltpu.VMEM((NZ, n, width), BF16),
        pltpu.VMEM((NZ - 1, n, width), BF16),
        pltpu.VMEM((NX, n, emb), F32),
    ]
    for size in (NC, NY, NZ, NX):
        scratch += sems(size - 1)
    return call(functools.partial(grad_kernel, emb), outs, scratch, 4, grads)


def unit_cotangent(g, unit, inverse):
    along = jnp.sum(g * unit, axis=-1, keepdims=True)
    return (inverse * (g - unit * along)).astype(BF16)


def local(
    passage_states,
    query_states,
    lengths,
    owner_map,
    candidates,
    teacher_scores,
    up_weight,
    down_weight,
    proj_weight,
):
    p_dev, pass_len, width = passage_states.shape
    q_dev, q_len, _ = query_states.shape
    emb = proj_weight.shape[1]
    hidden = up_weight.shape[1]
    n_dp = NY * NZ * NC
    me_dp, me_mp = lax.axis_index("dp"), lax.axis_index("mp")
    y, z, c, _ = place()
    my_block = (c * NY + y) * NZ + z
    p_own = p_dev // NX
    q_rows = q_dev * q_len
    q_own = q_rows // NX
    queries = n_dp * q_dev
    cands = candidates.shape[1]
    all_cands = cands * NX

    rows_q = query_states.reshape(q_rows, width)
    pre_q = dot(rows_q, up_weight, ((1,), (0,)))
    hid_q = jax.nn.gelu(pre_q).astype(BF16)
    part_q = dot(hid_q, down_weight, ((1,), (0,))).astype(BF16)
    pre_p = dot(passage_states, up_weight, ((2,), (0,)))
    hid_p = jax.nn.gelu(pre_p).astype(BF16)
    part_p = dot(hid_p, down_weight, ((2,), (0,))).astype(BF16)

    positions = jnp.take(owner_map, candidates).astype(F32)
    table = jnp.zeros((8, 2 * all_cands), F32)
    table = lax.dynamic_update_slice(table, positions, (0, me_mp * cands))
    table = lax.dynamic_update_slice(table, teacher_scores, (0, all_cands + me_mp * cands))

    part_p, part_q = lax.optimization_barrier((part_p, part_q))
    ffn_p = lax.psum_scatter(part_p, "mp", scatter_dimension=0, tiled=True)
    q_all, t_all, mixed_q, unit_q, inv_q = gather_queries(part_q, rows_q, proj_weight, table)
    q_all = q_all.reshape(n_dp * q_rows, emb)
    table = t_all.reshape(n_dp, 8, 2 * all_cands)[:, :q_dev].reshape(queries, -1)
    pos_all, teacher = table[:, :all_cands], table[:, all_cands:]
    teacher_exp = jnp.exp(teacher)
    teacher_sum = jnp.sum(teacher_exp, axis=1)
    teacher_dot = jnp.sum(teacher_exp * teacher, axis=1)
    base = me_dp * p_dev + me_mp * p_own
    mine = base + jnp.arange(p_own)
    hit = pos_all[None] == mine[:, None, None].astype(F32)
    count = jnp.sum(hit.astype(F32), axis=2)
    teacher_mass = jnp.sum(jnp.where(hit, teacher_exp[None], 0.0), axis=2)

    own_p = lax.dynamic_slice_in_dim(passage_states, me_mp * p_own, p_own, 0)
    mixed_p = (own_p.astype(F32) + ffn_p.astype(F32)).astype(BF16)
    projected = dot(mixed_p, proj_weight, ((2,), (0,)))
    inv_p = lax.rsqrt(jnp.sum(projected * projected, axis=-1, keepdims=True) + EPS)
    unit_p = projected * inv_p
    emb_p = unit_p.astype(BF16)

    own_len = lax.dynamic_slice_in_dim(lengths, base, p_own, 0)
    similar = dot(emb_p, q_all, ((2,), (1,)))
    live = jnp.arange(pass_len)[None, :] < own_len[:, None]
    terms = jnp.where(live[:, :, None], jnp.exp(similar / TAU), 0.0)
    denom = jnp.sum(terms, axis=1)
    scores = TAU * jnp.sum(jnp.log(denom).reshape(p_own, queries, q_len), axis=2)
    student = count * jnp.exp(scores)
    sums = jnp.stack([jnp.sum(student, axis=0), jnp.sum(teacher_mass * scores, axis=0)])
    sums = jnp.pad(sums.reshape(-1), (0, 1024 - 2 * queries)).reshape(8, 128)
    sums = total(sums).reshape(-1)[: 2 * queries].reshape(2, queries)
    student_sum = sums[0]
    loss = (teacher_dot - sums[1]) / teacher_sum - jnp.log(teacher_sum) + jnp.log(student_sum)
    query_loss = lax.dynamic_slice_in_dim(loss, my_block * q_dev, q_dev, 0)
    score_cot = student / student_sum - teacher_mass / teacher_sum
    scale = (score_cot[:, :, None] / denom.reshape(p_own, queries, q_len)).reshape(p_own, 1, -1)
    weights = (terms * scale).astype(BF16)
    cot_q = dot(weights, emb_p, ((0, 1), (0, 1))).astype(BF16)
    cot_p = dot(weights, q_all, ((2,), (0,)))
    uc_p = unit_cotangent(cot_p, unit_p, inv_p)

    pad_len = (pass_len + 15) // 16 * 16
    cot_q, uc_all = exchange_cot(
        cot_q.reshape(NC, NY, NZ, q_rows, emb),
        jnp.pad(uc_p, ((0, 0), (0, pad_len - pass_len), (0, 0))),
    )
    uc_q = unit_cotangent(cot_q, unit_q, inv_q)
    own_mixed = lax.dynamic_slice_in_dim(mixed_q, me_mp * q_own, q_own, 0)
    own_uc = lax.dynamic_slice_in_dim(uc_q, me_mp * q_own, q_own, 0)
    grad_proj = dot(mixed_p, uc_p, ((0, 1), (0, 1))) + dot(own_mixed, own_uc, ((0,), (0,)))
    uc_p = uc_all.reshape(p_dev, pad_len, emb)[:, :pass_len]

    def back(rows, pre, hid, uc):
        axes = tuple(range(rows.ndim - 1))
        last = (rows.ndim - 1,)
        mixed_cot = dot(uc, proj_weight, (last, (1,))).astype(BF16)
        down = dot(mixed_cot, hid, (axes, axes))
        hid_cot = dot(mixed_cot, down_weight, (last, (1,)))
        pre_cot = jax.vjp(jax.nn.gelu, pre)[1](hid_cot)[0].astype(BF16)
        return dot(rows, pre_cot, (axes, axes)), down

    up_p, down_p = back(passage_states, pre_p, hid_p, uc_p)
    up_q, down_q = back(rows_q, pre_q, hid_q, uc_q)
    grads = jnp.concatenate([up_p + up_q, down_p + down_q, grad_proj], axis=1).astype(BF16)
    rows = width // n_dp
    grads = jnp.pad(grads.reshape(NY, NZ, NC, rows, -1), ((0, 0),) * 3 + ((0, -rows % 16), (0, 0)))
    grads, grad_proj = exchange_grads(jnp.transpose(grads, (2, 0, 1, 3, 4)), emb)
    return (
        query_loss,
        grads[:rows, :hidden],
        grads[:rows, hidden:].T,
        grad_proj[:rows],
    )


def solution(mesh):
    return jax.shard_map(
        local,
        mesh=mesh,
        in_specs=(
            P("dp", None, None),
            P("dp", None, None),
            P(),
            P(),
            P("dp", "mp"),
            P("dp", "mp"),
            P(None, "mp"),
            P("mp", None),
            P(),
        ),
        out_specs=(P("dp"), P("dp", "mp"), P("mp", "dp"), P("dp", None)),
        check_vma=False,
    )
```

time: 855 us -> 237 us (0.28)
  waiting for transfers between devices: 498 us -> 2.56 us
  blocking collectives: 232 us -> 0 us
  Pallas kernels: 0 us -> 121 us
  local copies, waits for them, and re-layouts: 10.7 us -> 21 us
  matrix products: 78.7 us -> 69.2 us
    unnamed x7 -> x1, waiting for transfers between devices: 463 us -> 0.02 us
    all_gather x3 -> x0, blocking collectives: 141 us -> none  [the longest x1 121 us: local(): lax.all_gather(table.reshape(q_dev, -1), ('dp', 'mp'), axis=0, tiled=True)]
    pallas_call x0 -> x4, Pallas kernels: none -> 121 us  [call(): pl.pallas_call(kernel, out_shape=outs, in_specs=[VMEM] * len(args), out_s...]
    psum x2 -> x0, blocking collectives: 91.1 us -> none  [the longest x1 77.4 us: local(): lax.psum(jnp.stack([jnp.sum(student, axis=0), jnp.sum(teacher_mass * scor...]
    all_gather x1 -> x0, waiting for transfers between devices: 24.4 us -> none  [local(): lax.all_gather(unit_q.astype(BF16), ('dp', 'mp'), axis=0, tiled=True)]
    reduce_scatter x1 -> x0, waiting for transfers between devices: 11.4 us -> none  [local(): ffn_q = lax.psum_scatter(part_q, 'mp', scatter_dimension=0, tiled=True)]
    dot_general x17 -> x16, matrix products: 78.7 us -> 69.2 us  [dot(): return lax.dot_general(a, b, (dims, ((), ())), preferred_element_type=F32)]
  transfers between devices with their start and end apart: 5 -> 1, of which waited for: 4 -> 1; matrix products, arithmetic and copies ran while one was open for 6% -> 3% of each run, Pallas kernels for 0% -> 16%
where the time goes in v2:
time: 237 us; the launch traced here: 236 us
  Pallas kernels  121 us (51%)
  matrix products  69.2 us (29%)
  local copies, waits for them, and re-layouts  21 us (9%)
  between operations  14.5 us (6%)
  other arithmetic  7.36 us (3%)
  waiting for transfers between devices  2.56 us (1%)
    pallas_call x4, Pallas kernels, call(): pl.pallas_call(kernel, out_shape=outs, in_specs=[VMEM] * len(args), out_s...  121 us
    dot_general x16, matrix products, dot(): return lax.dot_general(a, b, (dims, ((), ())), preferred_element_type=F32)  69.2 us
    concatenate x3, local copies, waits for them, and re-layouts, local(): jnp.concatenate([up_p + up_q, down_p + down_q, grad_proj], axis=1)  5.35 us
    unnamed x33, local copies, waits for them, and re-layouts  5.29 us
  transfers between devices with their start and end apart: 1, of which 1 were waited for; matrix products, arithmetic and copies ran while one was open for 3% of the time, Pallas kernels for 16%

profile of v2, /device:TPU:1, one launch (start us, length us, event | category | flops | bytes accessed | tf_op | source)
XLA Modules:
  0.0 236.1 jit_solution(1263196089991945269)
XLA Ops:
  7.2 1.8 fusion.81
  9.0 5.3 %fusion.22 = f32[12,180,768]{2,1,0:T(8,128)S(1)} fusion(bf16[12,180,768]{2,1,0:T(8,128)(2,1)} %param.9, bf16[768,768]{1,0:T(8,128)(2,1)} %param.15), kind=kOutput, calls=%fused_computation.37 | convolution fusion | flops 2548039680 | bytes 11132928 | tf_op jit(solution)/shard_map/dot_general | solution.py:20
  14.7 2.4 copy-done.13
  17.0 5.6 %convolution_convert_fusion.1 = bf16[12,180,768]{2,1,0:T(8,128)(2,1)} fusion(bf16[768,768]{1,0:T(8,128)(2,1)S(1)} %copy-done, f32[12,180,768]{2,1,0:T(8,128)S(1)} %fusion.22), kind=kOutput, calls=%fused_computation.26 | convolution fusion | flops 2564628480 | bytes 11132928 | tf_op jit(solution)/shard_map/dot_general | solution.py:20
  25.1 38.5 %shard_map.120 = (bf16[2,4,8,96,128]{4,3,2,1,0:T(8,128)(2,1)S(1)}, f32[2,4,8,8,128]{4,3,2,1,0:T(8,128)S(1)}, bf16[96,768]{1,0:T(8,128)(2,1)S(1)}, f32[96,128]{1,0:T(8,128)S(1)}, f32[96,1]{1,0:T(8,128)S(1)}) custom-call(bf16[96,768]{1,0:T(8,128)(2,1)S(1)} %convolution_convert_fusion.3.part, bf16[96,768]{1,0:T(8,128)(2,1)S(1)} %bitcast.69, ...), custom_call_target="tpu_custom_call" | custom-call | flops 1000000000 | bytes 60000000 | tf_op jit(solution)/shard_map/pallas_call | solution.py:95
  64.3 1.0 reshape.139
  66.0 1.0 copy.16
  66.9 1.0 copy.17
  67.9 0.8 dynamic_slice.15
  69.5 2.5 %reduce-scatter.2.cloned.1.call-done = bf16[3,180,768]{2,1,0:T(8,128)(2,1)} async-done(((bf16[12,180,768]{2,1,0:T(8,128)(2,1)}), bf16[3,180,768]{2,1,0:T(8,128)(2,1)}) %reduce-scatter.2.cloned.1.call-update) | async-done | bytes 829456 | tf_op jit(solution)/shard_map/reduce_scatter | solution.py:383
  72.1 1.9 multiply_reduce_fusion
  74.0 6.7 %fusion.1 = (f32[3,6144]{1,0:T(4,128)S(1)}, f32[3,180,6144]{2,1,0:T(8,128)}) fusion(pred[3,180]{1,0:T(4,128)(4,1)S(1)} %iota_compare_fusion, bf16[6144,128,1]{1,0,2:T(8,128)(2,1)S(1)} %bitcast.74, f32[3,180,128]{2,1,0:T(8,128)S(1)} %get-tuple-element.39, f32[3,180]{1,0:T(4,128)S(1)} %add_rsqrt_fusion), kind=kOutput, calls=%fused_computation.4 | convolution fusion | flops 859419648 | bytes 15196812 | tf_op jit(solution)/shard_map/dot_general | solution.py:20
  80.8 0.9 log.14
  81.6 1.1 reduce_sum.103
  82.9 14.8 %shard_map.121 = f32[8,128]{1,0:T(8,128)S(1)} custom-call(f32[8,128]{1,0:T(8,128)S(1)} %pad_bitcast_fusion.1.vec), custom_call_target="tpu_custom_call" | custom-call | flops 1000000000 | bytes 60000000 | tf_op jit(solution)/shard_map/pallas_call | solution.py:95
  97.8 0.9 div.75
  98.7 1.1 div.76
  99.9 6.8 %fusion.52 = f32[3,180,128]{2,1,0:T(8,128)S(1)} fusion(bf16[6144,128,1]{1,0,2:T(8,128)(2,1)S(1)} %bitcast.75, f32[3,180,6144]{2,1,0:T(8,128)} %get-tuple-element.41, f32[3,6144]{1,0:T(4,128)S(1)} %div.77, pred[3,180]{1,0:T(4,128)(4,1)S(1)} %iota_compare_fusion), kind=kOutput, calls=%fused_computation.76 | convolution fusion | flops 862617600 | bytes 15194652 | tf_op jit(solution)/shard_map/dot_general | solution.py:20
  106.7 8.4 %fusion.2 = bf16[6144,128]{1,0:T(8,128)(2,1)S(1)} fusion(f32[3,180,6144]{2,1,0:T(8,128)} %get-tuple-element.41, f32[3,6144]{1,0:T(4,128)S(1)} %div.77, pred[3,180]{1,0:T(4,128)(4,1)S(1)} %iota_compare_fusion, f32[3,180,128]{2,1,0:T(8,128)S(1)} %copy-done.9, f32[3,180]{1,0:T(4,128)S(1)} %add_rsqrt_fusion), kind=kOutput, calls=%fused_computation.8 | convolution fusion | flops 863542272 | bytes 15196812 | tf_op jit(solution)/shard_map/dot_general | solution.py:20
  115.1 2.7 %fusion.28 = bf16[3,180,128]{2,1,0:T(8,128)(2,1)S(1)} fusion(f32[3,180,128]{2,1,0:T(8,128)S(1)} %fusion.52, f32[3,180,128]{2,1,0:T(8,128)S(1)} %copy-done.9, f32[3,180]{1,0:T(4,128)S(1)} %add_rsqrt_fusion), kind=kOutput, calls=%fused_computation.45 | output fusion | flops 484507 | bytes 693360 | tf_op jit(solution)/shard_map/mul | solution.py:340
  117.9 27.0 %shard_map.122 = (f32[96,128]{1,0:T(8,128)S(1)}, bf16[4,3,192,128]{3,2,1,0:T(8,128)(2,1)S(1)}) custom-call(bf16[2,4,8,96,128]{4,3,2,1,0:T(8,128)(2,1)S(1)} %bitcast.76, bf16[3,192,128]{2,1,0:T(8,128)(2,1)S(1)} %pad.13.uc), custom_call_target="tpu_custom_call" | custom-call | flops 1000000000 | bytes 60000000 | tf_op jit(solution)/shard_map/pallas_call | solution.py:95
  144.9 1.1 convolution_convert_fusion
  146.0 1.7 copy-done.7
  147.7 4.6 %fusion.77 = f32[768,768,1]{1,0,2:T(8,128)} fusion(bf16[12,180,768]{2,1,0:T(8,128)(2,1)S(1)} %convolution_convert_fusion, f32[12,180,768]{2,1,0:T(8,128)S(1)} %bitcast.83), kind=kOutput, calls=%fused_computation.118 | convolution fusion | flops 2562969600 | bytes 12312576 | tf_op jit(solution)/shard_map/dot_general | solution.py:20
  152.3 17.9 %fusion.10 = f32[768,768,1]{0,1,2:T(8,128)} fusion(bf16[12,180,768]{2,1,0:T(8,128)(2,1)} %param.9, f32[12,180,768]{2,1,0:T(8,128)} %copy-done.13, bf16[12,180,768]{2,1,0:T(8,128)(2,1)} %copy-done.7, bf16[768,768]{1,0:T(8,128)(2,1)S(1)} %copy-done), kind=kOutput, calls=%fused_computation.19 | convolution fusion | flops 5129256960 | bytes 16809984 | tf_op jit(solution)/shard_map/dot_general | solution.py:20
  170.7 1.6 convolution_bitcast_fusion.1
  172.6 3.6 %fusion.18 = bf16[768,768]{1,0:T(8,128)(2,1)} fusion(bf16[96,768]{1,0:T(8,128)(2,1)S(1)} %bitcast.70, f32[768,768,1]{0,1,2:T(8,128)} %fusion.10, f32[96,768]{1,0:T(8,128)S(1)} %copy-done.5, bf16[96,768]{1,0:T(8,128)(2,1)S(1)} %convolution_convert_fusion.2, bf16[768,768]{1,0:T(8,128)(2,1)S(1)} %copy-done), kind=kOutput, calls=%fused_computation.32 | convolution fusion | flops 229146624 | bytes 5308416 | tf_op jit(solution)/shard_map/dot_general | solution.py:20
  176.2 3.2 %fusion.16 = bf16[768,768]{1,0:T(8,128)(2,1)} fusion(f32[768,768,1]{1,0,2:T(8,128)} %fusion.77, bf16[96,768]{1,0:T(8,128)(2,1)S(1)} %convolution_convert_fusion.2, f32[96,768]{1,0:T(8,128)S(1)} %copy-done.5), kind=kOutput, calls=%fused_computation.28 | convolution fusion | flops 115089408 | bytes 3981312 | tf_op jit(solution)/shard_map/dot_general | solution.py:20
  179.4 2.2 concatenate.12
  181.6 3.2 %concatenate.11 = bf16[4,8,2,12,768]{4,3,2,1,0:T(8,128)(2,1)} reshape(bf16[768,768]{1,0:T(8,128)(2,1)} %fusion.18) | data formatting | bytes 2359296 | tf_op jit(solution)/shard_map/concatenate | solution.py:446
  184.7 1.6 pad_bitcast_fusion.grads
  186.4 41.1 %shard_map.123 = (f32[16,1536]{1,0:T(8,128)S(1)}, f32[16,128]{1,0:T(8,128)S(1)}) custom-call(bf16[2,4,8,16,1664]{4,3,2,1,0:T(8,128)(2,1)S(1)} %pad_bitcast_fusion.grads), custom_call_target="tpu_custom_call" | custom-call | flops 1000000000 | bytes 60000000 | tf_op jit(solution)/shard_map/pallas_call | solution.py:95
  (70 shorter events, 7.9 us)
Async XLA Ops:
  7.2 7.2 %copy-start = (bf16[768,768]{1,0:T(8,128)(2,1)S(1)}, bf16[768,768]{1,0:T(8,128)(2,1)}, u32[]{:S(2)}) copy-start(bf16[768,768]{1,0:T(8,128)(2,1)} %param.16) | copy-start | bytes 3538948
  7.2 64.9 %reduce-scatter.2.cloned.1.call-start = ((), (), s32[]{:S(2)}) async-start(), calls=%async_computation.1 | async-start | bytes 4239360 | tf_op jit(solution)/shard_map/reduce_scatter | solution.py:383
  9.0 5.3 %copy-start.4 = (f32[96,768]{1,0:T(8,128)}, f32[96,768]{1,0:T(8,128)S(1)}, u32[]{:S(2)}) copy-start(f32[96,768]{1,0:T(8,128)S(1)} %fusion.81) | copy-start | bytes 884740
  14.3 2.7 %copy-start.13 = (f32[12,180,768]{2,1,0:T(8,128)}, f32[12,180,768]{2,1,0:T(8,128)S(1)}, u32[]{:S(2)}) copy-start(f32[12,180,768]{2,1,0:T(8,128)S(1)} %fusion.22) | copy-start | bytes 19906564
  22.6 0.7 copy-start.10
  22.6 0.8 copy-start.3
  22.6 1.9 copy-start.12
  22.6 2.4 %copy-start.1 = (bf16[768,128]{1,0:T(8,128)(2,1)S(1)}, bf16[768,128]{1,0:T(8,128)(2,1)}, u32[]{:S(2)}) copy-start(bf16[768,128]{1,0:T(8,128)(2,1)} %proj.1) | copy-start | bytes 589828
  22.6 2.5 %copy-start.2 = (bf16[3,32,768]{2,1,0:T(8,128)(2,1)S(1)}, bf16[3,32,768]{2,1,0:T(8,128)(2,1)}, u32[]{:S(2)}) copy-start(bf16[3,32,768]{2,1,0:T(8,128)(2,1)} %param.10) | copy-start | bytes 442372
  74.0 6.7 %copy-start.8 = (f32[3,180,128]{2,1,0:T(8,128)}, f32[3,180,128]{2,1,0:T(8,128)S(1)}, u32[]{:S(2)}) copy-start(f32[3,180,128]{2,1,0:T(8,128)S(1)} %get-tuple-element.39) | copy-start | bytes 829444
  99.9 6.8 %copy-start.9 = (f32[3,180,128]{2,1,0:T(8,128)S(1)}, f32[3,180,128]{2,1,0:T(8,128)}, u32[]{:S(2)}) copy-start(f32[3,180,128]{2,1,0:T(8,128)} %copy-done.8) | copy-start | bytes 829444
  99.9 47.8 %slice-start = ((s8[6782976]{0:T(1024)(128)(4,1)}), s8[4194304]{0:T(1024)(128)(4,1)S(1)}, s32[]{:S(2)}) async-start(s8[6782976]{0:T(1024)(128)(4,1)} %bitcast.82), calls=%async_computation.2 | async-start | bytes 8388608
  106.7 41.0 %slice-start.1 = ((s8[6782976]{0:T(1024)(128)(4,1)}), s8[2588672]{0:T(1024)(128)(4,1)S(1)}, s32[]{:S(2)}) async-start(s8[6782976]{0:T(1024)(128)(4,1)} %bitcast.82), calls=%async_computation.3 | async-start | bytes 5177344
  146.0 1.7 copy-start.7
  152.3 18.0 %copy-start.11 = (f32[96]{0:T(128)S(1)}, f32[96]{0:T(128)}, u32[]{:S(2)}) copy-start(f32[96]{0:T(128)} %reduce) | copy-start | bytes 1156
  152.3 18.3 %copy-start.6 = (bf16[3,180,768]{2,1,0:T(8,128)(2,1)S(1)}, bf16[3,180,768]{2,1,0:T(8,128)(2,1)}, u32[]{:S(2)}) copy-start(bf16[3,180,768]{2,1,0:T(8,128)(2,1)} %reduce-scatter.2.cloned.1.call-done) | copy-start | bytes 2488324
  170.2 2.4 %copy-start.5 = (f32[96,768]{1,0:T(8,128)S(1)}, f32[96,768]{1,0:T(8,128)}, u32[]{:S(2)}) copy-start(f32[96,768]{1,0:T(8,128)} %copy-done.4) | copy-start | bytes 884740
Sparse Core Ops, SparseCore 0:
  22.8 49.2 reduce-scatter.1

commit v3 on v2

--- a/solution.py
+++ b/solution.py
@@ -99,7 +99,7 @@
         out_specs=[VMEM] * len(outs),
         scratch_shapes=scratch,
         compiler_params=pltpu.CompilerParams(
-            collective_id=number, has_side_effects=True, vmem_limit_bytes=48 * 2**20
+            collective_id=number, has_side_effects=True, vmem_limit_bytes=56 * 2**20
         ),
         cost_estimate=pl.CostEstimate(flops=10**9, bytes_accessed=60 * 10**6, transcendentals=0),
     )(*args)
@@ -236,108 +236,238 @@
     lax.fori_loop(0, index, body, 0)
 
 
-def cot_kernel(cot, uc, out, uc_all, cbuf, abuf, ybuf, bbuf, zbuf, xbuf, *sem):
+def nt(a, b):
+    return dot(a, b, ((1,), (1,)))
+
+
+TILE = 256
+
+
+def back_kernel(
+    cot, uc, rows, hid, dgelu, mixed, rows_q, hid_q, dgelu_q, mixed_q, unit_q, inv_q, down, proj,
+    projp, perm,
+    out_up, out_down, out_proj,
+    uc_all, cbuf, abuf, ybuf, bbuf, zbuf, xbuf, mc, mct, rowst, mixedt, mcq, mctq, rowstq, ucq,
+    acc_up, acc_down, acc_proj,
+    gd, gu, gp, cd, cu, cp, ad, au, ap, yd, yu, yp, fd, fu, fp, bd, bu, bp, zd, zu, zp, xp, *sem
+):
     y, z, c, x = place()
+    sem = list(sem)
+
+    def stage(axis):
+        send, recv = sem.pop(0), sem.pop(0)
+        return Stage(axis, send, recv)
+
     greet("xzyc")
-    sc, su = Stage("c", sem[0], sem[1]), Stage("x", sem[2], sem[3])
-    sy, sz, sx = Stage("y", sem[4], sem[5]), Stage("z", sem[6], sem[7]), Stage("x", sem[8], sem[9])
+    sc, su, sy, sz, sx = (stage(a) for a in "cxyzx")
     sc.start(lambda to: cot.at[to], lambda k: cbuf)
     su.start(lambda to: uc, lambda k: uc_all.at[x])
     uc_all[x] = uc[...]
+    width = down.shape[1]
+    tiles = width // TILE
+
+    def cut(j):
+        return pl.ds(pl.multiple_of(j * TILE, TILE), TILE)
+
+    def prepare(u, r, m, mt, rt):
+        def body(j, carry):
+            m[:, cut(j)] = nt(u[...], proj[cut(j), :]).astype(BF16)
+            mt[cut(j), :] = nt(projp[cut(j), :], u[...]).astype(BF16)
+            rt[cut(j), :] = nt(perm[cut(j), :], r[...]).astype(BF16)
+            return carry
+
+        lax.fori_loop(0, tiles, body, 0)
+
+    def passages(g, first):
+        u, r = uc_all.at[g], rows.at[g]
+        prepare(u, r, mc, mct, rowst)
+
+        def body(j, carry):
+            term = jnp.dot(mct[...], hid[g, :, cut(j)], preferred_element_type=F32)
+            back = nt(mc[...], down[cut(j), :])
+            pre = (back * dgelu[g, :, cut(j)]).astype(BF16)
+            up = jnp.dot(rowst[...], pre, preferred_element_type=F32)
+            if first:
+                acc_down[:, cut(j)] = term
+                acc_up[:, cut(j)] = up
+            else:
+                acc_down[:, cut(j)] += term
+                acc_up[:, cut(j)] += up
+            return carry
+
+        lax.fori_loop(0, tiles, body, 0)
+
+    passages(x, True)
+
+    def mix(j, carry):
+        mixedt[cut(j), :] = nt(perm[cut(j), :], mixed[...]).astype(BF16)
+        return carry
+
+    lax.fori_loop(0, tiles, mix, 0)
+    acc_proj[...] = jnp.dot(mixedt[...], uc[...], preferred_element_type=F32)
+
     sc.arrive(lambda k, frm: cbuf)
     for i in range(NY):
         add_into(abuf.at[i], NZ, lambda j: cot[c, i, j], [cbuf.at[i]])
     sy.start(lambda to: abuf.at[to], lambda k: ybuf.at[k - 1])
+    su.arrive(lambda k, frm: uc_all.at[frm])
+    passages(lax.rem(x + 3, NX), False)
     sy.arrive(lambda k, frm: ybuf.at[k - 1])
     add_into(bbuf, NZ, lambda j: abuf[y, j], [ybuf.at[i] for i in range(NY - 1)])
     sz.start(lambda to: bbuf.at[to], lambda k: zbuf.at[k - 1])
+    passages(lax.rem(x + 1, NX), False)
     sz.arrive(lambda k, frm: zbuf.at[k - 1])
     value = bbuf[z].astype(F32)
     for i in range(NZ - 1):
         value = value + zbuf[i].astype(F32)
     xbuf[x] = value.astype(BF16)
     sx.start(lambda to: xbuf.at[x], lambda k: xbuf.at[x])
+    passages(lax.rem(x + 2, NX), False)
     sx.arrive(lambda k, frm: xbuf.at[frm])
-    value = xbuf[0].astype(F32)
+    g = xbuf[0].astype(F32)
     for i in range(1, NX):
-        value = value + xbuf[i].astype(F32)
-    out[...] = value
-    su.arrive(lambda k, frm: uc_all.at[frm])
-    for stage in (sc, su, sy, sz, sx):
-        stage.finish()
-
-
-def exchange_cot(cot, uc):
+        g = g + xbuf[i].astype(F32)
+    along = jnp.sum(g * unit_q[...], axis=-1, keepdims=True)
+    n = g.shape[0]
+    ucq[...] = jnp.zeros(ucq.shape, BF16)
+    ucq[0:n, :] = (inv_q[...] * (g - unit_q[...] * along)).astype(BF16)
+    prepare(ucq, rows_q, mcq, mctq, rowstq)
+    blocks = gd.shape[:3]
+
+    def down_last(j, carry):
+        term = acc_down[:, cut(j)] + jnp.dot(
+            mctq[...], hid_q[:, cut(j)], preferred_element_type=F32
+        )
+        gd[:, :, :, cut(j)] = term.astype(BF16).reshape(blocks + (TILE,))
+        return carry
+
+    lax.fori_loop(0, tiles, down_last, 0)
+    chunks = []
+    for grads, near, total_a, far, f32_sum, padded, last in (
+        (gd, cd, ad, yd, fd, bd, zd),
+        (gp, cp, ap, yp, fp, bp, zp),
+        (gu, cu, au, yu, fu, bu, zu),
+    ):
+        chunks.append((grads, near, total_a, far, f32_sum, padded, last) + tuple(stage(a) for a in "cyz"))
+
+    def leave(chunk):
+        chunk[7].start(lambda to: chunk[0].at[to], lambda k: chunk[1])
+
+    leave(chunks[0])
+
+    def mixq(j, carry):
+        mctq[cut(j), :] = nt(perm[cut(j), :], mixed_q[...]).astype(BF16)
+        return carry
+
+    lax.fori_loop(0, tiles, mixq, 0)
+    part = n // NX
+    at_row = lax.broadcasted_iota(jnp.int32, ucq.shape, 0)
+    mine = jnp.logical_and(at_row >= x * part, at_row < (x + 1) * part)
+    own = jnp.where(mine, ucq[...].astype(F32), 0.0).astype(BF16)
+    term = acc_proj[...] + jnp.dot(mctq[...], own, preferred_element_type=F32)
+    gp[...] = term.astype(BF16).reshape(gp.shape)
+    leave(chunks[1])
+
+    def up_last(j, carry):
+        back = nt(mcq[...], down[cut(j), :])
+        pre = (back * dgelu_q[:, cut(j)]).astype(BF16)
+        up = acc_up[:, cut(j)] + jnp.dot(rowstq[...], pre, preferred_element_type=F32)
+        gu[:, :, :, cut(j)] = up.astype(BF16).reshape(blocks + (TILE,))
+        return carry
+
+    lax.fori_loop(0, tiles, up_last, 0)
+    leave(chunks[2])
+
+    for grads, near, total_a, far, f32_sum, padded, last, s1, s2, s3 in chunks:
+        s1.arrive(lambda k, frm: near)
+        add_into(total_a, NY, lambda j: grads[c, j], [near])
+        s2.start(lambda to: total_a.at[to], lambda k: far.at[k - 1])
+    per = width // (NY * NZ * NC)
+    for grads, near, total_a, far, f32_sum, padded, last, s1, s2, s3 in chunks:
+        s2.arrive(lambda k, frm: far.at[k - 1])
+        value = total_a[y].astype(F32)
+        for i in range(NY - 1):
+            value = value + far[i].astype(F32)
+        tall = value.shape[0]
+        f32_sum[0:tall, :] = value
+        f32_sum[tall : tall + 8, :] = jnp.zeros((8, value.shape[1]), F32)
+        for i in range(NZ):
+            padded[i] = f32_sum[i * per : i * per + 16, :].astype(BF16)
+        s3.start(lambda to: padded.at[to], lambda k: last.at[k - 1])
+    finals = []
+    s4 = stage("x")
+    for at_chunk in (1, 0, 2):
+        grads, near, total_a, far, f32_sum, padded, last, s1, s2, s3 = chunks[at_chunk]
+        s3.arrive(lambda k, frm: last.at[k - 1])
+        value = padded[z].astype(F32)
+        for i in range(NZ - 1):
+            value = value + last[i].astype(F32)
+        if at_chunk == 1:
+            xp[x] = value
+            s4.start(lambda to: xp.at[x], lambda k: xp.at[x])
+        elif at_chunk == 0:
+            out_down[...] = value
+        else:
+            out_up[...] = value
+    s4.arrive(lambda k, frm: xp.at[frm])
+    value = xp[0]
+    for i in range(1, NX):
+        value = value + xp[i]
+    out_proj[...] = value
+    for s in [sc, su, sy, sz, sx, s4] + [s for chunk in chunks for s in chunk[7:]]:
+        s.finish()
+
+
+def backward(*args):
+    cot, uc, rows, hid, _, _, rows_q = args[:7]
     n, emb = cot.shape[-2:]
-    outs = [
-        jax.ShapeDtypeStruct((n, emb), F32),
-        jax.ShapeDtypeStruct((NX,) + uc.shape, BF16),
+    many, width = rows.shape[1:]
+    hidden = hid.shape[2]
+    few = rows_q.shape[0]
+    tall = width // (NC * NY)
+    V = pltpu.VMEM
+    outs = [jax.ShapeDtypeStruct((16, w), F32) for w in (hidden, hidden, emb)]
+    scratch = [
+        V((NX, many, emb), BF16),
+        V((NY, NZ, n, emb), BF16),
+        V((NY, NZ, n, emb), BF16),
+        V((NY - 1, NZ, n, emb), BF16),
+        V((NZ, n, emb), BF16),
+        V((NZ - 1, n, emb), BF16),
+        V((NX, n, emb), BF16),
+        V((many, width), BF16),
+        V((width, many), BF16),
+        V((width, many), BF16),
+        V((width, many), BF16),
+        V((few, width), BF16),
+        V((width, few), BF16),
+        V((width, few), BF16),
+        V((few, emb), BF16),
+        V((width, hidden), F32),
+        V((width, hidden), F32),
+        V((width, emb), F32),
     ]
-    scratch = [
-        pltpu.VMEM((NY, NZ, n, emb), BF16),
-        pltpu.VMEM((NY, NZ, n, emb), BF16),
-        pltpu.VMEM((NY - 1, NZ, n, emb), BF16),
-        pltpu.VMEM((NZ, n, emb), BF16),
-        pltpu.VMEM((NZ - 1, n, emb), BF16),
-        pltpu.VMEM((NX, n, emb), BF16),
-    ]
-    for size in (NC, NX, NY, NZ, NX):
-        scratch += sems(size - 1)
-    return call(cot_kernel, outs, scratch, 3, cot, uc)
-
-
-def grad_kernel(emb, grads, out, proj_out, cbuf, abuf, ybuf, bbuf, zbuf, xbuf, *sem):
-    y, z, c, x = place()
-    greet("xzyc")
-    sc = Stage("c", sem[0], sem[1])
-    sy, sz, sx = Stage("y", sem[2], sem[3]), Stage("z", sem[4], sem[5]), Stage("x", sem[6], sem[7])
-    sc.start(lambda to: grads.at[to], lambda k: cbuf)
-    sc.arrive(lambda k, frm: cbuf)
-    for i in range(NY):
-        add_into(abuf.at[i], NZ, lambda j: grads[c, i, j], [cbuf.at[i]])
-    sy.start(lambda to: abuf.at[to], lambda k: ybuf.at[k - 1])
-    sy.arrive(lambda k, frm: ybuf.at[k - 1])
-    add_into(bbuf, NZ, lambda j: abuf[y, j], [ybuf.at[i] for i in range(NY - 1)])
-    sz.start(lambda to: bbuf.at[to], lambda k: zbuf.at[k - 1])
-    sz.arrive(lambda k, frm: zbuf.at[k - 1])
-    value = bbuf[z].astype(F32)
-    for i in range(NZ - 1):
-        value = value + zbuf[i].astype(F32)
-    width = value.shape[1] - emb
-    out[...] = value[:, :width]
-    xbuf[x] = value[:, width:]
-    sx.start(lambda to: xbuf.at[x], lambda k: xbuf.at[x])
-    sx.arrive(lambda k, frm: xbuf.at[frm])
-    value = xbuf[0]
-    for i in range(1, NX):
-        value = value + xbuf[i]
-    proj_out[...] = value
-    for stage in (sc, sy, sz, sx):
-        stage.finish()
-
-
-def exchange_grads(grads, emb):
-    n, width = grads.shape[-2:]
-    outs = [
-        jax.ShapeDtypeStruct((n, width - emb), F32),
-        jax.ShapeDtypeStruct((n, emb), F32),
-    ]
-    scratch = [
-        pltpu.VMEM((NY, NZ, n, width), BF16),
-        pltpu.VMEM((NY, NZ, n, width), BF16),
-        pltpu.VMEM((NY - 1, NZ, n, width), BF16),
-        pltpu.VMEM((NZ, n, width), BF16),
-        pltpu.VMEM((NZ - 1, n, width), BF16),
-        pltpu.VMEM((NX, n, emb), F32),
-    ]
-    for size in (NC, NY, NZ, NX):
-        scratch += sems(size - 1)
-    return call(functools.partial(grad_kernel, emb), outs, scratch, 4, grads)
+    wide = (hidden, hidden, emb)
+    scratch += [V((NC, NY, tall, w), BF16) for w in wide]
+    scratch += [V((NY, tall, w), BF16) for w in wide]
+    scratch += [V((NY, tall, w), BF16) for w in wide]
+    scratch += [V((NY - 1, tall, w), BF16) for w in wide]
+    scratch += [V((tall + 8, w), F32) for w in wide]
+    scratch += [V((NZ, 16, w), BF16) for w in wide]
+    scratch += [V((NZ - 1, 16, w), BF16) for w in wide]
+    scratch += [V((NX, 16, emb), F32)]
+    for a in "cxyzx" + "cyz" * 3 + "x":
+        scratch += sems({"x": NX, "y": NY, "z": NZ, "c": NC}[a] - 1)
+    return call(back_kernel, outs, scratch, 3, *args)
 
 
 def unit_cotangent(g, unit, inverse):
     along = jnp.sum(g * unit, axis=-1, keepdims=True)
     return (inverse * (g - unit * along)).astype(BF16)
+
+
+def gelu_slope(v):
+    return jax.vjp(jax.nn.gelu, v)[1](jnp.ones_like(v))[0]
 
 
 def local(
@@ -361,11 +491,13 @@
     my_block = (c * NY + y) * NZ + z
     p_own = p_dev // NX
     q_rows = q_dev * q_len
-    q_own = q_rows // NX
+    rows = width // n_dp
     queries = n_dp * q_dev
     cands = candidates.shape[1]
     all_cands = cands * NX
 
+    pad_len = (pass_len + 15) // 16 * 16
+    passage_states = jnp.pad(passage_states, ((0, 0), (0, pad_len - pass_len), (0, 0)))
     rows_q = query_states.reshape(q_rows, width)
     pre_q = dot(rows_q, up_weight, ((1,), (0,)))
     hid_q = jax.nn.gelu(pre_q).astype(BF16)
@@ -382,6 +514,8 @@
     part_p, part_q = lax.optimization_barrier((part_p, part_q))
     ffn_p = lax.psum_scatter(part_p, "mp", scatter_dimension=0, tiled=True)
     q_all, t_all, mixed_q, unit_q, inv_q = gather_queries(part_q, rows_q, proj_weight, table)
+    q_all, pre_p, pre_q = lax.optimization_barrier((q_all, pre_p, pre_q))
+    dgelu_p, dgelu_q = gelu_slope(pre_p), gelu_slope(pre_q)
     q_all = q_all.reshape(n_dp * q_rows, emb)
     table = t_all.reshape(n_dp, 8, 2 * all_cands)[:, :q_dev].reshape(queries, -1)
     pos_all, teacher = table[:, :all_cands], table[:, all_cands:]
@@ -403,7 +537,7 @@
 
     own_len = lax.dynamic_slice_in_dim(lengths, base, p_own, 0)
     similar = dot(emb_p, q_all, ((2,), (1,)))
-    live = jnp.arange(pass_len)[None, :] < own_len[:, None]
+    live = jnp.arange(pad_len)[None, :] < own_len[:, None]
     terms = jnp.where(live[:, :, None], jnp.exp(similar / TAU), 0.0)
     denom = jnp.sum(terms, axis=1)
     scores = TAU * jnp.sum(jnp.log(denom).reshape(p_own, queries, q_len), axis=2)
@@ -421,38 +555,32 @@
     cot_p = dot(weights, q_all, ((2,), (0,)))
     uc_p = unit_cotangent(cot_p, unit_p, inv_p)
 
-    pad_len = (pass_len + 15) // 16 * 16
-    cot_q, uc_all = exchange_cot(
+    few = (q_rows + 127) // 128 * 128
+    more = ((0, few - q_rows), (0, 0))
+    order = jnp.arange(width).reshape(NC, NY, NZ, rows)
+    order = (((order // (NZ * rows)) % NY * NZ + (order // rows) % NZ) * NC + order // (NY * NZ * rows)) * rows
+    order = (order + jnp.arange(rows)).reshape(width)
+    perm = (order[:, None] == jnp.arange(width)[None, :]).astype(BF16)
+    proj_order = jnp.transpose(proj_weight.reshape(NY, NZ, NC, rows, emb), (2, 0, 1, 3, 4))
+    up, down, grad_proj = backward(
         cot_q.reshape(NC, NY, NZ, q_rows, emb),
-        jnp.pad(uc_p, ((0, 0), (0, pad_len - pass_len), (0, 0))),
+        uc_p.reshape(p_own * pad_len, emb),
+        passage_states.reshape(NX, p_own * pad_len, width),
+        hid_p.reshape(NX, p_own * pad_len, hidden),
+        dgelu_p.reshape(NX, p_own * pad_len, hidden),
+        mixed_p.reshape(p_own * pad_len, width),
+        jnp.pad(rows_q, more),
+        jnp.pad(hid_q, more),
+        jnp.pad(dgelu_q, more),
+        jnp.pad(mixed_q, more),
+        unit_q,
+        inv_q,
+        down_weight,
+        proj_weight,
+        proj_order.reshape(width, emb),
+        perm,
     )
-    uc_q = unit_cotangent(cot_q, unit_q, inv_q)
-    own_mixed = lax.dynamic_slice_in_dim(mixed_q, me_mp * q_own, q_own, 0)
-    own_uc = lax.dynamic_slice_in_dim(uc_q, me_mp * q_own, q_own, 0)
-    grad_proj = dot(mixed_p, uc_p, ((0, 1), (0, 1))) + dot(own_mixed, own_uc, ((0,), (0,)))
-    uc_p = uc_all.reshape(p_dev, pad_len, emb)[:, :pass_len]
-
-    def back(rows, pre, hid, uc):
-        axes = tuple(range(rows.ndim - 1))
-        last = (rows.ndim - 1,)
-        mixed_cot = dot(uc, proj_weight, (last, (1,))).astype(BF16)
-        down = dot(mixed_cot, hid, (axes, axes))
-        hid_cot = dot(mixed_cot, down_weight, (last, (1,)))
-        pre_cot = jax.vjp(jax.nn.gelu, pre)[1](hid_cot)[0].astype(BF16)
-        return dot(rows, pre_cot, (axes, axes)), down
-
-    up_p, down_p = back(passage_states, pre_p, hid_p, uc_p)
-    up_q, down_q = back(rows_q, pre_q, hid_q, uc_q)
-    grads = jnp.concatenate([up_p + up_q, down_p + down_q, grad_proj], axis=1).astype(BF16)
-    rows = width // n_dp
-    grads = jnp.pad(grads.reshape(NY, NZ, NC, rows, -1), ((0, 0),) * 3 + ((0, -rows % 16), (0, 0)))
-    grads, grad_proj = exchange_grads(jnp.transpose(grads, (2, 0, 1, 3, 4)), emb)
-    return (
-        query_loss,
-        grads[:rows, :hidden],
-        grads[:rows, hidden:].T,
-        grad_proj[:rows],
-    )
+    return query_loss, up[:rows], down[:rows].T, grad_proj[:rows]
 
 
 def solution(mesh):

time: 237 us -> 224 us (0.945)
  matrix products: 69.2 us -> 40.5 us
  Pallas kernels: 121 us -> 130 us
  other arithmetic: 7.36 us -> 15.4 us
  waiting for transfers between devices: 2.56 us -> 0.02 us
    dot_general x16 -> x8, matrix products: 69.2 us -> 40.5 us  [dot(): return lax.dot_general(a, b, (dims, ((), ())), preferred_element_type=F32)]
    pallas_call x4 -> x3, Pallas kernels: 121 us -> 130 us  [call(): pl.pallas_call(kernel, out_shape=outs, in_specs=[VMEM] * len(args), out_s...]
    add_any x0 -> x2, other arithmetic: none -> 8.2 us  [gelu_slope(): return jax.vjp(jax.nn.gelu, v)[1](jnp.ones_like(v))[0]]
    pad x1 -> x5, local copies, waits for them, and re-layouts: 0.04 us -> 7.93 us  [the longest x1 4.16 us: local(): jnp.pad(passage_states, ((0, 0), (0, pad_len - pass_len), (0, 0)))]
    concatenate x3 -> x0, local copies, waits for them, and re-layouts: 5.35 us -> none  [local(): jnp.concatenate([up_p + up_q, down_p + down_q, grad_proj], axis=1)]
    convert_element_type x1 -> x2, other arithmetic: 0.09 us -> 2.91 us  [the longest x1 1.62 us: local(): mixed_p = (own_p.astype(F32) + ffn_p.astype(F32)).astype(BF16)]
    reduce_scatter x1, waiting for transfers between devices: 2.55 us -> 0.01 us  [local(): ffn_p = lax.psum_scatter(part_p, 'mp', scatter_dimension=0, tiled=True)]
    unnamed x33 -> x26, local copies, waits for them, and re-layouts: 5.29 us -> 5.09 us
  transfers between devices with their start and end apart: 1 -> 1, of which waited for: 1 -> 0; matrix products, arithmetic and copies ran while one was open for 3% -> 10% of each run, Pallas kernels for 16% -> 21%
where the time goes in v3:
time: 224 us; the launch traced here: 222 us
  Pallas kernels  130 us (58%)
  matrix products  40.5 us (18%)
  local copies, waits for them, and re-layouts  21.8 us (10%)
  other arithmetic  15.4 us (7%)
  between operations  14.3 us (6%)
    pallas_call x3, Pallas kernels, call(): pl.pallas_call(kernel, out_shape=outs, in_specs=[VMEM] * len(args), out_s...  130 us
    dot_general x8, matrix products, dot(): return lax.dot_general(a, b, (dims, ((), ())), preferred_element_type=F32)  40.5 us
    add_any x2, other arithmetic, gelu_slope(): return jax.vjp(jax.nn.gelu, v)[1](jnp.ones_like(v))[0]  8.2 us
    unnamed x26, local copies, waits for them, and re-layouts  5.09 us
  transfers between devices with their start and end apart: 1, of which 0 were waited for; matrix products, arithmetic and copies ran while one was open for 10% of the time, Pallas kernels for 21%

profile of v3, /device:TPU:1, one launch (start us, length us, event | category | flops | bytes accessed | tf_op | source)
XLA Modules:
  0.0 222.1 jit_solution(8467449237533316957)
XLA Ops:
  7.2 1.2 copy-done
  8.4 1.3 fusion.38
  9.7 9.5 %fusion.16 = (bf16[12,192,768]{2,1,0:T(8,128)(2,1)S(1)}, f32[12,192,768]{2,1,0:T(8,128)}) fusion(bf16[768,768]{1,0:T(8,128)(2,1)S(1)} %copy-done, bf16[12,180,768]{2,1,0:T(8,128)(2,1)} %param.9), kind=kOutput, calls=%fused_computation.23 | convolution fusion | flops 2733834240 | bytes 15114240 | tf_op jit(solution)/shard_map/dot_general | solution.py:20
  19.2 1.3 convolution_convert_fusion.1.part
  20.5 0.5 copy-done.4
  21.1 4.3 %convolution_convert_fusion = bf16[12,192,768]{2,1,0:T(8,128)(2,1)} fusion(bf16[12,192,768]{2,1,0:T(8,128)(2,1)S(1)} %get-tuple-element.40, bf16[768,768]{1,0:T(8,128)(2,1)S(1)} %copy-done.3), kind=kOutput, calls=%fused_computation.24 | convolution fusion | flops 2719678464 | bytes 8257536 | tf_op jit(solution)/shard_map/dot_general | solution.py:20
  25.4 0.7 pad.25.hid_q
  26.1 0.7 pad.24.rows_q
  26.8 4.2 %pad.22 = bf16[12,192,768]{2,1,0:T(8,128)(2,1)} pad(bf16[12,180,768]{2,1,0:T(8,128)(2,1)} %param.9, bf16[]{:T(256)} %constant.122.clone.1), padding=0_0x0_12x0_0 | pad | bytes 6856706 | tf_op jit(solution)/shard_map/jit(_pad)/pad | solution.py:500
  31.1 0.7 gather_fusion
  32.8 0.6 copy-done.9
  33.4 46.9 %shard_map.120 = (bf16[2,4,8,96,128]{4,3,2,1,0:T(8,128)(2,1)}, f32[2,4,8,8,128]{4,3,2,1,0:T(8,128)}, bf16[96,768]{1,0:T(8,128)(2,1)}, f32[96,128]{1,0:T(8,128)}, f32[96,1]{1,0:T(8,128)}) custom-call(bf16[96,768]{1,0:T(8,128)(2,1)} %convolution_convert_fusion.1.part, bf16[96,768]{1,0:T(8,128)(2,1)} %bitcast.62, bf16[768,128]{1,0:T(8,128)(2,1)} %proj.3, ...), custom_call_target="tpu_custom_call" | custom-call | flops 1000000000 | bytes 60000000 | tf_op jit(solution)/shard_map/pallas_call | solution.py:95
  80.3 1.0 slice.39
  82.0 0.8 pad.26.dgelu_q
  82.7 1.6 pad.27.mixed_q
  84.8 0.7 reshape.282.projp
  85.5 0.8 dynamic_slice.9
  86.5 1.3 fusion.17.perm
  87.8 8.0 %fusion.8 = f32[12,192,768]{2,1,0:T(8,128)} fusion(f32[12,192,768]{2,1,0:T(8,128)} %get-tuple-element.22), kind=kLoop, calls=%fused_computation.15 | loop fusion | flops 30081024 | bytes 14155776 | tf_op jit(solution)/shard_map/transpose(jvp())/add_any | solution.py:470
  95.9 1.6 add_convert_fusion
  98.0 6.9 %fusion.1 = (f32[3,6144]{1,0:T(4,128)S(1)}, f32[3,192,6144]{2,1,0:T(8,128)}) fusion(pred[3,192]{1,0:T(4,128)(4,1)S(1)} %iota_compare_fusion.1, bf16[6144,128,1]{1,0,2:T(8,128)(2,1)S(1)} %bitcast.74, f32[3,192,128]{2,1,0:T(8,128)S(1)} %get-tuple-element.45, f32[3,192]{1,0:T(4,128)S(1)} %add_rsqrt_fusion), kind=kOutput, calls=%fused_computation.4 | convolution fusion | flops 916715520 | bytes 16100160 | tf_op jit(solution)/shard_map/dot_general | solution.py:20
  105.4 0.6 pad_bitcast_fusion.vec
  106.0 15.2 %shard_map.121 = f32[8,128]{1,0:T(8,128)} custom-call(f32[8,128]{1,0:T(8,128)} %pad_bitcast_fusion.vec), custom_call_target="tpu_custom_call" | custom-call | flops 1000000000 | bytes 60000000 | tf_op jit(solution)/shard_map/pallas_call | solution.py:95
  121.2 0.7 slice.31
  122.4 7.0 %fusion.46 = f32[3,192,128]{2,1,0:T(8,128)S(1)} fusion(bf16[6144,128,1]{1,0,2:T(8,128)(2,1)} %bitcast.73, f32[3,192,6144]{2,1,0:T(8,128)} %get-tuple-element.47, f32[3,6144]{1,0:T(4,128)S(1)} %div.103, pred[3,192]{1,0:T(4,128)(4,1)S(1)} %iota_compare_fusion.1), kind=kOutput, calls=%fused_computation.65 | convolution fusion | flops 920125440 | bytes 16097856 | tf_op jit(solution)/shard_map/dot_general | solution.py:20
  129.4 9.7 %fusion.2 = bf16[6144,128]{1,0:T(8,128)(2,1)} fusion(f32[3,192,6144]{2,1,0:T(8,128)} %get-tuple-element.47, f32[3,6144]{1,0:T(4,128)S(1)} %div.103, pred[3,192]{1,0:T(4,128)(4,1)S(1)} %iota_compare_fusion.1, f32[3,192,128]{2,1,0:T(8,128)S(1)} %get-tuple-element.45, f32[3,192]{1,0:T(4,128)S(1)} %add_rsqrt_fusion), kind=kOutput, calls=%fused_computation.9 | convolution fusion | flops 921059328 | bytes 16100160 | tf_op jit(solution)/shard_map/dot_general | solution.py:20
  139.1 3.5 %fusion.24 = bf16[3,192,128]{2,1,0:T(8,128)(2,1)} fusion(f32[3,192,128]{2,1,0:T(8,128)S(1)} %fusion.46, f32[3,192,128]{2,1,0:T(8,128)S(1)} %get-tuple-element.45, f32[3,192]{1,0:T(4,128)S(1)} %add_rsqrt_fusion), kind=kOutput, calls=%fused_computation.34 | output fusion | flops 516799 | bytes 739584 | tf_op jit(solution)/shard_map/mul | solution.py:466
  142.6 67.9 %shard_map.122 = (f32[16,768]{1,0:T(8,128)}, f32[16,768]{1,0:T(8,128)}, f32[16,128]{1,0:T(8,128)}) custom-call(bf16[2,4,8,96,128]{4,3,2,1,0:T(8,128)(2,1)} %bitcast.59, bf16[576,128]{1,0:T(8,128)(2,1)} %bitcast.64, bf16[4,576,768]{2,1,0:T(8,128)(2,1)} %bitcast.56, bf16[4,576,768]{2,1,0:T(8,128)(2,1)} %bitcast.58, f32[4,576,768]{2,1,0:T(8,128)} %bitcast.55, ...), custom_call_target="tpu_custom_call" | custom-call | flops 1000000000 | bytes 60000000 | tf_op jit(solution)/shard_map/pallas_call | solution.py:95
  210.5 1.4 slice_bitcast_fusion
  211.9 0.6 dynamic_slice.11
  212.5 1.4 copy.22
  214.0 1.3 copy.23
  (66 shorter events, 3.9 us)
Async XLA Ops:
  7.2 1.3 copy-start
  7.2 88.7 %reduce-scatter.2.cloned.1.call-start = ((), (), s32[]{:S(2)}) async-start(), calls=%async_computation.1 | async-start | bytes 4423680 | tf_op jit(solution)/shard_map/reduce_scatter | solution.py:515
  9.7 9.5 %copy-start.3 = (bf16[768,768]{1,0:T(8,128)(2,1)S(1)}, bf16[768,768]{1,0:T(8,128)(2,1)}, u32[]{:S(2)}) copy-start(bf16[768,768]{1,0:T(8,128)(2,1)} %down.1) | copy-start | bytes 3538948
  19.2 1.8 copy-start.4
  21.1 5.1 %copy-start.7 = (bf16[3,32,768]{2,1,0:T(8,128)(2,1)S(1)}, bf16[3,32,768]{2,1,0:T(8,128)(2,1)}, u32[]{:S(2)}) copy-start(bf16[3,32,768]{2,1,0:T(8,128)(2,1)} %param.10) | copy-start | bytes 442372
  25.4 5.6 %copy-start.8 = (s32[3,16]{1,0:T(4,128)S(1)}, s32[3,16]{1,0:T(4,128)}, u32[]{:S(2)}) copy-start(s32[3,16]{1,0:T(4,128)} %param.13) | copy-start | bytes 580
  25.4 5.7 %copy-start.1 = (s32[768]{0:T(1024)S(1)}, s32[768]{0:T(1024)}, u32[]{:S(2)}) copy-start(s32[768]{0:T(1024)} %param.12) | copy-start | bytes 9220
  25.4 6.5 %copy-start.5 = (bf16[768,128]{1,0:T(8,128)(2,1)S(1)}, bf16[768,128]{1,0:T(8,128)(2,1)}, u32[]{:S(2)}) copy-start(bf16[768,128]{1,0:T(8,128)(2,1)} %proj.3) | copy-start | bytes 589828
  25.4 6.9 %copy-start.10 = (f32[3,16]{1,0:T(4,128)S(1)}, f32[3,16]{1,0:T(4,128)}, u32[]{:S(2)}) copy-start(f32[3,16]{1,0:T(4,128)} %param.14) | copy-start | bytes 580
  32.8 0.6 copy-start.9
  87.8 9.7 %copy-start.6 = (bf16[768,128]{1,0:T(8,128)(2,1)S(1)}, bf16[768,128]{1,0:T(8,128)(2,1)}, u32[]{:S(2)}) copy-start(bf16[768,128]{1,0:T(8,128)(2,1)} %proj.3) | copy-start | bytes 589828
  87.8 10.2 %copy-start.11 = (bf16[2,4,8,96,128]{4,3,2,1,0:T(8,128)(2,1)S(1)}, bf16[2,4,8,96,128]{4,3,2,1,0:T(8,128)(2,1)}, u32[]{:S(2)}) copy-start(bf16[2,4,8,96,128]{4,3,2,1,0:T(8,128)(2,1)} %get-tuple-element.21) | copy-start | bytes 4718596
  97.5 7.4 %copy-start.2 = (bf16[3,192,768]{2,1,0:T(8,128)(2,1)}, bf16[3,192,768]{2,1,0:T(8,128)(2,1)S(1)}, u32[]{:S(2)}) copy-start(bf16[3,192,768]{2,1,0:T(8,128)(2,1)S(1)} %add_convert_fusion) | copy-start | bytes 2654212
Sparse Core Ops, SparseCore 0:
  25.5 54.3 reduce-scatter.1

commit v4 on v3

--- a/solution.py
+++ b/solution.py
@@ -1,6 +1,7 @@
 import functools
 
 import jax
+import numpy as np
 import jax.numpy as jnp
 from jax import lax
 from jax.experimental import pallas as pl
@@ -91,22 +92,49 @@
     return [pltpu.SemaphoreType.DMA((max(n, 1),)), pltpu.SemaphoreType.DMA((max(n, 1),))]
 
 
-def call(kernel, outs, scratch, number, *args):
+def call(kernel, outs, scratch, number, *args, outer=((), ())):
+    def spec(i, which):
+        return pl.BlockSpec(memory_space=pl.ANY) if i in which else VMEM
+
     return pl.pallas_call(
         kernel,
         out_shape=outs,
-        in_specs=[VMEM] * len(args),
-        out_specs=[VMEM] * len(outs),
+        in_specs=[spec(i, outer[0]) for i in range(len(args))],
+        out_specs=[spec(i, outer[1]) for i in range(len(outs))],
         scratch_shapes=scratch,
         compiler_params=pltpu.CompilerParams(
-            collective_id=number, has_side_effects=True, vmem_limit_bytes=56 * 2**20
+            collective_id=number, has_side_effects=True, vmem_limit_bytes=52 * 2**20
         ),
         cost_estimate=pl.CostEstimate(flops=10**9, bytes_accessed=60 * 10**6, transcendentals=0),
     )(*args)
 
 
-def gather_kernel(
-    part, rows, proj, table, q_all, t_all, mixed, unit, inverse, pbuf, tbuf, *sem
+TILE = 256
+ROOT = (2.0 / np.pi) ** 0.5
+
+
+def cut(j):
+    return pl.ds(pl.multiple_of(j * TILE, TILE), TILE)
+
+
+def nt(a, b):
+    return dot(a, b, ((1,), (1,)))
+
+
+def tiled(tiles, body):
+    def step(j, carry):
+        body(j)
+        return carry
+
+    lax.fori_loop(0, tiles, step, 0)
+
+
+def encode_kernel(
+    states, rows_q, up, down, proj, table, perm,
+    rowst_out, hid_out, slope_out, mixedt, unit, inverse, q_all, t_all,
+    rowstq, hid_q, slope_q, mixedtq, unit_q, inv_q, projp,
+    rows, hid, slope, rowst, part, relay, onward, arrived, mixed, padq, partq, pbuf, tbuf,
+    ring_send, ring_recv, save, *sem
 ):
     y, z, c, x = place()
     greet("xzyc")
@@ -114,57 +142,204 @@
     sz, tz = Stage("z", sem[4], sem[5]), Stage("z", sem[6], sem[7])
     sy, ty = Stage("y", sem[8], sem[9]), Stage("y", sem[10], sem[11])
     sc, tc = Stage("c", sem[12], sem[13]), Stage("c", sem[14], sem[15])
+    width = up.shape[0]
+    tiles = width // TILE
+    nq = rows_q.shape[0]
+    own, length = states.shape[0] // NX, states.shape[1]
+    many = rows.shape[1]
+    each, half = many // own, many // 2
+    right, left = at(y, z, c, lax.rem(x + 1, NX)), at(y, z, c, lax.rem(x + NX - 1, NX))
+    ring, saves = [], []
+
+    def ring_copy(i, src, dst, who):
+        return pltpu.make_async_remote_copy(
+            src_ref=src, dst_ref=dst, send_sem=ring_send.at[i], recv_sem=ring_recv.at[i],
+            device_id=who, device_id_type=MESH,
+        )
+
+    def send(i, src, dst, who):
+        copy = ring_copy(i, src, dst, who)
+        copy.start()
+        ring.append(copy)
+
+    def keep(src, dst):
+        copy = pltpu.make_async_copy(src, dst, save.at[len(saves)])
+        copy.start()
+        saves.append(copy)
+
+    def feed(r, h, d, out):
+        def first(j):
+            v = jnp.dot(r[...], up[:, cut(j)], preferred_element_type=F32)
+            v2 = v * v
+            t = jnp.tanh(ROOT * v * (1.0 + 0.044715 * v2))
+            h[:, cut(j)] = (0.5 * v * (1.0 + t)).astype(BF16)
+            d[:, cut(j)] = 0.5 * (1.0 + t) + (0.5 * ROOT) * v * (1.0 - t * t) * (
+                1.0 + (3 * 0.044715) * v2
+            )
+
+        tiled(tiles, first)
+
+        def second(j):
+            out[:, cut(j)] = jnp.dot(
+                h[...], down[:, cut(j)], preferred_element_type=F32
+            ).astype(BF16)
+
+        tiled(tiles, second)
+
+    def group(k):
+        g = lax.rem(x + k, NX)
+        for i in range(own):
+            rows[g, each * (i + 1) - 16 : each * (i + 1), :] = jnp.zeros((16, width), BF16)
+            rows[g, each * i : each * i + length, :] = states[g * own + i]
+        feed(rows.at[g], hid.at[g], slope.at[g], part.at[k])
+        keep(hid.at[g], hid_out.at[g])
+        keep(slope.at[g], slope_out.at[g])
+
+    lower, upper = pl.ds(0, half), pl.ds(half, half)
     tx.start(lambda to: table, lambda k: tbuf.at[x])
-    sx.start(lambda to: part, lambda k: pbuf.at[x])
     tbuf[x] = table[...]
-    pbuf[x] = part[...]
+    padq[...] = jnp.zeros(padq.shape, BF16)
+    padq[0:nq, :] = rows_q[...]
+    feed(padq, hid_q, slope_q, partq)
+    short = partq.at[pl.ds(0, nq)]
+    sx.start(lambda to: short, lambda k: pbuf.at[x])
+    pbuf[x] = partq[0:nq, :]
+    group(2)
+    send(0, part.at[2, lower], relay.at[0], right)
+    send(1, part.at[2, upper], relay.at[1], left)
     tx.arrive(lambda k, frm: tbuf.at[frm])
     merged = tbuf[0]
     for i in range(1, NX):
         merged = merged + tbuf[i]
     t_all[c, y, z] = merged
     tz.start(lambda to: t_all.at[c, y, z], lambda k: t_all.at[c, y, z])
+    group(1)
+    send(2, part.at[1, upper], arrived.at[0, upper], right)
     sx.arrive(lambda k, frm: pbuf.at[frm])
     ffn = pbuf[0].astype(F32)
     for i in range(1, NX):
         ffn = ffn + pbuf[i].astype(F32)
-    blend = (rows[...].astype(F32) + ffn).astype(BF16)
-    mixed[...] = blend
+    blend = (rows_q[...].astype(F32) + ffn).astype(BF16)
     projected = jnp.dot(blend, proj[...], preferred_element_type=F32)
     inv = lax.rsqrt(jnp.sum(projected * projected, axis=-1, keepdims=True) + EPS)
-    inverse[...] = inv
-    unit[...] = projected * inv
+    inv_q[...] = inv
+    unit_q[...] = projected * inv
     q_all[c, y, z] = (projected * inv).astype(BF16)
     sz.start(lambda to: q_all.at[c, y, z], lambda k: q_all.at[c, y, z])
+    group(3)
+    send(3, part.at[3, lower], arrived.at[1, lower], left)
+    for i, k, rows_of, side, who in ((0, 1, lower, 0, right), (1, 3, upper, 1, left)):
+        ring_copy(i, relay.at[i], relay.at[i], who).wait_recv()
+        onward[i] = (part[k, rows_of, :].astype(F32) + relay[i].astype(F32)).astype(BF16)
+        send(4 + i, onward.at[i], arrived.at[side, rows_of], who)
     tz.arrive(lambda k, frm: t_all.at[c, y, frm])
     ty.start(lambda to: t_all.at[c, y], lambda k: t_all.at[c, y])
+    group(0)
     sz.arrive(lambda k, frm: q_all.at[c, y, frm])
     sy.start(lambda to: q_all.at[c, y], lambda k: q_all.at[c, y])
     ty.arrive(lambda k, frm: t_all.at[c, frm])
     tc.start(lambda to: t_all.at[c], lambda k: t_all.at[c])
+    for k in range(NX):
+        g = lax.rem(x + k, NX)
+
+        def turn(j):
+            rowst[g, cut(j), :] = nt(perm[cut(j), :], rows[g]).astype(BF16)
+
+        tiled(tiles, turn)
+        keep(rowst.at[g], rowst_out.at[g])
+
+    def turn_q(j):
+        rowstq[cut(j), :] = nt(perm[cut(j), :], padq[...]).astype(BF16)
+        projp[cut(j), :] = jnp.dot(
+            perm[cut(j), :], proj[...], preferred_element_type=F32
+        ).astype(BF16)
+
+    tiled(tiles, turn_q)
+    padq[0:nq, :] = blend
+
+    def turn_mixed_q(j):
+        mixedtq[cut(j), :] = nt(perm[cut(j), :], padq[...]).astype(BF16)
+
+    tiled(tiles, turn_mixed_q)
     sy.arrive(lambda k, frm: q_all.at[c, frm])
     sc.start(lambda to: q_all.at[c], lambda k: q_all.at[c])
     tc.arrive(lambda k, frm: t_all.at[frm])
+    for i, side, rows_of, who in (
+        (2, 0, upper, right), (3, 1, lower, left), (4, 0, lower, right), (5, 1, upper, left)
+    ):
+        ref = arrived.at[side, rows_of]
+        ring_copy(i, ref, ref, who).wait_recv()
+    step_rows = each
+
+    def finish_rows(i):
+        at_rows = pl.ds(pl.multiple_of(i * step_rows, 16), step_rows)
+        ffn = part[0, at_rows, :].astype(F32)
+        ffn = ffn + arrived[0, at_rows, :].astype(F32) + arrived[1, at_rows, :].astype(F32)
+        blend = (rows[x, at_rows, :].astype(F32) + ffn).astype(BF16)
+        mixed[at_rows, :] = blend
+        projected = jnp.dot(blend, proj[...], preferred_element_type=F32)
+        inv = lax.rsqrt(jnp.sum(projected * projected, axis=-1, keepdims=True) + EPS)
+        inverse[at_rows, :] = inv
+        unit[at_rows, :] = projected * inv
+
+    tiled(own, finish_rows)
+
+    def turn_mixed(j):
+        mixedt[cut(j), :] = nt(perm[cut(j), :], mixed[...]).astype(BF16)
+
+    tiled(tiles, turn_mixed)
     sc.arrive(lambda k, frm: q_all.at[frm])
     for stage in (sx, tx, sz, tz, sy, ty, sc, tc):
         stage.finish()
-
-
-def gather_queries(part, rows, proj, table):
-    n, width = part.shape
-    emb = proj.shape[1]
-    shape = jax.ShapeDtypeStruct
+    for copy in ring:
+        copy.wait_send()
+    for copy in saves:
+        copy.wait()
+
+
+def encode(states, rows_q, up, down, proj, table, perm):
+    nq, width = rows_q.shape
+    hidden, emb = up.shape[1], proj.shape[1]
+    own = states.shape[0] // NX
+    many = own * ((states.shape[1] + 15) // 16 * 16)
+    few = (nq + 127) // 128 * 128
+    shape, V = jax.ShapeDtypeStruct, pltpu.VMEM
     outs = [
-        shape((NC, NY, NZ, n, emb), BF16),
+        shape((NX, width, many), BF16),
+        shape((NX, many, hidden), BF16),
+        shape((NX, many, hidden), F32),
+        shape((width, many), BF16),
+        shape((many, emb), F32),
+        shape((many, 1), F32),
+        shape((NC, NY, NZ, nq, emb), BF16),
         shape((NC, NY, NZ) + table.shape, F32),
-        shape((n, width), BF16),
-        shape((n, emb), F32),
-        shape((n, 1), F32),
+        shape((width, few), BF16),
+        shape((few, hidden), BF16),
+        shape((few, hidden), F32),
+        shape((width, few), BF16),
+        shape((nq, emb), F32),
+        shape((nq, 1), F32),
+        shape((width, emb), BF16),
     ]
-    scratch = [pltpu.VMEM((NX, n, width), BF16), pltpu.VMEM((NX,) + table.shape, F32)]
+    scratch = [
+        V((NX, many, width), BF16),
+        V((NX, many, hidden), BF16),
+        V((NX, many, hidden), F32),
+        V((NX, width, many), BF16),
+        V((NX, many, width), BF16),
+        V((2, many // 2, width), BF16),
+        V((2, many // 2, width), BF16),
+        V((2, many, width), BF16),
+        V((many, width), BF16),
+        V((few, width), BF16),
+        V((few, width), BF16),
+        V((NX, nq, width), BF16),
+        V((NX,) + table.shape, F32),
+    ] + sems(6) + [pltpu.SemaphoreType.DMA((3 * NX,))]
     for size in (NX, NX, NZ, NZ, NY, NY, NC, NC):
         scratch += sems(size - 1)
-    return call(gather_kernel, outs, scratch, 1, part, rows, proj, table)
+    args = (states, rows_q, up, down, proj, table, perm)
+    return call(encode_kernel, outs, scratch, 1, *args, outer=([], [0, 1, 2]))
 
 
 def total_kernel(vec, out, abuf, bbuf, *sem):
@@ -236,20 +411,13 @@
     lax.fori_loop(0, index, body, 0)
 
 
-def nt(a, b):
-    return dot(a, b, ((1,), (1,)))
-
-
-TILE = 256
-
-
 def back_kernel(
-    cot, uc, rows, hid, dgelu, mixed, rows_q, hid_q, dgelu_q, mixed_q, unit_q, inv_q, down, proj,
-    projp, perm,
+    cot, uc, rowst_in, hid_in, slope_in, mixedt, rowstq, hid_q, dgelu_q, mixedtq, unit_q, inv_q,
+    down, proj, projp,
     out_up, out_down, out_proj,
-    uc_all, cbuf, abuf, ybuf, bbuf, zbuf, xbuf, mc, mct, rowst, mixedt, mcq, mctq, rowstq, ucq,
+    uc_all, cbuf, abuf, ybuf, bbuf, zbuf, xbuf, mc, mct, mcq, mctq, ucq, rowst, hid, dgelu,
     acc_up, acc_down, acc_proj,
-    gd, gu, gp, cd, cu, cp, ad, au, ap, yd, yu, yp, fd, fu, fp, bd, bu, bp, zd, zu, zp, xp, *sem
+    gd, gu, gp, cd, cu, cp, ad, au, ap, yd, yu, yp, fd, fu, fp, bd, bu, bp, zd, zu, zp, xp, load, *sem
 ):
     y, z, c, x = place()
     sem = list(sem)
@@ -266,27 +434,35 @@
     width = down.shape[1]
     tiles = width // TILE
 
-    def cut(j):
-        return pl.ds(pl.multiple_of(j * TILE, TILE), TILE)
-
-    def prepare(u, r, m, mt, rt):
+    loads = {}
+    for i, k in enumerate((0, 3, 1, 2)):
+        g = lax.rem(x + k, NX)
+        loads[k] = [
+            pltpu.make_async_copy(src.at[g], dst.at[g], load.at[3 * i + n])
+            for n, (src, dst) in enumerate(((hid_in, hid), (slope_in, dgelu), (rowst_in, rowst)))
+        ]
+        for copy in loads[k]:
+            copy.start()
+
+    def prepare(u, m, mt):
         def body(j, carry):
             m[:, cut(j)] = nt(u[...], proj[cut(j), :]).astype(BF16)
             mt[cut(j), :] = nt(projp[cut(j), :], u[...]).astype(BF16)
-            rt[cut(j), :] = nt(perm[cut(j), :], r[...]).astype(BF16)
             return carry
 
         lax.fori_loop(0, tiles, body, 0)
 
-    def passages(g, first):
-        u, r = uc_all.at[g], rows.at[g]
-        prepare(u, r, mc, mct, rowst)
+    def passages(k, first):
+        g = lax.rem(x + k, NX)
+        prepare(uc_all.at[g], mc, mct)
+        for copy in loads[k]:
+            copy.wait()
 
         def body(j, carry):
             term = jnp.dot(mct[...], hid[g, :, cut(j)], preferred_element_type=F32)
             back = nt(mc[...], down[cut(j), :])
             pre = (back * dgelu[g, :, cut(j)]).astype(BF16)
-            up = jnp.dot(rowst[...], pre, preferred_element_type=F32)
+            up = jnp.dot(rowst[g], pre, preferred_element_type=F32)
             if first:
                 acc_down[:, cut(j)] = term
                 acc_up[:, cut(j)] = up
@@ -297,13 +473,7 @@
 
         lax.fori_loop(0, tiles, body, 0)
 
-    passages(x, True)
-
-    def mix(j, carry):
-        mixedt[cut(j), :] = nt(perm[cut(j), :], mixed[...]).astype(BF16)
-        return carry
-
-    lax.fori_loop(0, tiles, mix, 0)
+    passages(0, True)
     acc_proj[...] = jnp.dot(mixedt[...], uc[...], preferred_element_type=F32)
 
     sc.arrive(lambda k, frm: cbuf)
@@ -311,18 +481,18 @@
         add_into(abuf.at[i], NZ, lambda j: cot[c, i, j], [cbuf.at[i]])
     sy.start(lambda to: abuf.at[to], lambda k: ybuf.at[k - 1])
     su.arrive(lambda k, frm: uc_all.at[frm])
-    passages(lax.rem(x + 3, NX), False)
+    passages(3, False)
     sy.arrive(lambda k, frm: ybuf.at[k - 1])
     add_into(bbuf, NZ, lambda j: abuf[y, j], [ybuf.at[i] for i in range(NY - 1)])
     sz.start(lambda to: bbuf.at[to], lambda k: zbuf.at[k - 1])
-    passages(lax.rem(x + 1, NX), False)
+    passages(1, False)
     sz.arrive(lambda k, frm: zbuf.at[k - 1])
     value = bbuf[z].astype(F32)
     for i in range(NZ - 1):
         value = value + zbuf[i].astype(F32)
     xbuf[x] = value.astype(BF16)
     sx.start(lambda to: xbuf.at[x], lambda k: xbuf.at[x])
-    passages(lax.rem(x + 2, NX), False)
+    passages(2, False)
     sx.arrive(lambda k, frm: xbuf.at[frm])
     g = xbuf[0].astype(F32)
     for i in range(1, NX):
@@ -331,7 +501,7 @@
     n = g.shape[0]
     ucq[...] = jnp.zeros(ucq.shape, BF16)
     ucq[0:n, :] = (inv_q[...] * (g - unit_q[...] * along)).astype(BF16)
-    prepare(ucq, rows_q, mcq, mctq, rowstq)
+    prepare(ucq, mcq, mctq)
     blocks = gd.shape[:3]
 
     def down_last(j, carry):
@@ -355,16 +525,11 @@
 
     leave(chunks[0])
 
-    def mixq(j, carry):
-        mctq[cut(j), :] = nt(perm[cut(j), :], mixed_q[...]).astype(BF16)
-        return carry
-
-    lax.fori_loop(0, tiles, mixq, 0)
     part = n // NX
     at_row = lax.broadcasted_iota(jnp.int32, ucq.shape, 0)
     mine = jnp.logical_and(at_row >= x * part, at_row < (x + 1) * part)
     own = jnp.where(mine, ucq[...].astype(F32), 0.0).astype(BF16)
-    term = acc_proj[...] + jnp.dot(mctq[...], own, preferred_element_type=F32)
+    term = acc_proj[...] + jnp.dot(mixedtq[...], own, preferred_element_type=F32)
     gp[...] = term.astype(BF16).reshape(gp.shape)
     leave(chunks[1])
 
@@ -419,11 +584,11 @@
 
 
 def backward(*args):
-    cot, uc, rows, hid, _, _, rows_q = args[:7]
+    cot, uc, rowst, hid, _, _, rowstq = args[:7]
     n, emb = cot.shape[-2:]
-    many, width = rows.shape[1:]
+    width, many = rowst.shape[1:]
     hidden = hid.shape[2]
-    few = rows_q.shape[0]
+    few = rowstq.shape[1]
     tall = width // (NC * NY)
     V = pltpu.VMEM
     outs = [jax.ShapeDtypeStruct((16, w), F32) for w in (hidden, hidden, emb)]
@@ -437,12 +602,12 @@
         V((NX, n, emb), BF16),
         V((many, width), BF16),
         V((width, many), BF16),
-        V((width, many), BF16),
-        V((width, many), BF16),
         V((few, width), BF16),
         V((width, few), BF16),
-        V((width, few), BF16),
         V((few, emb), BF16),
+        V((NX, width, many), BF16),
+        V((NX, many, hidden), BF16),
+        V((NX, many, hidden), F32),
         V((width, hidden), F32),
         V((width, hidden), F32),
         V((width, emb), F32),
@@ -455,19 +620,15 @@
     scratch += [V((tall + 8, w), F32) for w in wide]
     scratch += [V((NZ, 16, w), BF16) for w in wide]
     scratch += [V((NZ - 1, 16, w), BF16) for w in wide]
-    scratch += [V((NX, 16, emb), F32)]
+    scratch += [V((NX, 16, emb), F32), pltpu.SemaphoreType.DMA((3 * NX,))]
     for a in "cxyzx" + "cyz" * 3 + "x":
         scratch += sems({"x": NX, "y": NY, "z": NZ, "c": NC}[a] - 1)
-    return call(back_kernel, outs, scratch, 3, *args)
+    return call(back_kernel, outs, scratch, 3, *args, outer=([2, 3, 4], ()))
 
 
 def unit_cotangent(g, unit, inverse):
     along = jnp.sum(g * unit, axis=-1, keepdims=True)
     return (inverse * (g - unit * along)).astype(BF16)
-
-
-def gelu_slope(v):
-    return jax.vjp(jax.nn.gelu, v)[1](jnp.ones_like(v))[0]
 
 
 def local(
@@ -484,7 +645,6 @@
     p_dev, pass_len, width = passage_states.shape
     q_dev, q_len, _ = query_states.shape
     emb = proj_weight.shape[1]
-    hidden = up_weight.shape[1]
     n_dp = NY * NZ * NC
     me_dp, me_mp = lax.axis_index("dp"), lax.axis_index("mp")
     y, z, c, _ = place()
@@ -497,25 +657,21 @@
     all_cands = cands * NX
 
     pad_len = (pass_len + 15) // 16 * 16
-    passage_states = jnp.pad(passage_states, ((0, 0), (0, pad_len - pass_len), (0, 0)))
-    rows_q = query_states.reshape(q_rows, width)
-    pre_q = dot(rows_q, up_weight, ((1,), (0,)))
-    hid_q = jax.nn.gelu(pre_q).astype(BF16)
-    part_q = dot(hid_q, down_weight, ((1,), (0,))).astype(BF16)
-    pre_p = dot(passage_states, up_weight, ((2,), (0,)))
-    hid_p = jax.nn.gelu(pre_p).astype(BF16)
-    part_p = dot(hid_p, down_weight, ((2,), (0,))).astype(BF16)
 
     positions = jnp.take(owner_map, candidates).astype(F32)
     table = jnp.zeros((8, 2 * all_cands), F32)
     table = lax.dynamic_update_slice(table, positions, (0, me_mp * cands))
     table = lax.dynamic_update_slice(table, teacher_scores, (0, all_cands + me_mp * cands))
 
-    part_p, part_q = lax.optimization_barrier((part_p, part_q))
-    ffn_p = lax.psum_scatter(part_p, "mp", scatter_dimension=0, tiled=True)
-    q_all, t_all, mixed_q, unit_q, inv_q = gather_queries(part_q, rows_q, proj_weight, table)
-    q_all, pre_p, pre_q = lax.optimization_barrier((q_all, pre_p, pre_q))
-    dgelu_p, dgelu_q = gelu_slope(pre_p), gelu_slope(pre_q)
+    order = np.arange(width).reshape(NY, NZ, NC, rows).transpose(2, 0, 1, 3).reshape(-1)
+    perm = jnp.asarray(np.eye(width)[order], BF16)
+    (
+        rowst, hid_p, slope_p, mixedt, unit_p, inv_p, q_all, t_all,
+        rowstq, hid_q, slope_q, mixedtq, unit_q, inv_q, projp,
+    ) = encode(
+        passage_states, query_states.reshape(q_rows, width), up_weight, down_weight,
+        proj_weight, table, perm,
+    )
     q_all = q_all.reshape(n_dp * q_rows, emb)
     table = t_all.reshape(n_dp, 8, 2 * all_cands)[:, :q_dev].reshape(queries, -1)
     pos_all, teacher = table[:, :all_cands], table[:, all_cands:]
@@ -528,11 +684,8 @@
     count = jnp.sum(hit.astype(F32), axis=2)
     teacher_mass = jnp.sum(jnp.where(hit, teacher_exp[None], 0.0), axis=2)
 
-    own_p = lax.dynamic_slice_in_dim(passage_states, me_mp * p_own, p_own, 0)
-    mixed_p = (own_p.astype(F32) + ffn_p.astype(F32)).astype(BF16)
-    projected = dot(mixed_p, proj_weight, ((2,), (0,)))
-    inv_p = lax.rsqrt(jnp.sum(projected * projected, axis=-1, keepdims=True) + EPS)
-    unit_p = projected * inv_p
+    unit_p = unit_p.reshape(p_own, pad_len, emb)
+    inv_p = inv_p.reshape(p_own, pad_len, 1)
     emb_p = unit_p.astype(BF16)
 
     own_len = lax.dynamic_slice_in_dim(lengths, base, p_own, 0)
@@ -555,30 +708,11 @@
     cot_p = dot(weights, q_all, ((2,), (0,)))
     uc_p = unit_cotangent(cot_p, unit_p, inv_p)
 
-    few = (q_rows + 127) // 128 * 128
-    more = ((0, few - q_rows), (0, 0))
-    order = jnp.arange(width).reshape(NC, NY, NZ, rows)
-    order = (((order // (NZ * rows)) % NY * NZ + (order // rows) % NZ) * NC + order // (NY * NZ * rows)) * rows
-    order = (order + jnp.arange(rows)).reshape(width)
-    perm = (order[:, None] == jnp.arange(width)[None, :]).astype(BF16)
-    proj_order = jnp.transpose(proj_weight.reshape(NY, NZ, NC, rows, emb), (2, 0, 1, 3, 4))
     up, down, grad_proj = backward(
         cot_q.reshape(NC, NY, NZ, q_rows, emb),
         uc_p.reshape(p_own * pad_len, emb),
-        passage_states.reshape(NX, p_own * pad_len, width),
-        hid_p.reshape(NX, p_own * pad_len, hidden),
-        dgelu_p.reshape(NX, p_own * pad_len, hidden),
-        mixed_p.reshape(p_own * pad_len, width),
-        jnp.pad(rows_q, more),
-        jnp.pad(hid_q, more),
-        jnp.pad(dgelu_q, more),
-        jnp.pad(mixed_q, more),
-        unit_q,
-        inv_q,
-        down_weight,
-        proj_weight,
-        proj_order.reshape(width, emb),
-        perm,
+        rowst, hid_p, slope_p, mixedt, rowstq, hid_q, slope_q, mixedtq, unit_q, inv_q,
+        down_weight, proj_weight, projp,
     )
     return query_loss, up[:rows], down[:rows].T, grad_proj[:rows]
 

time: 224 us -> 170 us (0.76)
  matrix products: 40.5 us -> 25 us
  between operations: 14.3 us -> 0.92 us
  local copies, waits for them, and re-layouts: 21.8 us -> 8.88 us
  other arithmetic: 15.4 us -> 4.37 us
    dot_general x8 -> x3, matrix products: 40.5 us -> 25 us  [dot(): return lax.dot_general(a, b, (dims, ((), ())), preferred_element_type=F32)]
    add_any x2 -> x0, other arithmetic: 8.2 us -> none  [gelu_slope(): return jax.vjp(jax.nn.gelu, v)[1](jnp.ones_like(v))[0]]
    pad x5 -> x0, local copies, waits for them, and re-layouts: 7.93 us -> none  [the longest x1 4.16 us: local(): jnp.pad(passage_states, ((0, 0), (0, pad_len - pass_len), (0, 0)))]
    convert_element_type x2 -> x1, other arithmetic: 2.91 us -> 0.02 us  [local(): emb_p = unit_p.astype(BF16)]
    mul x1, other arithmetic: 3.5 us -> 1.01 us  [unit_cotangent(): return (inverse * (g - unit * along)).astype(BF16)]
    unnamed x26 -> x14, local copies, waits for them, and re-layouts: 5.09 us -> 3.07 us
  transfers between devices with their start and end apart: 1 -> 0, of which waited for: 0 -> 0; matrix products, arithmetic and copies ran while one was open for 10% -> 0% of each run, Pallas kernels for 21% -> 0%
where the time goes in v4:
time: 170 us; the launch traced here: 169 us
  Pallas kernels  130 us (76%)
  matrix products  25 us (15%)
  local copies, waits for them, and re-layouts  8.88 us (5%)
  other arithmetic  4.37 us (3%)
    pallas_call x3, Pallas kernels, call(): pl.pallas_call(kernel, out_shape=outs, in_specs=[spec(i, outer[0]) for i...  130 us
    dot_general x3, matrix products, dot(): return lax.dot_general(a, b, (dims, ((), ())), preferred_element_type=F32)  25 us

profile of v4, /device:TPU:1, one launch (start us, length us, event | category | flops | bytes accessed | tf_op | source)
XLA Modules:
  0.0 168.9 jit_solution(2255935461667960337)
XLA Ops:
  0.7 0.8 dynamic_slice.6
  1.6 0.7 compare_select_fusion.1
  2.2 0.1 reshape.141
  2.3 0.7 gather_fusion
  3.1 0.1 reshape.140
  3.1 0.7 select_convert_fusion
  3.8 0.3 dynamic_update_slice.6
  4.1 1.7 %dynamic_update_slice.7.table = f32[8,128]{1,0:T(8,128)S(1)} dynamic-update-slice(f32[8,128]{1,0:T(8,128)S(1)} %dynamic_update_slice.6, f32[3,16]{1,0:T(4,128)} %param.15, s32[]{:T(128)} %constant.73.clone.1, s32[]{:T(128)S(6)} %select_n.50) | dynamic-update-slice | bytes 388 | tf_op jit(solution)/shard_map/dynamic_update_slice | solution.py:664
  5.8 0.9 copy-done.1
  6.8 0.9 copy-done.4
  7.7 55.8 %shard_map.129 = (bf16[4,768,576]{2,1,0:T(8,128)(2,1)}, bf16[4,576,768]{2,1,0:T(8,128)(2,1)}, f32[4,576,768]{2,1,0:T(8,128)}, bf16[768,576]{1,0:T(8,128)(2,1)}, ...) custom-call(bf16[12,180,768]{2,1,0:T(8,128)(2,1)} %states.1, ...), custom_call_target="tpu_custom_call" | custom-call | flops 1000000000 | bytes 60000000 | tf_op jit(solution)/shard_map/pallas_call | solution.py:99
  63.5 1.2 reduce
  64.8 0.2 multiply_reduce_fusion.1
  65.1 0.1 copy.14
  65.2 0.1 copy.15
  65.3 0.1 fusion.8
  65.4 8.2 %fusion.1 = (f32[3,6144]{1,0:T(4,128)S(1)}, f32[3,192,6144]{2,1,0:T(8,128)}) fusion(pred[3,192]{1,0:T(4,128)(4,1)S(1)} %iota_compare_fusion, bf16[3,192,128]{2,1,0:T(8,128)(2,1)S(1)} %bitcast.34, bf16[6144,128,1]{1,0,2:T(8,128)(2,1)} %bitcast.40), kind=kOutput, calls=%fused_computation.4 | convolution fusion | flops 916568064 | bytes 15950400 | tf_op jit(solution)/shard_map/dot_general | solution.py:21
  73.7 0.1 log.14
  73.8 0.2 reduce_sum.84
  74.1 0.1 reshape.133
  74.1 15.2 %shard_map.130 = f32[8,128]{1,0:T(8,128)S(1)} custom-call(f32[8,128]{1,0:T(8,128)S(1)} %pad_bitcast_fusion.vec), custom_call_target="tpu_custom_call" | custom-call | flops 1000000000 | bytes 60000000 | tf_op jit(solution)/shard_map/pallas_call | solution.py:99
  89.3 0.1 reshape.135
  89.5 0.6 dynamic_slice.7
  90.0 0.1 div.75
  90.2 0.2 div.76
  90.4 6.6 %fusion.11 = f32[3,192,128]{2,1,0:T(8,128)S(1)} fusion(bf16[6144,128,1]{1,0,2:T(8,128)(2,1)S(1)} %bitcast.41, f32[3,192,6144]{2,1,0:T(8,128)} %get-tuple-element.51, f32[3,6144]{1,0:T(4,128)S(1)} %div.77, pred[3,192]{1,0:T(4,128)(4,1)S(1)} %iota_compare_fusion), kind=kOutput, calls=%fused_computation.18 | convolution fusion | flops 920125440 | bytes 16097856 | tf_op jit(solution)/shard_map/dot_general | solution.py:21
  97.0 10.2 %fusion.2 = bf16[6144,128]{1,0:T(8,128)(2,1)} fusion(f32[3,192,128]{2,1,0:T(8,128)S(1)} %bitcast.26, f32[3,192,6144]{2,1,0:T(8,128)} %get-tuple-element.51, f32[3,6144]{1,0:T(4,128)S(1)} %div.77, pred[3,192]{1,0:T(4,128)(4,1)S(1)} %iota_compare_fusion), kind=kOutput, calls=%fused_computation.6 | convolution fusion | flops 920985600 | bytes 16097856 | tf_op jit(solution)/shard_map/dot_general | solution.py:21
  107.2 1.0 fusion.6
  108.3 58.8 %shard_map.131 = (f32[16,768]{1,0:T(8,128)S(1)}, f32[16,768]{1,0:T(8,128)S(1)}, f32[16,128]{1,0:T(8,128)S(1)}) custom-call(bf16[2,4,8,96,128]{4,3,2,1,0:T(8,128)(2,1)} %bitcast.33, bf16[576,128]{1,0:T(8,128)(2,1)S(1)} %bitcast.28, bf16[4,768,576]{2,1,0:T(8,128)(2,1)} %get-tuple-element.26.rowst_in, bf16[4,576,768]{2,1,0:T(8,128)(2,1)} %get-tuple-element.27.hid_in, ...), custom_call_target="tpu_custom_call" | custom-call | flops 1000000000 | bytes 60000000 | tf_op jit(solution)/shard_map/pallas_call | solution.py:99
  167.1 0.6 slice_bitcast_fusion
  167.7 0.6 copy.20
  168.3 0.6 copy.21
  (27 shorter events, 0.4 us)
Async XLA Ops:
  0.6 1.7 %copy-start = (s32[768]{0:T(1024)S(1)}, s32[768]{0:T(1024)}, u32[]{:S(2)}) copy-start(s32[768]{0:T(1024)} %param.13) | copy-start | bytes 9220
  5.8 0.9 copy-start.1
  6.8 0.9 copy-start.4
  63.4 27.0 %copy-start.5 = (bf16[2,4,8,96,128]{4,3,2,1,0:T(8,128)(2,1)S(1)}, bf16[2,4,8,96,128]{4,3,2,1,0:T(8,128)(2,1)}, u32[]{:S(2)}) copy-start(bf16[2,4,8,96,128]{4,3,2,1,0:T(8,128)(2,1)} %get-tuple-element.24) | copy-start | bytes 4718596
  97.0 11.2 %copy-start.2 = (bf16[768,128]{1,0:T(8,128)(2,1)S(1)}, bf16[768,128]{1,0:T(8,128)(2,1)}, u32[]{:S(2)}) copy-start(bf16[768,128]{1,0:T(8,128)(2,1)} %proj.3) | copy-start | bytes 589828
  97.0 11.2 %copy-start.3 = (f32[128,768]{1,0:T(8,128)S(1)}, f32[128,768]{1,0:T(8,128)}, u32[]{:S(2)}) copy-start(f32[128,768]{1,0:T(8,128)} %get-tuple-element.32.dgelu_q) | copy-start | bytes 1179652

commit v5 on v4

--- a/solution.py
+++ b/solution.py
@@ -92,18 +92,20 @@
     return [pltpu.SemaphoreType.DMA((max(n, 1),)), pltpu.SemaphoreType.DMA((max(n, 1),))]
 
 
-def call(kernel, outs, scratch, number, *args, outer=((), ())):
-    def spec(i, which):
+def call(kernel, outs, scratch, number, *args, outer=((), ()), scalars=()):
+    def spec(i, which, small=()):
+        if i in small:
+            return pl.BlockSpec(memory_space=pltpu.SMEM)
         return pl.BlockSpec(memory_space=pl.ANY) if i in which else VMEM
 
     return pl.pallas_call(
         kernel,
         out_shape=outs,
-        in_specs=[spec(i, outer[0]) for i in range(len(args))],
+        in_specs=[spec(i, outer[0], scalars) for i in range(len(args))],
         out_specs=[spec(i, outer[1]) for i in range(len(outs))],
         scratch_shapes=scratch,
         compiler_params=pltpu.CompilerParams(
-            collective_id=number, has_side_effects=True, vmem_limit_bytes=52 * 2**20
+            collective_id=number, has_side_effects=True, vmem_limit_bytes=58 * 2**20
         ),
         cost_estimate=pl.CostEstimate(flops=10**9, bytes_accessed=60 * 10**6, transcendentals=0),
     )(*args)
@@ -130,10 +132,10 @@
 
 
 def encode_kernel(
-    states, rows_q, up, down, proj, table, perm,
+    states, rows_q, up, down, proj, perm, owner_map, candidates, teacher,
     rowst_out, hid_out, slope_out, mixedt, unit, inverse, q_all, t_all,
     rowstq, hid_q, slope_q, mixedtq, unit_q, inv_q, projp,
-    rows, hid, slope, rowst, part, relay, onward, arrived, mixed, padq, partq, pbuf, tbuf,
+    rows, hid, slope, rowst, part, relay, onward, arrived, mixed, padq, partq, pbuf, tbuf, table,
     ring_send, ring_recv, save, *sem
 ):
     y, z, c, x = place()
@@ -196,6 +198,17 @@
         keep(slope.at[g], slope_out.at[g])
 
     lower, upper = pl.ds(0, half), pl.ds(half, half)
+    row = lax.broadcasted_iota(jnp.int32, table.shape, 0)
+    lane = lax.broadcasted_iota(jnp.int32, table.shape, 1)
+    value = jnp.zeros(table.shape, F32)
+    few_c = candidates.shape[1]
+    for b in range(few_c):
+        at_b = jnp.logical_and(lane % (few_c * NX) == x * few_c + b, row < candidates.shape[0])
+        for a in range(candidates.shape[0]):
+            here = jnp.logical_and(at_b, row == a)
+            position = owner_map[candidates[a, b]].astype(F32)
+            value = jnp.where(here, jnp.where(lane < few_c * NX, position, teacher[a, b]), value)
+    table[...] = value
     tx.start(lambda to: table, lambda k: tbuf.at[x])
     tbuf[x] = table[...]
     padq[...] = jnp.zeros(padq.shape, BF16)
@@ -297,13 +310,14 @@
         copy.wait()
 
 
-def encode(states, rows_q, up, down, proj, table, perm):
+def encode(states, rows_q, up, down, proj, perm, owner_map, candidates, teacher):
     nq, width = rows_q.shape
     hidden, emb = up.shape[1], proj.shape[1]
     own = states.shape[0] // NX
     many = own * ((states.shape[1] + 15) // 16 * 16)
     few = (nq + 127) // 128 * 128
     shape, V = jax.ShapeDtypeStruct, pltpu.VMEM
+    table = (8, 2 * NX * candidates.shape[1])
     outs = [
         shape((NX, width, many), BF16),
         shape((NX, many, hidden), BF16),
@@ -312,7 +326,7 @@
         shape((many, emb), F32),
         shape((many, 1), F32),
         shape((NC, NY, NZ, nq, emb), BF16),
-        shape((NC, NY, NZ) + table.shape, F32),
+        shape((NC, NY, NZ) + table, F32),
         shape((width, few), BF16),
         shape((few, hidden), BF16),
         shape((few, hidden), F32),
@@ -334,70 +348,55 @@
         V((few, width), BF16),
         V((few, width), BF16),
         V((NX, nq, width), BF16),
-        V((NX,) + table.shape, F32),
+        V((NX,) + table, F32),
+        V(table, F32),
     ] + sems(6) + [pltpu.SemaphoreType.DMA((3 * NX,))]
     for size in (NX, NX, NZ, NZ, NY, NY, NC, NC):
         scratch += sems(size - 1)
-    args = (states, rows_q, up, down, proj, table, perm)
-    return call(encode_kernel, outs, scratch, 1, *args, outer=([], [0, 1, 2]))
-
-
-def total_kernel(vec, out, abuf, bbuf, *sem):
-    y, z, c, x = place()
-    barrier = pltpu.get_barrier_semaphore()
-    groups = [
+    args = (states, rows_q, up, down, proj, perm, owner_map, candidates, teacher)
+    return call(encode_kernel, outs, scratch, 1, *args, outer=([], [0, 1, 2]), scalars=[6, 7, 8])
+
+
+def circles(y, z, c, x):
+    return (
         (NY * NX, y * NX + x, lambda i: at(i // NX, z, c, i % NX)),
         (NZ * NC, z * NC + c, lambda i: at(y, i // NC, i % NC, x)),
-    ]
-    for size, mine, who in groups:
-        for k in range(1, size):
-            pl.semaphore_signal(
-                barrier, inc=1, device_id=who((mine + k) % size), device_id_type=MESH
-            )
-    pl.semaphore_wait(barrier, NY * NX + NZ * NC - 2)
-    held = vec
-    for (size, mine, who), buf, send, recv in zip(
-        groups, (abuf, bbuf), (sem[0], sem[2]), (sem[1], sem[3])
-    ):
-        copies = []
-        buf[mine] = held[...]
-        for k in range(1, size):
-            copy = pltpu.make_async_remote_copy(
-                src_ref=held,
-                dst_ref=buf.at[mine],
-                send_sem=send.at[k - 1],
-                recv_sem=recv.at[k - 1],
-                device_id=who((mine + k) % size),
-                device_id_type=MESH,
-            )
-            copy.start()
-            copies.append(copy)
-        for k in range(1, size):
-            ref = buf.at[(mine + size - k) % size]
-            pltpu.make_async_remote_copy(
-                src_ref=ref,
-                dst_ref=ref,
-                send_sem=send.at[k - 1],
-                recv_sem=recv.at[k - 1],
-                device_id=who((mine + k) % size),
-                device_id_type=MESH,
-            ).wait_recv()
-        total = buf[0]
-        for i in range(1, size):
-            total = total + buf[i]
-        for copy in copies:
-            copy.wait_send()
-        out[...] = total
-        held = out
-
-
-def total(vec):
-    outs = [jax.ShapeDtypeStruct(vec.shape, F32)]
-    scratch = [
-        pltpu.VMEM((NY * NX,) + vec.shape, F32),
-        pltpu.VMEM((NZ * NC,) + vec.shape, F32),
-    ] + sems(NY * NX - 1) + sems(NZ * NC - 1)
-    return call(total_kernel, outs, scratch, 2, vec)[0]
+    )
+
+
+def circle_sum(group, held, buf, out, send, recv):
+    size, mine, who = group
+    copies = []
+    buf[mine] = held[...]
+    for k in range(1, size):
+        copy = pltpu.make_async_remote_copy(
+            src_ref=held, dst_ref=buf.at[mine], send_sem=send.at[k - 1], recv_sem=recv.at[k - 1],
+            device_id=who((mine + k) % size), device_id_type=MESH,
+        )
+        copy.start()
+        copies.append(copy)
+    for k in range(1, size):
+        ref = buf.at[(mine + size - k) % size]
+        pltpu.make_async_remote_copy(
+            src_ref=ref, dst_ref=ref, send_sem=send.at[k - 1], recv_sem=recv.at[k - 1],
+            device_id=who((mine + k) % size), device_id_type=MESH,
+        ).wait_recv()
+    total = buf[0]
+    for i in range(1, size):
+        total = total + buf[i]
+    out[...] = total
+    return copies
+
+
+def spread_sum(v, span):
+    lane = lax.broadcasted_iota(jnp.int32, v.shape, 1)
+    width = v.shape[1]
+    k = 1
+    while k < span:
+        other = jnp.where((lane & k) != 0, pltpu.roll(v, k, 1), pltpu.roll(v, width - k, 1))
+        v = v + other
+        k *= 2
+    return v
 
 
 def add_into(dst, index, first, others):
@@ -411,10 +410,15 @@
     lax.fori_loop(0, index, body, 0)
 
 
+CHUNK = 512
+
+
 def back_kernel(
-    cot, uc, rowst_in, hid_in, slope_in, mixedt, rowstq, hid_q, dgelu_q, mixedtq, unit_q, inv_q,
-    down, proj, projp,
-    out_up, out_down, out_proj,
+    P_OWN, Q_LEN,
+    q_all, unit_p, inv_p, side, lens, rowst_in, hid_in, slope_in, mixedt, rowstq, hid_q, dgelu_q,
+    mixedtq, unit_q, inv_q, down, proj, projp,
+    out_up, out_down, out_proj, out_loss,
+    terms, emb_p, den, scale, cot_p, held, summed, totals, near_sums, far_sums, cot, uc,
     uc_all, cbuf, abuf, ybuf, bbuf, zbuf, xbuf, mc, mct, mcq, mctq, ucq, rowst, hid, dgelu,
     acc_up, acc_down, acc_proj,
     gd, gu, gp, cd, cu, cp, ad, au, ap, yd, yu, yp, fd, fu, fp, bd, bu, bp, zd, zu, zp, xp, load, *sem
@@ -426,11 +430,13 @@
         send, recv = sem.pop(0), sem.pop(0)
         return Stage(axis, send, recv)
 
-    greet("xzyc")
-    sc, su, sy, sz, sx = (stage(a) for a in "cxyzx")
-    sc.start(lambda to: cot.at[to], lambda k: cbuf)
-    su.start(lambda to: uc, lambda k: uc_all.at[x])
-    uc_all[x] = uc[...]
+    barrier = pltpu.get_barrier_semaphore()
+    groups = circles(y, z, c, x)
+    for size, mine, who in groups:
+        for k in range(1, size):
+            pl.semaphore_signal(
+                barrier, inc=1, device_id=who((mine + k) % size), device_id_type=MESH
+            )
     width = down.shape[1]
     tiles = width // TILE
 
@@ -443,6 +449,89 @@
         ]
         for copy in loads[k]:
             copy.start()
+
+    many = unit_p.shape[0]
+    many_q, emb = q_all.shape
+    own = P_OWN
+    each = many // own
+    n = unit_q.shape[0]
+    half = many_q // NC
+    base = ((y * NZ + z) * NC + c) * (own * NX) + x * own
+    emb_p[...] = unit_p[...].astype(BF16)
+    den[...] = jnp.ones(den.shape, F32)
+
+    def score(j, carry):
+        at_q = pl.ds(pl.multiple_of(j * CHUNK, CHUNK), CHUNK)
+        row = lax.broadcasted_iota(jnp.int32, (each, CHUNK), 0)
+        for k in range(own):
+            rows_k = slice(k * each, (k + 1) * each)
+            similar = nt(emb_p[rows_k, :], q_all[at_q, :])
+            value = jnp.where(row < lens[base + k], jnp.exp(similar * (1.0 / TAU)), 0.0)
+            terms[rows_k, at_q] = value
+            den[k : k + 1, at_q] = jnp.sum(value, axis=0, keepdims=True)
+        return carry
+
+    lax.fori_loop(0, many_q // CHUNK, score, 0)
+    scores = TAU * spread_sum(jnp.log(den[...]), Q_LEN)
+    student = side[0] * jnp.exp(scores)
+    scale[...] = student
+    first = jnp.sum(student, axis=0, keepdims=True)
+    second = jnp.sum(side[1] * scores, axis=0, keepdims=True)
+    lane = lax.broadcasted_iota(jnp.int32, (1, 128), 1) % Q_LEN
+    for r, line in enumerate((first, second)):
+        for u in range(held.shape[1] // 128):
+            packed = jnp.zeros((1, 128), F32)
+            for j in range(min(Q_LEN, many_q // 128 - u * Q_LEN)):
+                v = u * Q_LEN + j
+                packed = jnp.where(lane == j, line[:, v * 128 : (v + 1) * 128], packed)
+            held[r : r + 1, u * 128 : (u + 1) * 128] = packed
+    held[2:8, :] = jnp.zeros((6, held.shape[1]), F32)
+    pl.semaphore_wait(barrier, NY * NX + NZ * NC - 2)
+    sum_sems = [sem.pop(0) for _ in range(4)]
+    copies = circle_sum(groups[0], held, near_sums, summed, sum_sems[0], sum_sems[1])
+    copies += circle_sum(groups[1], summed, far_sums, totals, sum_sems[2], sum_sems[3])
+    lane = lax.broadcasted_iota(jnp.int32, (8, 128), 1) % Q_LEN
+    got = totals[...]
+    for v in range(many_q // 128):
+        u, j = v // Q_LEN, v % Q_LEN
+        at_v = slice(v * 128, (v + 1) * 128)
+        here = jnp.where(lane == j, got[:, u * 128 : (u + 1) * 128], 0.0)
+        here = spread_sum(here, Q_LEN)
+        student_sum, cross = here[0:1, :], here[1:2, :]
+        teacher_sum, teacher_dot = side[2, 0:1, at_v], side[2, 1:2, at_v]
+        out_loss[:, at_v] = (
+            (teacher_dot - cross) / teacher_sum - jnp.log(teacher_sum) + jnp.log(student_sum)
+        )
+        cotangent = scale[:, at_v] / student_sum - side[1, :, at_v] / teacher_sum
+        scale[:, at_v] = cotangent / den[:, at_v]
+    cot_p[...] = jnp.zeros(cot_p.shape, F32)
+
+    def spread(side_of):
+        def body(j, carry):
+            inside = pl.ds(pl.multiple_of(j * CHUNK, CHUNK), CHUNK)
+            at_q = pl.ds(pl.multiple_of(side_of * half + j * CHUNK, CHUNK), CHUNK)
+            weights = jnp.concatenate(
+                [
+                    (terms[k * each : (k + 1) * each, at_q] * scale[k : k + 1, at_q]).astype(BF16)
+                    for k in range(own)
+                ],
+                axis=0,
+            )
+            cot[side_of, inside, :] = dot(weights, emb_p[...], ((0,), (0,))).astype(BF16)
+            cot_p[...] += jnp.dot(weights, q_all[at_q, :], preferred_element_type=F32)
+            return carry
+
+        lax.fori_loop(0, half // CHUNK, body, 0)
+
+    sc, su, sy, sz, sx = (stage(a) for a in "cxyzx")
+    spread(1 - c)
+    sc.start(lambda to: cot.at[to], lambda k: cbuf)
+    spread(c)
+    g = cot_p[...]
+    along = jnp.sum(g * unit_p[...], axis=-1, keepdims=True)
+    uc[...] = (inv_p[...] * (g - unit_p[...] * along)).astype(BF16)
+    su.start(lambda to: uc, lambda k: uc_all.at[x])
+    uc_all[x] = uc[...]
 
     def prepare(u, m, mt):
         def body(j, carry):
@@ -478,7 +567,15 @@
 
     sc.arrive(lambda k, frm: cbuf)
     for i in range(NY):
-        add_into(abuf.at[i], NZ, lambda j: cot[c, i, j], [cbuf.at[i]])
+        def block(ref, j):
+            return ref[pl.ds(pl.multiple_of((i * NZ + j) * n, 16), n), :]
+
+        def near(j, carry):
+            value = block(cot.at[c], j).astype(F32) + block(cbuf, j).astype(F32)
+            abuf[i, j] = value.astype(BF16)
+            return carry
+
+        lax.fori_loop(0, NZ, near, 0)
     sy.start(lambda to: abuf.at[to], lambda k: ybuf.at[k - 1])
     su.arrive(lambda k, frm: uc_all.at[frm])
     passages(3, False)
@@ -498,7 +595,6 @@
     for i in range(1, NX):
         g = g + xbuf[i].astype(F32)
     along = jnp.sum(g * unit_q[...], axis=-1, keepdims=True)
-    n = g.shape[0]
     ucq[...] = jnp.zeros(ucq.shape, BF16)
     ucq[0:n, :] = (inv_q[...] * (g - unit_q[...] * along)).astype(BF16)
     prepare(ucq, mcq, mctq)
@@ -579,22 +675,39 @@
     for i in range(1, NX):
         value = value + xp[i]
     out_proj[...] = value
+    for copy in copies:
+        copy.wait_send()
     for s in [sc, su, sy, sz, sx, s4] + [s for chunk in chunks for s in chunk[7:]]:
         s.finish()
 
 
-def backward(*args):
-    cot, uc, rowst, hid, _, _, rowstq = args[:7]
-    n, emb = cot.shape[-2:]
+def backward(own, q_len, *args):
+    q_all, rowst, hid, rowstq, unit_q = args[0], args[5], args[6], args[9], args[13]
+    n, emb = unit_q.shape
+    many_q = q_all.shape[0]
     width, many = rowst.shape[1:]
     hidden = hid.shape[2]
     few = rowstq.shape[1]
     tall = width // (NC * NY)
     V = pltpu.VMEM
     outs = [jax.ShapeDtypeStruct((16, w), F32) for w in (hidden, hidden, emb)]
+    outs.append(jax.ShapeDtypeStruct((1, many_q), F32))
+    packed = (8, -(-many_q // (128 * q_len)) * 128)
     scratch = [
+        V((many, many_q), F32),
+        V((many, emb), BF16),
+        V((8, many_q), F32),
+        V((8, many_q), F32),
+        V((many, emb), F32),
+        V(packed, F32),
+        V(packed, F32),
+        V(packed, F32),
+        V((NY * NX,) + packed, F32),
+        V((NZ * NC,) + packed, F32),
+        V((NC, many_q // NC, emb), BF16),
+        V((many, emb), BF16),
         V((NX, many, emb), BF16),
-        V((NY, NZ, n, emb), BF16),
+        V((many_q // NC, emb), BF16),
         V((NY, NZ, n, emb), BF16),
         V((NY - 1, NZ, n, emb), BF16),
         V((NZ, n, emb), BF16),
@@ -621,14 +734,11 @@
     scratch += [V((NZ, 16, w), BF16) for w in wide]
     scratch += [V((NZ - 1, 16, w), BF16) for w in wide]
     scratch += [V((NX, 16, emb), F32), pltpu.SemaphoreType.DMA((3 * NX,))]
+    scratch += sems(NY * NX - 1) + sems(NZ * NC - 1)
     for a in "cxyzx" + "cyz" * 3 + "x":
         scratch += sems({"x": NX, "y": NY, "z": NZ, "c": NC}[a] - 1)
-    return call(back_kernel, outs, scratch, 3, *args, outer=([2, 3, 4], ()))
-
-
-def unit_cotangent(g, unit, inverse):
-    along = jnp.sum(g * unit, axis=-1, keepdims=True)
-    return (inverse * (g - unit * along)).astype(BF16)
+    kernel = functools.partial(back_kernel, own, q_len)
+    return call(kernel, outs, scratch, 3, *args, outer=([5, 6, 7], ()), scalars=[4])
 
 
 def local(
@@ -656,13 +766,6 @@
     cands = candidates.shape[1]
     all_cands = cands * NX
 
-    pad_len = (pass_len + 15) // 16 * 16
-
-    positions = jnp.take(owner_map, candidates).astype(F32)
-    table = jnp.zeros((8, 2 * all_cands), F32)
-    table = lax.dynamic_update_slice(table, positions, (0, me_mp * cands))
-    table = lax.dynamic_update_slice(table, teacher_scores, (0, all_cands + me_mp * cands))
-
     order = np.arange(width).reshape(NY, NZ, NC, rows).transpose(2, 0, 1, 3).reshape(-1)
     perm = jnp.asarray(np.eye(width)[order], BF16)
     (
@@ -670,7 +773,7 @@
         rowstq, hid_q, slope_q, mixedtq, unit_q, inv_q, projp,
     ) = encode(
         passage_states, query_states.reshape(q_rows, width), up_weight, down_weight,
-        proj_weight, table, perm,
+        proj_weight, perm, owner_map, candidates, teacher_scores,
     )
     q_all = q_all.reshape(n_dp * q_rows, emb)
     table = t_all.reshape(n_dp, 8, 2 * all_cands)[:, :q_dev].reshape(queries, -1)
@@ -684,36 +787,19 @@
     count = jnp.sum(hit.astype(F32), axis=2)
     teacher_mass = jnp.sum(jnp.where(hit, teacher_exp[None], 0.0), axis=2)
 
-    unit_p = unit_p.reshape(p_own, pad_len, emb)
-    inv_p = inv_p.reshape(p_own, pad_len, 1)
-    emb_p = unit_p.astype(BF16)
-
-    own_len = lax.dynamic_slice_in_dim(lengths, base, p_own, 0)
-    similar = dot(emb_p, q_all, ((2,), (1,)))
-    live = jnp.arange(pad_len)[None, :] < own_len[:, None]
-    terms = jnp.where(live[:, :, None], jnp.exp(similar / TAU), 0.0)
-    denom = jnp.sum(terms, axis=1)
-    scores = TAU * jnp.sum(jnp.log(denom).reshape(p_own, queries, q_len), axis=2)
-    student = count * jnp.exp(scores)
-    sums = jnp.stack([jnp.sum(student, axis=0), jnp.sum(teacher_mass * scores, axis=0)])
-    sums = jnp.pad(sums.reshape(-1), (0, 1024 - 2 * queries)).reshape(8, 128)
-    sums = total(sums).reshape(-1)[: 2 * queries].reshape(2, queries)
-    student_sum = sums[0]
-    loss = (teacher_dot - sums[1]) / teacher_sum - jnp.log(teacher_sum) + jnp.log(student_sum)
-    query_loss = lax.dynamic_slice_in_dim(loss, my_block * q_dev, q_dev, 0)
-    score_cot = student / student_sum - teacher_mass / teacher_sum
-    scale = (score_cot[:, :, None] / denom.reshape(p_own, queries, q_len)).reshape(p_own, 1, -1)
-    weights = (terms * scale).astype(BF16)
-    cot_q = dot(weights, emb_p, ((0, 1), (0, 1))).astype(BF16)
-    cot_p = dot(weights, q_all, ((2,), (0,)))
-    uc_p = unit_cotangent(cot_p, unit_p, inv_p)
-
-    up, down, grad_proj = backward(
-        cot_q.reshape(NC, NY, NZ, q_rows, emb),
-        uc_p.reshape(p_own * pad_len, emb),
+    def rows8(*lines):
+        lines = jnp.concatenate([line.reshape(-1, queries) for line in lines], axis=0)
+        return jnp.pad(lines, ((0, 8 - lines.shape[0]), (0, 0)))
+
+    side = jnp.stack([rows8(count), rows8(teacher_mass), rows8(teacher_sum, teacher_dot)])
+    side = jnp.broadcast_to(side[..., None], side.shape + (q_len,)).reshape(3, 8, -1)
+    up, down, grad_proj, loss = backward(
+        p_own, q_len, q_all, unit_p, inv_p, side, lengths,
         rowst, hid_p, slope_p, mixedt, rowstq, hid_q, slope_q, mixedtq, unit_q, inv_q,
         down_weight, proj_weight, projp,
     )
+    loss = lax.dynamic_slice_in_dim(loss.reshape(-1), my_block * q_rows, q_rows, 0)
+    query_loss = loss.reshape(q_dev, q_len)[:, 0]
     return query_loss, up[:rows], down[:rows].T, grad_proj[:rows]
 
 

time: 170 us -> 151 us (0.89)
  matrix products: 25 us -> 0 us
  Pallas kernels: 130 us -> 140 us
  other arithmetic: 4.37 us -> 0.39 us
    dot_general x3 -> x0, matrix products: 25 us -> none  [dot(): return lax.dot_general(a, b, (dims, ((), ())), preferred_element_type=F32)]
    pallas_call x3 -> x2, Pallas kernels: 130 us -> 140 us  [call(): pl.pallas_call(kernel, out_shape=outs, in_specs=[spec(i, outer[0], scalar...]
    dynamic_update_slice x2 -> x0, local copies, waits for them, and re-layouts: 1.96 us -> none  [the longest x1 1.7 us: local(): lax.dynamic_update_slice(table, teacher_scores, (0, all_cands + me_mp * c...]
    reshape x3 -> x2, local copies, waits for them, and re-layouts: 0.17 us -> 1.97 us  [the longest x1 1.88 us: local(): jnp.broadcast_to(side[..., None], side.shape + (q_len,)).reshape(3, 8, -1)]
where the time goes in v5:
time: 151 us
  Pallas kernels  140 us (93%)
  local copies, waits for them, and re-layouts  9.31 us (6%)
    pallas_call x2, Pallas kernels, call(): pl.pallas_call(kernel, out_shape=outs, in_specs=[spec(i, outer[0], scalar...  140 us

profile of v5, /device:TPU:1, one launch (start us, length us, event | category | flops | bytes accessed | tf_op | source)
XLA Modules:
  0.0 150.5 jit_solution(5315536162477930594)
XLA Ops:
  0.7 56.4 %shard_map.129 = (bf16[4,768,576]{2,1,0:T(8,128)(2,1)}, bf16[4,576,768]{2,1,0:T(8,128)(2,1)}, f32[4,576,768]{2,1,0:T(8,128)}, bf16[768,576]{1,0:T(8,128)(2,1)}, ...) custom-call(bf16[12,180,768]{2,1,0:T(8,128)(2,1)} %states.1, ...), custom_call_target="tpu_custom_call" | custom-call | flops 1000000000 | bytes 60000000 | tf_op jit(solution)/shard_map/pallas_call | solution.py:101
  57.1 1.0 slice.28
  58.1 0.2 fusion.3
  58.4 0.1 copy.15
  58.5 0.1 copy.14
  58.6 0.1 fusion
  58.7 0.7 broadcast_in_dim.23
  59.4 1.9 %reshape.50.side = f32[3,8,6144]{2,1,0:T(8,128)} reshape(f32[3,8,192,32]{3,2,1,0:T(8,128)S(1)} %broadcast_in_dim.23) | data formatting | bytes 1179648 | tf_op jit(solution)/shard_map/reshape | solution.py:795
  61.3 83.6 %shard_map.130 = (f32[16,768]{1,0:T(8,128)}, f32[16,768]{1,0:T(8,128)}, f32[16,128]{1,0:T(8,128)}, f32[1,6144]{1,0:T(1,128)}) custom-call(bf16[6144,128]{1,0:T(8,128)(2,1)} %bitcast.17, f32[576,128]{1,0:T(8,128)} %get-tuple-element.24.unit_p, f32[576,1]{1,0:T(8,128)} %get-tuple-element.25.inv_p, f32[3,8,6144]{2,1,0:T(8,128)} %reshape.50.side, s32[768]{0:T(1024)} %lens.1, ...), custom_call_target="tpu_custom_call" | custom-call | flops 1000000000 | bytes 60000000 | tf_op jit(solution)/shard_map/pallas_call | solution.py:101
  144.9 0.7 dynamic-slice_reduce_fusion
  145.7 0.1 reshape.51
  145.7 0.6 slice_reduce_fusion
  146.4 1.4 slice_bitcast_fusion
  147.8 1.4 copy.18
  149.2 1.3 copy.19
  (5 shorter events, 0.1 us)

commit v6 on v5

--- a/solution.py
+++ b/solution.py
@@ -132,10 +132,10 @@
 
 
 def encode_kernel(
-    states, rows_q, up, down, proj, perm, owner_map, candidates, teacher,
-    rowst_out, hid_out, slope_out, mixedt, unit, inverse, q_all, t_all,
+    q_len, states, rows_q, up, down, proj, perm, owner_map, candidates, teacher,
+    rowst_out, hid_out, slope_out, mixedt, unit, inverse, q_all, side,
     rowstq, hid_q, slope_q, mixedtq, unit_q, inv_q, projp,
-    rows, hid, slope, rowst, part, relay, onward, arrived, mixed, padq, partq, pbuf, tbuf, table,
+    rows, hid, slope, rowst, part, relay, onward, arrived, mixed, padq, partq, pbuf, tbuf, table, t_all,
     ring_send, ring_recv, save, *sem
 ):
     y, z, c, x = place()
@@ -241,10 +241,10 @@
     sz.start(lambda to: q_all.at[c, y, z], lambda k: q_all.at[c, y, z])
     group(3)
     send(3, part.at[3, lower], arrived.at[1, lower], left)
-    for i, k, rows_of, side, who in ((0, 1, lower, 0, right), (1, 3, upper, 1, left)):
+    for i, k, rows_of, way, who in ((0, 1, lower, 0, right), (1, 3, upper, 1, left)):
         ring_copy(i, relay.at[i], relay.at[i], who).wait_recv()
         onward[i] = (part[k, rows_of, :].astype(F32) + relay[i].astype(F32)).astype(BF16)
-        send(4 + i, onward.at[i], arrived.at[side, rows_of], who)
+        send(4 + i, onward.at[i], arrived.at[way, rows_of], who)
     tz.arrive(lambda k, frm: t_all.at[c, y, frm])
     ty.start(lambda to: t_all.at[c, y], lambda k: t_all.at[c, y])
     group(0)
@@ -277,10 +277,42 @@
     sy.arrive(lambda k, frm: q_all.at[c, frm])
     sc.start(lambda to: q_all.at[c], lambda k: q_all.at[c])
     tc.arrive(lambda k, frm: t_all.at[frm])
-    for i, side, rows_of, who in (
+
+    side[...] = jnp.zeros(side.shape, F32)
+    base = ((y * NZ + z) * NC + c) * (own * NX) + x * own
+    rows4, span = 4 * t_all.shape[3], 4 * nq
+    all_c = few_c * NX
+    r = lax.broadcasted_iota(jnp.int32, (rows4, span), 0)
+    start = (r // 8) * nq + (r % 8) * q_len
+    token = lax.broadcasted_iota(jnp.int32, (rows4, span), 1)
+    spread = jnp.logical_and(token >= start, token < start + q_len)
+    spread = jnp.logical_and(spread, r % 8 < candidates.shape[0]).astype(F32)
+    left_half = lax.broadcasted_iota(jnp.int32, (rows4, 2 * all_c), 1) < all_c
+
+    def tally(b):
+        per_y = NZ // 4
+        got = t_all[b // (NY * per_y), (b // per_y) % NY, pl.ds((b % per_y) * 4, 4)]
+        got = got.reshape(rows4, 2 * all_c)
+        scores = jnp.where(left_half, pltpu.roll(got, all_c, 1), 0.0)
+        mass = jnp.where(left_half, jnp.exp(scores), 0.0)
+        tokens = pl.ds(pl.multiple_of(b * span, 128), span)
+
+        def put(i, k, column):
+            line = jnp.sum(jnp.sum(column, axis=1, keepdims=True) * spread, axis=0, keepdims=True)
+            side[i, k : k + 1, tokens] = line
+
+        for k in range(own):
+            hit = jnp.logical_and(left_half, got == (base + k).astype(F32))
+            put(0, k, jnp.where(hit, 1.0, 0.0))
+            put(1, k, jnp.where(hit, mass, 0.0))
+        put(2, 0, mass)
+        put(2, 1, mass * scores)
+
+    tiled(NC * NY * NZ // 4, tally)
+    for i, way, rows_of, who in (
         (2, 0, upper, right), (3, 1, lower, left), (4, 0, lower, right), (5, 1, upper, left)
     ):
-        ref = arrived.at[side, rows_of]
+        ref = arrived.at[way, rows_of]
         ring_copy(i, ref, ref, who).wait_recv()
     step_rows = each
 
@@ -326,7 +358,7 @@
         shape((many, emb), F32),
         shape((many, 1), F32),
         shape((NC, NY, NZ, nq, emb), BF16),
-        shape((NC, NY, NZ) + table, F32),
+        shape((3, 8, NC * NY * NZ * nq), F32),
         shape((width, few), BF16),
         shape((few, hidden), BF16),
         shape((few, hidden), F32),
@@ -350,11 +382,13 @@
         V((NX, nq, width), BF16),
         V((NX,) + table, F32),
         V(table, F32),
+        V((NC, NY, NZ) + table, F32),
     ] + sems(6) + [pltpu.SemaphoreType.DMA((3 * NX,))]
     for size in (NX, NX, NZ, NZ, NY, NY, NC, NC):
         scratch += sems(size - 1)
     args = (states, rows_q, up, down, proj, perm, owner_map, candidates, teacher)
-    return call(encode_kernel, outs, scratch, 1, *args, outer=([], [0, 1, 2]), scalars=[6, 7, 8])
+    kernel = functools.partial(encode_kernel, nq // candidates.shape[0])
+    return call(kernel, outs, scratch, 1, *args, outer=([], [0, 1, 2]), scalars=[6, 7, 8])
 
 
 def circles(y, z, c, x):
@@ -492,6 +526,9 @@
     copies += circle_sum(groups[1], summed, far_sums, totals, sum_sems[2], sum_sems[3])
     lane = lax.broadcasted_iota(jnp.int32, (8, 128), 1) % Q_LEN
     got = totals[...]
+    lane_1 = lax.broadcasted_iota(jnp.int32, (1, 128), 1)
+    first_token = ((c * NY + y) * NZ + z) * n
+    picks = [jnp.zeros((1, 128), F32)] * (n // Q_LEN)
     for v in range(many_q // 128):
         u, j = v // Q_LEN, v % Q_LEN
         at_v = slice(v * 128, (v + 1) * 128)
@@ -499,11 +536,17 @@
         here = spread_sum(here, Q_LEN)
         student_sum, cross = here[0:1, :], here[1:2, :]
         teacher_sum, teacher_dot = side[2, 0:1, at_v], side[2, 1:2, at_v]
-        out_loss[:, at_v] = (
-            (teacher_dot - cross) / teacher_sum - jnp.log(teacher_sum) + jnp.log(student_sum)
-        )
+        loss = (teacher_dot - cross) / teacher_sum - jnp.log(teacher_sum) + jnp.log(student_sum)
+        picks = [
+            jnp.where(lane_1 == first_token + (a * Q_LEN - v * 128), loss, pick)
+            for a, pick in enumerate(picks)
+        ]
         cotangent = scale[:, at_v] / student_sum - side[1, :, at_v] / teacher_sum
         scale[:, at_v] = cotangent / den[:, at_v]
+    line = jnp.zeros((1, 128), F32)
+    for a, pick in enumerate(picks):
+        line = jnp.where(lane_1 == a, jnp.sum(pick, axis=1, keepdims=True), line)
+    out_loss[...] = line
     cot_p[...] = jnp.zeros(cot_p.shape, F32)
 
     def spread(side_of):
@@ -691,7 +734,7 @@
     tall = width // (NC * NY)
     V = pltpu.VMEM
     outs = [jax.ShapeDtypeStruct((16, w), F32) for w in (hidden, hidden, emb)]
-    outs.append(jax.ShapeDtypeStruct((1, many_q), F32))
+    outs.append(jax.ShapeDtypeStruct((1, 128), F32))
     packed = (8, -(-many_q // (128 * q_len)) * 128)
     scratch = [
         V((many, many_q), F32),
@@ -741,6 +784,21 @@
     return call(kernel, outs, scratch, 3, *args, outer=([5, 6, 7], ()), scalars=[4])
 
 
+def trim_kernel(n, *refs):
+    half = len(refs) // 2
+    for src, dst in zip(refs[:half], refs[half:]):
+        dst[...] = src[0:n, :]
+
+
+def trim(n, *arrays):
+    return pl.pallas_call(
+        functools.partial(trim_kernel, n),
+        out_shape=[jax.ShapeDtypeStruct((n, a.shape[1]), a.dtype) for a in arrays],
+        in_specs=[VMEM] * len(arrays),
+        out_specs=[VMEM] * len(arrays),
+    )(*arrays)
+
+
 def local(
     passage_states,
     query_states,
@@ -756,51 +814,27 @@
     q_dev, q_len, _ = query_states.shape
     emb = proj_weight.shape[1]
     n_dp = NY * NZ * NC
-    me_dp, me_mp = lax.axis_index("dp"), lax.axis_index("mp")
-    y, z, c, _ = place()
-    my_block = (c * NY + y) * NZ + z
     p_own = p_dev // NX
     q_rows = q_dev * q_len
     rows = width // n_dp
-    queries = n_dp * q_dev
-    cands = candidates.shape[1]
-    all_cands = cands * NX
 
     order = np.arange(width).reshape(NY, NZ, NC, rows).transpose(2, 0, 1, 3).reshape(-1)
     perm = jnp.asarray(np.eye(width)[order], BF16)
     (
-        rowst, hid_p, slope_p, mixedt, unit_p, inv_p, q_all, t_all,
+        rowst, hid_p, slope_p, mixedt, unit_p, inv_p, q_all, side,
         rowstq, hid_q, slope_q, mixedtq, unit_q, inv_q, projp,
     ) = encode(
         passage_states, query_states.reshape(q_rows, width), up_weight, down_weight,
         proj_weight, perm, owner_map, candidates, teacher_scores,
     )
     q_all = q_all.reshape(n_dp * q_rows, emb)
-    table = t_all.reshape(n_dp, 8, 2 * all_cands)[:, :q_dev].reshape(queries, -1)
-    pos_all, teacher = table[:, :all_cands], table[:, all_cands:]
-    teacher_exp = jnp.exp(teacher)
-    teacher_sum = jnp.sum(teacher_exp, axis=1)
-    teacher_dot = jnp.sum(teacher_exp * teacher, axis=1)
-    base = me_dp * p_dev + me_mp * p_own
-    mine = base + jnp.arange(p_own)
-    hit = pos_all[None] == mine[:, None, None].astype(F32)
-    count = jnp.sum(hit.astype(F32), axis=2)
-    teacher_mass = jnp.sum(jnp.where(hit, teacher_exp[None], 0.0), axis=2)
-
-    def rows8(*lines):
-        lines = jnp.concatenate([line.reshape(-1, queries) for line in lines], axis=0)
-        return jnp.pad(lines, ((0, 8 - lines.shape[0]), (0, 0)))
-
-    side = jnp.stack([rows8(count), rows8(teacher_mass), rows8(teacher_sum, teacher_dot)])
-    side = jnp.broadcast_to(side[..., None], side.shape + (q_len,)).reshape(3, 8, -1)
     up, down, grad_proj, loss = backward(
         p_own, q_len, q_all, unit_p, inv_p, side, lengths,
         rowst, hid_p, slope_p, mixedt, rowstq, hid_q, slope_q, mixedtq, unit_q, inv_q,
         down_weight, proj_weight, projp,
     )
-    loss = lax.dynamic_slice_in_dim(loss.reshape(-1), my_block * q_rows, q_rows, 0)
-    query_loss = loss.reshape(q_dev, q_len)[:, 0]
-    return query_loss, up[:rows], down[:rows].T, grad_proj[:rows]
+    up, down, grad_proj = trim(rows, up, down, grad_proj)
+    return loss[0, :q_dev], up, down.T, grad_proj
 
 
 def solution(mesh):

time: 151 us -> 144 us (0.954)
  local copies, waits for them, and re-layouts: 9.31 us -> 1.08 us
  Pallas kernels: 140 us -> 142 us
    unnamed x2 -> x0, local copies, waits for them, and re-layouts: 2.72 us -> none
    reshape x3 -> x0, local copies, waits for them, and re-layouts: 2.01 us -> none  [the longest x1 1.88 us: local(): jnp.broadcast_to(side[..., None], side.shape + (q_len,)).reshape(3, 8, -1)]
    slice x3 -> x0, local copies, waits for them, and re-layouts: 1.68 us -> none  [the longest x1 0.97 us: local(): t_all.reshape(n_dp, 8, 2 * all_cands)[:, :q_dev].reshape(queries, -1)]
where the time goes in v6:
time: 144 us
  Pallas kernels  142 us (99%)
    pallas_call x2, Pallas kernels, call(): pl.pallas_call(kernel, out_shape=outs, in_specs=[spec(i, outer[0], scalar...  141 us

profile of v6, /device:TPU:1, one launch (start us, length us, event | category | flops | bytes accessed | tf_op | source)
XLA Modules:
  0.0 144.0 jit_solution(2752236853481198684)
XLA Ops:
  0.6 56.5 %shard_map.129 = (bf16[4,768,576]{2,1,0:T(8,128)(2,1)}, bf16[4,576,768]{2,1,0:T(8,128)(2,1)}, f32[4,576,768]{2,1,0:T(8,128)}, bf16[768,576]{1,0:T(8,128)(2,1)}, ...) custom-call(bf16[12,180,768]{2,1,0:T(8,128)(2,1)} %states.1, ...), custom_call_target="tpu_custom_call" | custom-call | flops 1000000000 | bytes 60000000 | tf_op jit(solution)/shard_map/pallas_call | solution.py:101
  57.2 84.3 %shard_map.130 = (f32[16,768]{1,0:T(8,128)}, f32[16,768]{1,0:T(8,128)}, f32[16,128]{1,0:T(8,128)}, f32[1,128]{1,0:T(1,128)}) custom-call(bf16[6144,128]{1,0:T(8,128)(2,1)} %bitcast.5, f32[576,128]{1,0:T(8,128)} %get-tuple-element.27.unit_p, f32[576,1]{1,0:T(8,128)} %get-tuple-element.28.inv_p, f32[3,8,6144]{2,1,0:T(8,128)} %get-tuple-element.29.side, ...), custom_call_target="tpu_custom_call" | custom-call | flops 1000000000 | bytes 60000000 | tf_op jit(solution)/shard_map/pallas_call | solution.py:101
  141.5 1.1 slice_bitcast_fusion
  142.5 1.5 %shard_map.131 = (f32[12,768]{1,0:T(8,128)}, f32[12,768]{1,0:T(8,128)}, f32[12,128]{1,0:T(8,128)}) custom-call(f32[16,768]{1,0:T(8,128)} %get-tuple-element.42.refs_0_, f32[16,768]{1,0:T(8,128)} %get-tuple-element.43.refs_1_, f32[16,128]{1,0:T(8,128)} %get-tuple-element.44.refs_2_), custom_call_target="tpu_custom_call" | custom-call | tf_op jit(solution)/shard_map/pallas_call | solution.py:794

commit v7 on v6

--- a/solution.py
+++ b/solution.py
@@ -133,9 +133,9 @@
 
 def encode_kernel(
     q_len, states, rows_q, up, down, proj, perm, owner_map, candidates, teacher,
-    rowst_out, hid_out, slope_out, mixedt, unit, inverse, q_all, side,
-    rowstq, hid_q, slope_q, mixedtq, unit_q, inv_q, projp,
-    rows, hid, slope, rowst, part, relay, onward, arrived, mixed, padq, partq, pbuf, tbuf, table, t_all,
+    rowst_out, hid_out, slope_out, downt, unit, inverse, q_all, side,
+    rowstq, hid_q, slope_q, unit_q, inv_q, projp,
+    rows, hid, slope, rowst, part, sent, arrived, padq, partq, sent_q, pbuf, tbuf, table, t_all,
     ring_send, ring_recv, save, *sem
 ):
     y, z, c, x = place()
@@ -149,8 +149,7 @@
     nq = rows_q.shape[0]
     own, length = states.shape[0] // NX, states.shape[1]
     many = rows.shape[1]
-    each, half = many // own, many // 2
-    right, left = at(y, z, c, lax.rem(x + 1, NX)), at(y, z, c, lax.rem(x + NX - 1, NX))
+    each = many // own
     ring, saves = [], []
 
     def ring_copy(i, src, dst, who):
@@ -193,11 +192,13 @@
         for i in range(own):
             rows[g, each * (i + 1) - 16 : each * (i + 1), :] = jnp.zeros((16, width), BF16)
             rows[g, each * i : each * i + length, :] = states[g * own + i]
-        feed(rows.at[g], hid.at[g], slope.at[g], part.at[k])
+        feed(rows.at[g], hid.at[g], slope.at[g], part)
+        sent[k] = jnp.dot(part[...], proj[...], preferred_element_type=F32)
+        if k:
+            send(k - 1, sent.at[k], arrived.at[k - 1], at(y, z, c, g))
         keep(hid.at[g], hid_out.at[g])
         keep(slope.at[g], slope_out.at[g])
 
-    lower, upper = pl.ds(0, half), pl.ds(half, half)
     row = lax.broadcasted_iota(jnp.int32, table.shape, 0)
     lane = lax.broadcasted_iota(jnp.int32, table.shape, 1)
     value = jnp.zeros(table.shape, F32)
@@ -214,44 +215,34 @@
     padq[...] = jnp.zeros(padq.shape, BF16)
     padq[0:nq, :] = rows_q[...]
     feed(padq, hid_q, slope_q, partq)
-    short = partq.at[pl.ds(0, nq)]
-    sx.start(lambda to: short, lambda k: pbuf.at[x])
-    pbuf[x] = partq[0:nq, :]
+    sent_q[...] = jnp.dot(partq[0:nq, :], proj[...], preferred_element_type=F32)
+    sx.start(lambda to: sent_q, lambda k: pbuf.at[x])
+    pbuf[x] = sent_q[...]
     group(2)
-    send(0, part.at[2, lower], relay.at[0], right)
-    send(1, part.at[2, upper], relay.at[1], left)
     tx.arrive(lambda k, frm: tbuf.at[frm])
     merged = tbuf[0]
     for i in range(1, NX):
         merged = merged + tbuf[i]
     t_all[c, y, z] = merged
     tz.start(lambda to: t_all.at[c, y, z], lambda k: t_all.at[c, y, z])
-    group(1)
-    send(2, part.at[1, upper], arrived.at[0, upper], right)
     sx.arrive(lambda k, frm: pbuf.at[frm])
-    ffn = pbuf[0].astype(F32)
-    for i in range(1, NX):
-        ffn = ffn + pbuf[i].astype(F32)
-    blend = (rows_q[...].astype(F32) + ffn).astype(BF16)
-    projected = jnp.dot(blend, proj[...], preferred_element_type=F32)
+    projected = jnp.dot(rows_q[...], proj[...], preferred_element_type=F32)
+    for i in range(NX):
+        projected = projected + pbuf[i]
     inv = lax.rsqrt(jnp.sum(projected * projected, axis=-1, keepdims=True) + EPS)
     inv_q[...] = inv
     unit_q[...] = projected * inv
     q_all[c, y, z] = (projected * inv).astype(BF16)
     sz.start(lambda to: q_all.at[c, y, z], lambda k: q_all.at[c, y, z])
-    group(3)
-    send(3, part.at[3, lower], arrived.at[1, lower], left)
-    for i, k, rows_of, way, who in ((0, 1, lower, 0, right), (1, 3, upper, 1, left)):
-        ring_copy(i, relay.at[i], relay.at[i], who).wait_recv()
-        onward[i] = (part[k, rows_of, :].astype(F32) + relay[i].astype(F32)).astype(BF16)
-        send(4 + i, onward.at[i], arrived.at[way, rows_of], who)
+    group(1)
     tz.arrive(lambda k, frm: t_all.at[c, y, frm])
     ty.start(lambda to: t_all.at[c, y], lambda k: t_all.at[c, y])
-    group(0)
+    group(3)
     sz.arrive(lambda k, frm: q_all.at[c, y, frm])
     sy.start(lambda to: q_all.at[c, y], lambda k: q_all.at[c, y])
     ty.arrive(lambda k, frm: t_all.at[c, frm])
     tc.start(lambda to: t_all.at[c], lambda k: t_all.at[c])
+    group(0)
     for k in range(NX):
         g = lax.rem(x + k, NX)
 
@@ -268,12 +259,11 @@
         ).astype(BF16)
 
     tiled(tiles, turn_q)
-    padq[0:nq, :] = blend
-
-    def turn_mixed_q(j):
-        mixedtq[cut(j), :] = nt(perm[cut(j), :], padq[...]).astype(BF16)
-
-    tiled(tiles, turn_mixed_q)
+
+    def turn_down(j):
+        downt[cut(j), :] = nt(perm[cut(j), :], down[...]).astype(BF16)
+
+    tiled(tiles, turn_down)
     sy.arrive(lambda k, frm: q_all.at[c, frm])
     sc.start(lambda to: q_all.at[c], lambda k: q_all.at[c])
     tc.arrive(lambda k, frm: t_all.at[frm])
@@ -309,30 +299,20 @@
         put(2, 1, mass * scores)
 
     tiled(NC * NY * NZ // 4, tally)
-    for i, way, rows_of, who in (
-        (2, 0, upper, right), (3, 1, lower, left), (4, 0, lower, right), (5, 1, upper, left)
-    ):
-        ref = arrived.at[way, rows_of]
-        ring_copy(i, ref, ref, who).wait_recv()
-    step_rows = each
+    for i in range(NX - 1):
+        ring_copy(i, arrived.at[i], arrived.at[i], at(y, z, c, x)).wait_recv()
 
     def finish_rows(i):
-        at_rows = pl.ds(pl.multiple_of(i * step_rows, 16), step_rows)
-        ffn = part[0, at_rows, :].astype(F32)
-        ffn = ffn + arrived[0, at_rows, :].astype(F32) + arrived[1, at_rows, :].astype(F32)
-        blend = (rows[x, at_rows, :].astype(F32) + ffn).astype(BF16)
-        mixed[at_rows, :] = blend
-        projected = jnp.dot(blend, proj[...], preferred_element_type=F32)
+        at_rows = pl.ds(pl.multiple_of(i * each, 16), each)
+        projected = jnp.dot(rows[x, at_rows, :], proj[...], preferred_element_type=F32)
+        projected = projected + sent[0, at_rows, :]
+        for k in range(NX - 1):
+            projected = projected + arrived[k, at_rows, :]
         inv = lax.rsqrt(jnp.sum(projected * projected, axis=-1, keepdims=True) + EPS)
         inverse[at_rows, :] = inv
         unit[at_rows, :] = projected * inv
 
     tiled(own, finish_rows)
-
-    def turn_mixed(j):
-        mixedt[cut(j), :] = nt(perm[cut(j), :], mixed[...]).astype(BF16)
-
-    tiled(tiles, turn_mixed)
     sc.arrive(lambda k, frm: q_all.at[frm])
     for stage in (sx, tx, sz, tz, sy, ty, sc, tc):
         stage.finish()
@@ -354,7 +334,7 @@
         shape((NX, width, many), BF16),
         shape((NX, many, hidden), BF16),
         shape((NX, many, hidden), F32),
-        shape((width, many), BF16),
+        shape((width, hidden), BF16),
         shape((many, emb), F32),
         shape((many, 1), F32),
         shape((NC, NY, NZ, nq, emb), BF16),
@@ -362,7 +342,6 @@
         shape((width, few), BF16),
         shape((few, hidden), BF16),
         shape((few, hidden), F32),
-        shape((width, few), BF16),
         shape((nq, emb), F32),
         shape((nq, 1), F32),
         shape((width, emb), BF16),
@@ -372,18 +351,17 @@
         V((NX, many, hidden), BF16),
         V((NX, many, hidden), F32),
         V((NX, width, many), BF16),
-        V((NX, many, width), BF16),
-        V((2, many // 2, width), BF16),
-        V((2, many // 2, width), BF16),
-        V((2, many, width), BF16),
         V((many, width), BF16),
+        V((NX, many, emb), F32),
+        V((NX - 1, many, emb), F32),
         V((few, width), BF16),
         V((few, width), BF16),
-        V((NX, nq, width), BF16),
+        V((nq, emb), F32),
+        V((NX, nq, emb), F32),
         V((NX,) + table, F32),
         V(table, F32),
         V((NC, NY, NZ) + table, F32),
-    ] + sems(6) + [pltpu.SemaphoreType.DMA((3 * NX,))]
+    ] + sems(NX - 1) + [pltpu.SemaphoreType.DMA((3 * NX,))]
     for size in (NX, NX, NZ, NZ, NY, NY, NC, NC):
         scratch += sems(size - 1)
     args = (states, rows_q, up, down, proj, perm, owner_map, candidates, teacher)
@@ -449,11 +427,11 @@
 
 def back_kernel(
     P_OWN, Q_LEN,
-    q_all, unit_p, inv_p, side, lens, rowst_in, hid_in, slope_in, mixedt, rowstq, hid_q, dgelu_q,
-    mixedtq, unit_q, inv_q, down, proj, projp,
+    q_all, unit_p, inv_p, side, lens, rowst_in, hid_in, slope_in, downt, rowstq, hid_q, dgelu_q,
+    unit_q, inv_q, down, proj, projp,
     out_up, out_down, out_proj, out_loss,
     terms, emb_p, den, scale, cot_p, held, summed, totals, near_sums, far_sums, cot, uc,
-    uc_all, cbuf, abuf, ybuf, bbuf, zbuf, xbuf, mc, mct, mcq, mctq, ucq, rowst, hid, dgelu,
+    uc_all, cbuf, abuf, ybuf, bbuf, zbuf, xbuf, mc, mct, mcq, mctq, ucq, rowst, hid, dgelu, turned,
     acc_up, acc_down, acc_proj,
     gd, gu, gp, cd, cu, cp, ad, au, ap, yd, yu, yp, fd, fu, fp, bd, bu, bp, zd, zu, zp, xp, load, *sem
 ):
@@ -584,11 +562,21 @@
 
         lax.fori_loop(0, tiles, body, 0)
 
+    unit_matrix = lax.broadcasted_iota(jnp.int32, (emb, emb), 0)
+    unit_matrix = unit_matrix == lax.broadcasted_iota(jnp.int32, (emb, emb), 1)
+    unit_matrix = jnp.where(unit_matrix, 1.0, 0.0).astype(BF16)
+
     def passages(k, first):
         g = lax.rem(x + k, NX)
         prepare(uc_all.at[g], mc, mct)
         for copy in loads[k]:
             copy.wait()
+        uct = nt(unit_matrix, uc_all[g]).astype(BF16)
+        cot_hid = jnp.dot(uct, hid[g], preferred_element_type=F32)
+        if first:
+            turned[...] = cot_hid
+        else:
+            turned[...] += cot_hid
 
         def body(j, carry):
             term = jnp.dot(mct[...], hid[g, :, cut(j)], preferred_element_type=F32)
@@ -606,7 +594,7 @@
         lax.fori_loop(0, tiles, body, 0)
 
     passages(0, True)
-    acc_proj[...] = jnp.dot(mixedt[...], uc[...], preferred_element_type=F32)
+    acc_proj[...] = jnp.dot(rowst[x], uc[...], preferred_element_type=F32)
 
     sc.arrive(lambda k, frm: cbuf)
     for i in range(NY):
@@ -668,7 +656,13 @@
     at_row = lax.broadcasted_iota(jnp.int32, ucq.shape, 0)
     mine = jnp.logical_and(at_row >= x * part, at_row < (x + 1) * part)
     own = jnp.where(mine, ucq[...].astype(F32), 0.0).astype(BF16)
-    term = acc_proj[...] + jnp.dot(mixedtq[...], own, preferred_element_type=F32)
+    term = acc_proj[...] + jnp.dot(rowstq[...], own, preferred_element_type=F32)
+    cot_hid = turned[...] + jnp.dot(
+        nt(unit_matrix, ucq[...]).astype(BF16), hid_q[...], preferred_element_type=F32
+    )
+    high = cot_hid.astype(BF16)
+    low = (cot_hid - high.astype(F32)).astype(BF16)
+    term = term + nt(downt[...], high) + nt(downt[...], low)
     gp[...] = term.astype(BF16).reshape(gp.shape)
     leave(chunks[1])
 
@@ -725,7 +719,7 @@
 
 
 def backward(own, q_len, *args):
-    q_all, rowst, hid, rowstq, unit_q = args[0], args[5], args[6], args[9], args[13]
+    q_all, rowst, hid, rowstq, unit_q = args[0], args[5], args[6], args[9], args[12]
     n, emb = unit_q.shape
     many_q = q_all.shape[0]
     width, many = rowst.shape[1:]
@@ -764,6 +758,7 @@
         V((NX, width, many), BF16),
         V((NX, many, hidden), BF16),
         V((NX, many, hidden), F32),
+        V((emb, hidden), F32),
         V((width, hidden), F32),
         V((width, hidden), F32),
         V((width, emb), F32),
@@ -821,8 +816,8 @@
     order = np.arange(width).reshape(NY, NZ, NC, rows).transpose(2, 0, 1, 3).reshape(-1)
     perm = jnp.asarray(np.eye(width)[order], BF16)
     (
-        rowst, hid_p, slope_p, mixedt, unit_p, inv_p, q_all, side,
-        rowstq, hid_q, slope_q, mixedtq, unit_q, inv_q, projp,
+        rowst, hid_p, slope_p, downt, unit_p, inv_p, q_all, side,
+        rowstq, hid_q, slope_q, unit_q, inv_q, projp,
     ) = encode(
         passage_states, query_states.reshape(q_rows, width), up_weight, down_weight,
         proj_weight, perm, owner_map, candidates, teacher_scores,
@@ -830,7 +825,7 @@
     q_all = q_all.reshape(n_dp * q_rows, emb)
     up, down, grad_proj, loss = backward(
         p_own, q_len, q_all, unit_p, inv_p, side, lengths,
-        rowst, hid_p, slope_p, mixedt, rowstq, hid_q, slope_q, mixedtq, unit_q, inv_q,
+        rowst, hid_p, slope_p, downt, rowstq, hid_q, slope_q, unit_q, inv_q,
         down_weight, proj_weight, projp,
     )
     up, down, grad_proj = trim(rows, up, down, grad_proj)

time: 144 us -> 136 us (0.944)
  Pallas kernels: 142 us -> 133 us
    pallas_call x2, Pallas kernels: 141 us -> 132 us  [call(): pl.pallas_call(kernel, out_shape=outs, in_specs=[spec(i, outer[0], scalar...]
where the time goes in v7:
time: 136 us; the launch traced here: 135 us
  Pallas kernels  133 us (98%)
    pallas_call x2, Pallas kernels, call(): pl.pallas_call(kernel, out_shape=outs, in_specs=[spec(i, outer[0], scalar...  132 us

profile of v7, /device:TPU:1, one launch (start us, length us, event | category | flops | bytes accessed | tf_op | source)
XLA Modules:
  0.0 135.0 jit_solution(10868976198477648223)
XLA Ops:
  0.6 45.9 %shard_map.129 = (bf16[4,768,576]{2,1,0:T(8,128)(2,1)}, bf16[4,576,768]{2,1,0:T(8,128)(2,1)}, f32[4,576,768]{2,1,0:T(8,128)}, bf16[768,768]{1,0:T(8,128)(2,1)}, ...) custom-call(bf16[12,180,768]{2,1,0:T(8,128)(2,1)} %states.1, ...), custom_call_target="tpu_custom_call" | custom-call | flops 1000000000 | bytes 60000000 | tf_op jit(solution)/shard_map/pallas_call | solution.py:101
  46.6 85.9 %shard_map.130 = (f32[16,768]{1,0:T(8,128)}, f32[16,768]{1,0:T(8,128)}, f32[16,128]{1,0:T(8,128)}, f32[1,128]{1,0:T(1,128)}) custom-call(bf16[6144,128]{1,0:T(8,128)(2,1)} %bitcast.5, f32[576,128]{1,0:T(8,128)} %get-tuple-element.26.unit_p, f32[576,1]{1,0:T(8,128)} %get-tuple-element.27.inv_p, f32[3,8,6144]{2,1,0:T(8,128)} %get-tuple-element.28.side, ...), custom_call_target="tpu_custom_call" | custom-call | flops 1000000000 | bytes 60000000 | tf_op jit(solution)/shard_map/pallas_call | solution.py:101
  132.5 1.1 slice_bitcast_fusion
  133.6 1.5 %shard_map.131 = (f32[12,768]{1,0:T(8,128)}, f32[12,768]{1,0:T(8,128)}, f32[12,128]{1,0:T(8,128)}) custom-call(f32[16,768]{1,0:T(8,128)} %get-tuple-element.40.refs_0_, f32[16,768]{1,0:T(8,128)} %get-tuple-element.41.refs_1_, f32[16,128]{1,0:T(8,128)} %get-tuple-element.42.refs_2_), custom_call_target="tpu_custom_call" | custom-call | tf_op jit(solution)/shard_map/pallas_call | solution.py:789

commit v8 on v7

--- a/solution.py
+++ b/solution.py
@@ -433,10 +433,13 @@
     terms, emb_p, den, scale, cot_p, held, summed, totals, near_sums, far_sums, cot, uc,
     uc_all, cbuf, abuf, ybuf, bbuf, zbuf, xbuf, mc, mct, mcq, mctq, ucq, rowst, hid, dgelu, turned,
     acc_up, acc_down, acc_proj,
-    gd, gu, gp, cd, cu, cp, ad, au, ap, yd, yu, yp, fd, fu, fp, bd, bu, bp, zd, zu, zp, xp, load, *sem
+    gp, cp, ap, yp, fp, bp, zp, xp, load, *rest
 ):
     y, z, c, x = place()
-    sem = list(sem)
+    tiles = down.shape[1] // TILE
+    parts = 2 * tiles
+    bufs = [rest[i * parts : (i + 1) * parts] for i in range(7)]
+    sem = list(rest[7 * parts :])
 
     def stage(axis):
         send, recv = sem.pop(0), sem.pop(0)
@@ -450,7 +453,6 @@
                 barrier, inc=1, device_id=who((mine + k) % size), device_id_type=MESH
             )
     width = down.shape[1]
-    tiles = width // TILE
 
     loads = {}
     for i, k in enumerate((0, 3, 1, 2)):
@@ -629,28 +631,32 @@
     ucq[...] = jnp.zeros(ucq.shape, BF16)
     ucq[0:n, :] = (inv_q[...] * (g - unit_q[...] * along)).astype(BF16)
     prepare(ucq, mcq, mctq)
-    blocks = gd.shape[:3]
-
-    def down_last(j, carry):
-        term = acc_down[:, cut(j)] + jnp.dot(
-            mctq[...], hid_q[:, cut(j)], preferred_element_type=F32
+    blocks = gp.shape[:3]
+    chunks = []
+
+    def onward(chunk):
+        grads, near, total_a, far, _, _, _, s1, s2, _ = chunk
+        s1.arrive(lambda k, frm: near)
+        add_into(total_a, NY, lambda j: grads[c, j], [near])
+        s2.start(lambda to: total_a.at[to], lambda k: far.at[k - 1])
+
+    def leave(refs):
+        chunk = tuple(refs) + tuple(stage(a) for a in "cyz")
+        chunk[7].start(lambda to: chunk[0].at[to], lambda k: chunk[1])
+        if chunks:
+            onward(chunks[-1])
+        chunks.append(chunk)
+
+    def columns(i):
+        return tuple(buf[i] for buf in bufs)
+
+    for j in range(tiles):
+        at_j = slice(j * TILE, (j + 1) * TILE)
+        term = acc_down[:, at_j] + jnp.dot(
+            mctq[...], hid_q[:, at_j], preferred_element_type=F32
         )
-        gd[:, :, :, cut(j)] = term.astype(BF16).reshape(blocks + (TILE,))
-        return carry
-
-    lax.fori_loop(0, tiles, down_last, 0)
-    chunks = []
-    for grads, near, total_a, far, f32_sum, padded, last in (
-        (gd, cd, ad, yd, fd, bd, zd),
-        (gp, cp, ap, yp, fp, bp, zp),
-        (gu, cu, au, yu, fu, bu, zu),
-    ):
-        chunks.append((grads, near, total_a, far, f32_sum, padded, last) + tuple(stage(a) for a in "cyz"))
-
-    def leave(chunk):
-        chunk[7].start(lambda to: chunk[0].at[to], lambda k: chunk[1])
-
-    leave(chunks[0])
+        bufs[0][j][...] = term.astype(BF16).reshape(blocks + (TILE,))
+        leave(columns(j))
 
     part = n // NX
     at_row = lax.broadcasted_iota(jnp.int32, ucq.shape, 0)
@@ -664,22 +670,16 @@
     low = (cot_hid - high.astype(F32)).astype(BF16)
     term = term + nt(downt[...], high) + nt(downt[...], low)
     gp[...] = term.astype(BF16).reshape(gp.shape)
-    leave(chunks[1])
-
-    def up_last(j, carry):
-        back = nt(mcq[...], down[cut(j), :])
-        pre = (back * dgelu_q[:, cut(j)]).astype(BF16)
-        up = acc_up[:, cut(j)] + jnp.dot(rowstq[...], pre, preferred_element_type=F32)
-        gu[:, :, :, cut(j)] = up.astype(BF16).reshape(blocks + (TILE,))
-        return carry
-
-    lax.fori_loop(0, tiles, up_last, 0)
-    leave(chunks[2])
-
-    for grads, near, total_a, far, f32_sum, padded, last, s1, s2, s3 in chunks:
-        s1.arrive(lambda k, frm: near)
-        add_into(total_a, NY, lambda j: grads[c, j], [near])
-        s2.start(lambda to: total_a.at[to], lambda k: far.at[k - 1])
+    leave((gp, cp, ap, yp, fp, bp, zp))
+    for j in range(tiles):
+        at_j = slice(j * TILE, (j + 1) * TILE)
+        back = nt(mcq[...], down[at_j, :])
+        pre = (back * dgelu_q[:, at_j]).astype(BF16)
+        up = acc_up[:, at_j] + jnp.dot(rowstq[...], pre, preferred_element_type=F32)
+        bufs[0][tiles + j][...] = up.astype(BF16).reshape(blocks + (TILE,))
+        leave(columns(tiles + j))
+
+    onward(chunks[-1])
     per = width // (NY * NZ * NC)
     for grads, near, total_a, far, f32_sum, padded, last, s1, s2, s3 in chunks:
         s2.arrive(lambda k, frm: far.at[k - 1])
@@ -692,21 +692,21 @@
         for i in range(NZ):
             padded[i] = f32_sum[i * per : i * per + 16, :].astype(BF16)
         s3.start(lambda to: padded.at[to], lambda k: last.at[k - 1])
-    finals = []
     s4 = stage("x")
-    for at_chunk in (1, 0, 2):
+    for at_chunk in [tiles] + [i for i in range(len(chunks)) if i != tiles]:
         grads, near, total_a, far, f32_sum, padded, last, s1, s2, s3 = chunks[at_chunk]
         s3.arrive(lambda k, frm: last.at[k - 1])
         value = padded[z].astype(F32)
         for i in range(NZ - 1):
             value = value + last[i].astype(F32)
-        if at_chunk == 1:
+        if at_chunk == tiles:
             xp[x] = value
             s4.start(lambda to: xp.at[x], lambda k: xp.at[x])
-        elif at_chunk == 0:
-            out_down[...] = value
+        elif at_chunk < tiles:
+            out_down[:, at_chunk * TILE : (at_chunk + 1) * TILE] = value
         else:
-            out_up[...] = value
+            at_j = at_chunk - tiles - 1
+            out_up[:, at_j * TILE : (at_j + 1) * TILE] = value
     s4.arrive(lambda k, frm: xp.at[frm])
     value = xp[0]
     for i in range(1, NX):
@@ -763,17 +763,25 @@
         V((width, hidden), F32),
         V((width, emb), F32),
     ]
-    wide = (hidden, hidden, emb)
-    scratch += [V((NC, NY, tall, w), BF16) for w in wide]
-    scratch += [V((NY, tall, w), BF16) for w in wide]
-    scratch += [V((NY, tall, w), BF16) for w in wide]
-    scratch += [V((NY - 1, tall, w), BF16) for w in wide]
-    scratch += [V((tall + 8, w), F32) for w in wide]
-    scratch += [V((NZ, 16, w), BF16) for w in wide]
-    scratch += [V((NZ - 1, 16, w), BF16) for w in wide]
+    parts = 2 * (hidden // TILE)
+
+    def chunk_buffers(w):
+        return [
+            V((NC, NY, tall, w), BF16),
+            V((NY, tall, w), BF16),
+            V((NY, tall, w), BF16),
+            V((NY - 1, tall, w), BF16),
+            V((tall + 8, w), F32),
+            V((NZ, 16, w), BF16),
+            V((NZ - 1, 16, w), BF16),
+        ]
+
+    scratch += chunk_buffers(emb)
     scratch += [V((NX, 16, emb), F32), pltpu.SemaphoreType.DMA((3 * NX,))]
+    for buffer in chunk_buffers(TILE):
+        scratch += [buffer] * parts
     scratch += sems(NY * NX - 1) + sems(NZ * NC - 1)
-    for a in "cxyzx" + "cyz" * 3 + "x":
+    for a in "cxyzx" + "cyz" * (parts + 1) + "x":
         scratch += sems({"x": NX, "y": NY, "z": NZ, "c": NC}[a] - 1)
     kernel = functools.partial(back_kernel, own, q_len)
     return call(kernel, outs, scratch, 3, *args, outer=([5, 6, 7], ()), scalars=[4])

time: 136 us -> 135 us (level)
  no operation moved by 1% of the time
where the time goes in v8:
time: 135 us
  Pallas kernels  133 us (99%)
    pallas_call x2, Pallas kernels, call(): pl.pallas_call(kernel, out_shape=outs, in_specs=[spec(i, outer[0], scalar...  132 us

profile of v8, /device:TPU:1, one launch (start us, length us, event | category | flops | bytes accessed | tf_op | source)
XLA Modules:
  0.0 135.0 jit_solution(5500499780331432035)
XLA Ops:
  0.6 45.9 %shard_map.129 = (bf16[4,768,576]{2,1,0:T(8,128)(2,1)}, bf16[4,576,768]{2,1,0:T(8,128)(2,1)}, f32[4,576,768]{2,1,0:T(8,128)}, bf16[768,768]{1,0:T(8,128)(2,1)}, ...) custom-call(bf16[12,180,768]{2,1,0:T(8,128)(2,1)} %states.1, ...), custom_call_target="tpu_custom_call" | custom-call | flops 1000000000 | bytes 60000000 | tf_op jit(solution)/shard_map/pallas_call | solution.py:101
  46.6 85.8 %shard_map.130 = (f32[16,768]{1,0:T(8,128)}, f32[16,768]{1,0:T(8,128)}, f32[16,128]{1,0:T(8,128)}, f32[1,128]{1,0:T(1,128)}) custom-call(bf16[6144,128]{1,0:T(8,128)(2,1)} %bitcast.5, f32[576,128]{1,0:T(8,128)} %get-tuple-element.26.unit_p, f32[576,1]{1,0:T(8,128)} %get-tuple-element.27.inv_p, f32[3,8,6144]{2,1,0:T(8,128)} %get-tuple-element.28.side, ...), custom_call_target="tpu_custom_call" | custom-call | flops 1000000000 | bytes 60000000 | tf_op jit(solution)/shard_map/pallas_call | solution.py:101
  132.4 1.1 slice_bitcast_fusion
  133.5 1.5 %shard_map.131 = (f32[12,768]{1,0:T(8,128)}, f32[12,768]{1,0:T(8,128)}, f32[12,128]{1,0:T(8,128)}) custom-call(f32[16,768]{1,0:T(8,128)} %get-tuple-element.40.refs_0_, f32[16,768]{1,0:T(8,128)} %get-tuple-element.41.refs_1_, f32[16,128]{1,0:T(8,128)} %get-tuple-element.42.refs_2_), custom_call_target="tpu_custom_call" | custom-call | tf_op jit(solution)/shard_map/pallas_call | solution.py:797

commit v9 on v8

--- a/solution.py
+++ b/solution.py
@@ -133,9 +133,9 @@
 
 def encode_kernel(
     q_len, states, rows_q, up, down, proj, perm, owner_map, candidates, teacher,
-    rowst_out, hid_out, slope_out, downt, unit, inverse, q_all, side,
+    rows_out, hid_out, slope_out, unit, inverse, q_all, side,
     rowstq, hid_q, slope_q, unit_q, inv_q, projp,
-    rows, hid, slope, rowst, part, sent, arrived, padq, partq, sent_q, pbuf, tbuf, table, t_all,
+    rows, hid, slope, part, sent, arrived, padq, partq, sent_q, pbuf, tbuf, table, t_all,
     ring_send, ring_recv, save, *sem
 ):
     y, z, c, x = place()
@@ -192,6 +192,7 @@
         for i in range(own):
             rows[g, each * (i + 1) - 16 : each * (i + 1), :] = jnp.zeros((16, width), BF16)
             rows[g, each * i : each * i + length, :] = states[g * own + i]
+        keep(rows.at[g], rows_out.at[g])
         feed(rows.at[g], hid.at[g], slope.at[g], part)
         sent[k] = jnp.dot(part[...], proj[...], preferred_element_type=F32)
         if k:
@@ -243,14 +244,6 @@
     ty.arrive(lambda k, frm: t_all.at[c, frm])
     tc.start(lambda to: t_all.at[c], lambda k: t_all.at[c])
     group(0)
-    for k in range(NX):
-        g = lax.rem(x + k, NX)
-
-        def turn(j):
-            rowst[g, cut(j), :] = nt(perm[cut(j), :], rows[g]).astype(BF16)
-
-        tiled(tiles, turn)
-        keep(rowst.at[g], rowst_out.at[g])
 
     def turn_q(j):
         rowstq[cut(j), :] = nt(perm[cut(j), :], padq[...]).astype(BF16)
@@ -260,10 +253,6 @@
 
     tiled(tiles, turn_q)
 
-    def turn_down(j):
-        downt[cut(j), :] = nt(perm[cut(j), :], down[...]).astype(BF16)
-
-    tiled(tiles, turn_down)
     sy.arrive(lambda k, frm: q_all.at[c, frm])
     sc.start(lambda to: q_all.at[c], lambda k: q_all.at[c])
     tc.arrive(lambda k, frm: t_all.at[frm])
@@ -331,10 +320,9 @@
     shape, V = jax.ShapeDtypeStruct, pltpu.VMEM
     table = (8, 2 * NX * candidates.shape[1])
     outs = [
-        shape((NX, width, many), BF16),
+        shape((NX, many, width), BF16),
         shape((NX, many, hidden), BF16),
         shape((NX, many, hidden), F32),
-        shape((width, hidden), BF16),
         shape((many, emb), F32),
         shape((many, 1), F32),
         shape((NC, NY, NZ, nq, emb), BF16),
@@ -350,7 +338,6 @@
         V((NX, many, width), BF16),
         V((NX, many, hidden), BF16),
         V((NX, many, hidden), F32),
-        V((NX, width, many), BF16),
         V((many, width), BF16),
         V((NX, many, emb), F32),
         V((NX - 1, many, emb), F32),
@@ -376,7 +363,7 @@
     )
 
 
-def circle_sum(group, held, buf, out, send, recv):
+def circle_sum(group, held, buf, out, send, recv, meanwhile):
     size, mine, who = group
     copies = []
     buf[mine] = held[...]
@@ -387,6 +374,7 @@
         )
         copy.start()
         copies.append(copy)
+    meanwhile()
     for k in range(1, size):
         ref = buf.at[(mine + size - k) % size]
         pltpu.make_async_remote_copy(
@@ -427,19 +415,19 @@
 
 def back_kernel(
     P_OWN, Q_LEN,
-    q_all, unit_p, inv_p, side, lens, rowst_in, hid_in, slope_in, downt, rowstq, hid_q, dgelu_q,
+    q_all, unit_p, inv_p, side, lens, rows_in, hid_in, slope_in, perm, rowstq, hid_q, dgelu_q,
     unit_q, inv_q, down, proj, projp,
     out_up, out_down, out_proj, out_loss,
     terms, emb_p, den, scale, cot_p, held, summed, totals, near_sums, far_sums, cot, uc,
-    uc_all, cbuf, abuf, ybuf, bbuf, zbuf, xbuf, mc, mct, mcq, mctq, ucq, rowst, hid, dgelu, turned,
+    uc_all, cbuf, abuf, ybuf, bbuf, zbuf, xbuf, mc, mct, mcq, mctq, ucq, rowst, hid, dgelu, turned, downt,
     acc_up, acc_down, acc_proj,
-    gp, cp, ap, yp, fp, bp, zp, xp, load, *rest
+    gp, cp, yp, fp, bp, zp, xp, load, *rest
 ):
     y, z, c, x = place()
     tiles = down.shape[1] // TILE
     parts = 2 * tiles
-    bufs = [rest[i * parts : (i + 1) * parts] for i in range(7)]
-    sem = list(rest[7 * parts :])
+    bufs = [rest[i * parts : (i + 1) * parts] for i in range(6)]
+    sem = list(rest[6 * parts :])
 
     def stage(axis):
         send, recv = sem.pop(0), sem.pop(0)
@@ -454,15 +442,42 @@
             )
     width = down.shape[1]
 
-    loads = {}
+    loads, row_loads = {}, []
     for i, k in enumerate((0, 3, 1, 2)):
         g = lax.rem(x + k, NX)
         loads[k] = [
-            pltpu.make_async_copy(src.at[g], dst.at[g], load.at[3 * i + n])
-            for n, (src, dst) in enumerate(((hid_in, hid), (slope_in, dgelu), (rowst_in, rowst)))
+            pltpu.make_async_copy(src.at[g], dst.at[g], load.at[2 * i + n])
+            for n, (src, dst) in enumerate(((hid_in, hid), (slope_in, dgelu)))
         ]
+        row_loads.append(
+            pltpu.make_async_copy(rows_in.at[g], mc, load.at[2 * NX + i])
+        )
+    row_loads[0].start()
+    for k in (0, 3, 1, 2):
         for copy in loads[k]:
             copy.start()
+
+    def turn(i, k):
+        row_loads[i].wait()
+
+        def body(j):
+            rowst[lax.rem(x + k, NX), cut(j), :] = nt(perm[cut(j), :], mc[...]).astype(BF16)
+
+        tiled(tiles, body)
+        if i + 1 < NX:
+            row_loads[i + 1].start()
+
+    def turn_first():
+        for i, k in ((0, 0), (1, 3)):
+            turn(i, k)
+
+    def turn_rest():
+        def body(j):
+            downt[cut(j), :] = nt(perm[cut(j), :], down[...]).astype(BF16)
+
+        tiled(tiles, body)
+        for i, k in ((2, 1), (3, 2)):
+            turn(i, k)
 
     many = unit_p.shape[0]
     many_q, emb = q_all.shape
@@ -502,8 +517,8 @@
     held[2:8, :] = jnp.zeros((6, held.shape[1]), F32)
     pl.semaphore_wait(barrier, NY * NX + NZ * NC - 2)
     sum_sems = [sem.pop(0) for _ in range(4)]
-    copies = circle_sum(groups[0], held, near_sums, summed, sum_sems[0], sum_sems[1])
-    copies += circle_sum(groups[1], summed, far_sums, totals, sum_sems[2], sum_sems[3])
+    copies = circle_sum(groups[0], held, near_sums, summed, sum_sems[0], sum_sems[1], turn_first)
+    copies += circle_sum(groups[1], summed, far_sums, totals, sum_sems[2], sum_sems[3], turn_rest)
     lane = lax.broadcasted_iota(jnp.int32, (8, 128), 1) % Q_LEN
     got = totals[...]
     lane_1 = lax.broadcasted_iota(jnp.int32, (1, 128), 1)
@@ -635,14 +650,14 @@
     chunks = []
 
     def onward(chunk):
-        grads, near, total_a, far, _, _, _, s1, s2, _ = chunk
+        grads, near, far, _, _, _, s1, s2, _ = chunk
         s1.arrive(lambda k, frm: near)
-        add_into(total_a, NY, lambda j: grads[c, j], [near])
-        s2.start(lambda to: total_a.at[to], lambda k: far.at[k - 1])
+        add_into(grads.at[c], NY, lambda j: grads[c, j], [near])
+        s2.start(lambda to: grads.at[c, to], lambda k: far.at[k - 1])
 
     def leave(refs):
         chunk = tuple(refs) + tuple(stage(a) for a in "cyz")
-        chunk[7].start(lambda to: chunk[0].at[to], lambda k: chunk[1])
+        chunk[6].start(lambda to: chunk[0].at[to], lambda k: chunk[1])
         if chunks:
             onward(chunks[-1])
         chunks.append(chunk)
@@ -670,7 +685,7 @@
     low = (cot_hid - high.astype(F32)).astype(BF16)
     term = term + nt(downt[...], high) + nt(downt[...], low)
     gp[...] = term.astype(BF16).reshape(gp.shape)
-    leave((gp, cp, ap, yp, fp, bp, zp))
+    leave((gp, cp, yp, fp, bp, zp))
     for j in range(tiles):
         at_j = slice(j * TILE, (j + 1) * TILE)
         back = nt(mcq[...], down[at_j, :])
@@ -681,9 +696,9 @@
 
     onward(chunks[-1])
     per = width // (NY * NZ * NC)
-    for grads, near, total_a, far, f32_sum, padded, last, s1, s2, s3 in chunks:
+    for grads, near, far, f32_sum, padded, last, s1, s2, s3 in chunks:
         s2.arrive(lambda k, frm: far.at[k - 1])
-        value = total_a[y].astype(F32)
+        value = grads[c, y].astype(F32)
         for i in range(NY - 1):
             value = value + far[i].astype(F32)
         tall = value.shape[0]
@@ -694,7 +709,7 @@
         s3.start(lambda to: padded.at[to], lambda k: last.at[k - 1])
     s4 = stage("x")
     for at_chunk in [tiles] + [i for i in range(len(chunks)) if i != tiles]:
-        grads, near, total_a, far, f32_sum, padded, last, s1, s2, s3 = chunks[at_chunk]
+        grads, near, far, f32_sum, padded, last, s1, s2, s3 = chunks[at_chunk]
         s3.arrive(lambda k, frm: last.at[k - 1])
         value = padded[z].astype(F32)
         for i in range(NZ - 1):
@@ -714,15 +729,15 @@
     out_proj[...] = value
     for copy in copies:
         copy.wait_send()
-    for s in [sc, su, sy, sz, sx, s4] + [s for chunk in chunks for s in chunk[7:]]:
+    for s in [sc, su, sy, sz, sx, s4] + [s for chunk in chunks for s in chunk[6:]]:
         s.finish()
 
 
 def backward(own, q_len, *args):
-    q_all, rowst, hid, rowstq, unit_q = args[0], args[5], args[6], args[9], args[12]
+    q_all, rows, hid, rowstq, unit_q = args[0], args[5], args[6], args[9], args[12]
     n, emb = unit_q.shape
     many_q = q_all.shape[0]
-    width, many = rowst.shape[1:]
+    many, width = rows.shape[1:]
     hidden = hid.shape[2]
     few = rowstq.shape[1]
     tall = width // (NC * NY)
@@ -759,6 +774,7 @@
         V((NX, many, hidden), BF16),
         V((NX, many, hidden), F32),
         V((emb, hidden), F32),
+        V((width, hidden), BF16),
         V((width, hidden), F32),
         V((width, hidden), F32),
         V((width, emb), F32),
@@ -768,7 +784,6 @@
     def chunk_buffers(w):
         return [
             V((NC, NY, tall, w), BF16),
-            V((NY, tall, w), BF16),
             V((NY, tall, w), BF16),
             V((NY - 1, tall, w), BF16),
             V((tall + 8, w), F32),
@@ -824,7 +839,7 @@
     order = np.arange(width).reshape(NY, NZ, NC, rows).transpose(2, 0, 1, 3).reshape(-1)
     perm = jnp.asarray(np.eye(width)[order], BF16)
     (
-        rowst, hid_p, slope_p, downt, unit_p, inv_p, q_all, side,
+        rows_p, hid_p, slope_p, unit_p, inv_p, q_all, side,
         rowstq, hid_q, slope_q, unit_q, inv_q, projp,
     ) = encode(
         passage_states, query_states.reshape(q_rows, width), up_weight, down_weight,
@@ -833,7 +848,7 @@
     q_all = q_all.reshape(n_dp * q_rows, emb)
     up, down, grad_proj, loss = backward(
         p_own, q_len, q_all, unit_p, inv_p, side, lengths,
-        rowst, hid_p, slope_p, downt, rowstq, hid_q, slope_q, unit_q, inv_q,
+        rows_p, hid_p, slope_p, perm, rowstq, hid_q, slope_q, unit_q, inv_q,
         down_weight, proj_weight, projp,
     )
     up, down, grad_proj = trim(rows, up, down, grad_proj)

time: 135 us -> 130 us (0.963)
  Pallas kernels: 133 us -> 128 us
    pallas_call x2, Pallas kernels: 132 us -> 127 us  [call(): pl.pallas_call(kernel, out_shape=outs, in_specs=[spec(i, outer[0], scalar...]
where the time goes in v9:
time: 130 us
  Pallas kernels  128 us (98%)
    pallas_call x2, Pallas kernels, call(): pl.pallas_call(kernel, out_shape=outs, in_specs=[spec(i, outer[0], scalar...  127 us

profile of v9, /device:TPU:1, one launch (start us, length us, event | category | flops | bytes accessed | tf_op | source)
XLA Modules:
  0.0 130.0 jit_solution(5318654165256779358)
XLA Ops:
  0.6 42.5 %shard_map.129 = (bf16[4,576,768]{2,1,0:T(8,128)(2,1)}, bf16[4,576,768]{2,1,0:T(8,128)(2,1)}, f32[4,576,768]{2,1,0:T(8,128)}, f32[576,128]{1,0:T(8,128)}, f32[57...) custom-call(bf16[12,180,768]{2,1,0:T(8,128)(2,1)} %states.1, ...), custom_call_target="tpu_custom_call" | custom-call | flops 1000000000 | bytes 60000000 | tf_op jit(solution)/shard_map/pallas_call | solution.py:101
  43.2 84.1 %shard_map.130 = (f32[16,768]{1,0:T(8,128)}, f32[16,768]{1,0:T(8,128)}, f32[16,128]{1,0:T(8,128)}, f32[1,128]{1,0:T(1,128)}) custom-call(bf16[6144,128]{1,0:T(8,128)(2,1)} %bitcast.5, f32[576,128]{1,0:T(8,128)} %get-tuple-element.25.unit_p, f32[576,1]{1,0:T(8,128)} %get-tuple-element.26.inv_p, f32[3,8,6144]{2,1,0:T(8,128)} %get-tuple-element.27.side, ...), custom_call_target="tpu_custom_call" | custom-call | flops 1000000000 | bytes 60000000 | tf_op jit(solution)/shard_map/pallas_call | solution.py:101
  127.3 1.2 slice_bitcast_fusion
  128.5 1.5 %shard_map.131 = (f32[12,768]{1,0:T(8,128)}, f32[12,768]{1,0:T(8,128)}, f32[12,128]{1,0:T(8,128)}) custom-call(f32[16,768]{1,0:T(8,128)} %get-tuple-element.38.refs_0_, f32[16,768]{1,0:T(8,128)} %get-tuple-element.39.refs_1_, f32[16,128]{1,0:T(8,128)} %get-tuple-element.40.refs_2_), custom_call_target="tpu_custom_call" | custom-call | tf_op jit(solution)/shard_map/pallas_call | solution.py:812
